TPU v7x, 256 devices: a whole 4x4x8 slice. The times are simulated.
256 devices in a mesh: seq: 16 (over y, x), head: 8 (over z), dp: 2 (over core).
Axes of the slice: x: 4, y: 4, z: 8, core: 2. Of those that a mesh axis runs over, the one named last changes fastest.
Arguments:
- hidden: bfloat16 [8192, 2560], P(('dp', 'seq', 'head')), parts along dimension 0, may hold values from -6 to 6
- x_input: bfloat16 [8192, 5120], P(('dp', 'seq', 'head')), parts along dimension 0, may hold values from -6 to 6
- grad_out: bfloat16 [8192, 5120], P(('dp', 'seq', 'head')), parts along dimension 0, may hold values from -6 to 6
- bc_weight: bfloat16 [2560, 256], replicated, may hold values from -0.01953125 to 0.01953125
- dt_weight: bfloat16 [2560, 80], replicated, may hold values from -0.125 to 0.125
- dt_bias: float32 [80], replicated, may hold values from -3 to -2
- a_log: float32 [80], replicated, may hold values from -10 to -1.6
- d_skip: float32 [80], replicated, may hold values from 0.5 to 1.5
Outputs:
- mixer_out: bfloat16 [8192, 5120], P(('dp', 'seq', 'head')), parts along dimension 0
- grad_x: bfloat16 [8192, 5120], P(('dp', 'seq', 'head')), parts along dimension 0
- grad_hidden: bfloat16 [8192, 2560], P(('dp', 'seq', 'head')), parts along dimension 0
- grad_bc_weight: float32 [5120, 256], P('dp'), parts along dimension 0
- grad_dt_weight: float32 [5120, 80], P('dp'), parts along dimension 0
- param_grads: float32 [6, 80], P('dp'), parts along dimension 0
There are 2 independent parts, one for each index of `dp`. A program takes and returns all parts, laid end to end along the dimension named above; an argument that names none is the same for every part. Nothing has to cross between parts.
All inputs are finite; a program needn't handle non-finite values.
Results may differ from a plain program's by a relative error of at most 0.02.
Values may be sent and summed in bfloat16 or wider, within the bound.
No kernel may reach another device: no remote copies, remote signals or barrier semaphores. Data moves between devices by JAX's collectives and lax.ppermute only.
A program may use at most 128 MiB of HBM per device.

v0:
```python
import jax
import jax.numpy as jnp
from jax import lax
from jax.sharding import PartitionSpec as P

Q = 256


precise = lax.Precision.HIGHEST


def prefix_2(value, axis, combine, identity):
    devices, place = (lax.axis_size(axis), lax.axis_index(axis))
    everything = jax.tree.map(
        lambda part, kind: lax.all_gather(part.astype(kind), axis),
        value,
        (jnp.bfloat16, jnp.bfloat16),
    )
    start = jax.tree.map(
        lambda part, zero: jnp.broadcast_to(jnp.asarray(zero, part.dtype), part.shape),
        value,
        identity,
    )

    def step(k, before):
        reached = k < place
        new = combine(
            before, jax.tree.map(lambda part, own: part[k].astype(own.dtype), everything, value)
        )
        return jax.tree.map(lambda a, b: jnp.where(reached, a, b), new, before)

    return lax.fori_loop(0, devices, step, start)


def prefix_3(part, axis, combine, identity):
    count = lax.axis_size(axis)
    place = lax.axis_index(axis)
    ahead = count - 1 - place
    gathered = jax.tree.map(lambda a: lax.all_gather(a, axis), part)
    state = jax.tree.map(lambda a, e: jnp.zeros_like(a) + jnp.asarray(e, a.dtype), part, identity)

    def one(step, state):
        source = count - 1 - step
        return combine(
            state, jax.tree.map(lambda a: lax.dynamic_index_in_dim(a, source, 0, False), gathered)
        )

    return lax.fori_loop(0, ahead, one, state)


def span_scan(x_heads, step_size, b_rows, c_rows, neg_rate, state_in):
    length = x_heads.shape[0]
    blocks = length // Q
    heads_here = x_heads.shape[1]
    head_width = x_heads.shape[2]
    states = b_rows.shape[1]
    causal = (jnp.arange(Q)[:, None] >= jnp.arange(Q)[None, :])[:, :, None]

    def span_advance(carry, block):
        x_block, step_block, b_block, c_block = block
        running = jnp.cumsum(step_block * neg_rate[None, :], axis=0)
        scores = jnp.dot(c_block, b_block.T, precision=precise)
        spread = running[:, None, :] - running[None, :, :]
        decay = jnp.where(causal, jnp.exp(jnp.where(causal, spread, 0.0)), 0.0)
        scaled_x = x_block * step_block[:, :, None]
        inner = jnp.einsum("qkh,khp->qhp", decay * scores[:, :, None], scaled_x, precision=precise)
        carried = (
            jnp.einsum("qn,hnp->qhp", c_block, carry, precision=precise)
            * jnp.exp(running)[:, :, None]
        )
        total = running[-1]
        weights_end = jnp.exp(total[None, :] - running)
        fresh = jnp.einsum(
            "kn,khp->hnp", b_block, scaled_x * weights_end[:, :, None], precision=precise
        )
        return (jnp.exp(total)[:, None, None] * carry + fresh, inner + carried)

    pieces = (
        x_heads.reshape(blocks, Q, heads_here, head_width),
        step_size.reshape(blocks, Q, heads_here),
        b_rows.reshape(blocks, Q, states),
        c_rows.reshape(blocks, Q, states),
    )
    state_out, outputs = lax.scan(jax.checkpoint(span_advance), state_in, pieces)
    return (outputs.reshape(length, heads_here, head_width), state_out)


def mixer_local(x_heads, raw_step, b_rows, c_rows, log_decay, skip_gain, step_bias, state_in):
    step_size = jax.nn.softplus(raw_step + step_bias[None, :])
    neg_rate = -jnp.exp(log_decay)
    mixed, state_out = span_scan(x_heads, step_size, b_rows, c_rows, neg_rate, state_in)
    return (mixed + skip_gain[None, :, None] * x_heads, state_out)


def device_totals(x_heads, step_size, b_rows, c_rows, grad_heads, neg_rate):
    length = x_heads.shape[0]
    heads_here = x_heads.shape[1]
    head_width = x_heads.shape[2]
    states = b_rows.shape[1]
    blocks = length // Q

    def device_advance(carry, block):
        prefix, state_sum, adjoint_sum = carry
        x_block, step_block, b_block, c_block, grad_block = block
        running = jnp.cumsum(step_block * neg_rate[None, :], axis=0)
        total = running[-1]
        weights_end = jnp.exp(total[None, :] - running)
        scaled_x = x_block * step_block[:, :, None]
        fresh = jnp.einsum(
            "kn,khp->hnp", b_block, scaled_x * weights_end[:, :, None], precision=precise
        )
        state_sum = jnp.exp(total)[:, None, None] * state_sum + fresh
        reach = jnp.exp(prefix[None, :] + running)
        adjoint_sum = adjoint_sum + jnp.einsum(
            "qn,qhp->hnp", c_block, grad_block * reach[:, :, None], precision=precise
        )
        return ((prefix + total, state_sum, adjoint_sum), None)

    pieces = (
        x_heads.reshape(blocks, Q, heads_here, head_width),
        step_size.reshape(blocks, Q, heads_here),
        b_rows.reshape(blocks, Q, states),
        c_rows.reshape(blocks, Q, states),
        grad_heads.reshape(blocks, Q, heads_here, head_width),
    )
    start = (
        jnp.zeros((heads_here,), jnp.float32),
        jnp.zeros((heads_here, states, head_width), jnp.float32),
        jnp.zeros((heads_here, states, head_width), jnp.float32),
    )
    (prefix, state_sum, adjoint_sum), unused = lax.scan(device_advance, start, pieces)
    return (jnp.exp(prefix), state_sum, adjoint_sum)


def combine_pairs(earlier, later):
    return (earlier[0] * later[0], later[0][:, None, None] * earlier[1] + later[1])


def per_device(hidden, x_input, grad_out, bc_weight, dt_weight, dt_bias, a_log, d_skip):
    groups = lax.axis_size("head")
    head_index = lax.axis_index("head")
    heads_all = dt_weight.shape[1]
    heads_local = heads_all // groups
    head_width = x_input.shape[1] // heads_all
    states = bc_weight.shape[1] // 2
    proj_bc = jnp.dot(hidden, bc_weight, preferred_element_type=jnp.float32).astype(jnp.bfloat16)
    proj_dt = jnp.dot(hidden, dt_weight, preferred_element_type=jnp.float32).astype(jnp.bfloat16)
    x_local, raw_local, grad_local = (
        lax.all_to_all(x_input, "head", split_axis=1, concat_axis=0, tiled=True),
        lax.all_to_all(proj_dt, "head", split_axis=1, concat_axis=0, tiled=True),
        lax.all_to_all(grad_out, "head", split_axis=1, concat_axis=0, tiled=True),
    )
    bc_local = lax.all_gather(proj_bc, "head", axis=0, tiled=True)
    length = x_local.shape[0]
    x_heads = x_local.astype(jnp.float32).reshape(length, heads_local, head_width)
    grad_heads = grad_local.astype(jnp.float32).reshape(length, heads_local, head_width)
    raw_step = raw_local.astype(jnp.float32)
    b_rows = bc_local[:, :states].astype(jnp.float32)
    c_rows = bc_local[:, states:].astype(jnp.float32)
    offset = head_index * heads_local
    bias_local = lax.dynamic_slice_in_dim(dt_bias, offset, heads_local)
    log_local = lax.dynamic_slice_in_dim(a_log, offset, heads_local)
    skip_local = lax.dynamic_slice_in_dim(d_skip, offset, heads_local)
    step_size = jax.nn.softplus(raw_step + bias_local[None, :])
    neg_rate = -jnp.exp(log_local)
    decay_all, state_sum, adjoint_sum = device_totals(
        x_heads, step_size, b_rows, c_rows, grad_heads, neg_rate
    )
    identity = (
        jnp.ones((heads_local,), jnp.float32),
        jnp.zeros((heads_local, states, head_width), jnp.float32),
    )
    state_in = prefix_2((decay_all, state_sum), "seq", combine_pairs, identity)[1]
    state_grad = prefix_3((decay_all, adjoint_sum), "seq", combine_pairs, identity)[1]

    def forward(x_arg, raw_arg, b_arg, c_arg, log_arg, skip_arg, bias_arg):
        return mixer_local(x_arg, raw_arg, b_arg, c_arg, log_arg, skip_arg, bias_arg, state_in)

    (mixed, state_end), pullback = jax.vjp(
        forward, x_heads, raw_step, b_rows, c_rows, log_local, skip_local, bias_local
    )
    grad_xs, grad_raw, grad_b, grad_c, grad_alog, grad_skip, grad_bias = pullback(
        (grad_heads, state_grad)
    )
    out_local = mixed.reshape(length, heads_local * head_width).astype(jnp.bfloat16)
    gradx_local = grad_xs.reshape(length, heads_local * head_width).astype(jnp.bfloat16)
    step_local = grad_raw.astype(jnp.bfloat16)
    mixer_out, grad_x, d_step = (
        lax.all_to_all(out_local, "head", split_axis=0, concat_axis=1, tiled=True),
        lax.all_to_all(gradx_local, "head", split_axis=0, concat_axis=1, tiled=True),
        lax.all_to_all(step_local, "head", split_axis=0, concat_axis=1, tiled=True),
    )
    d_bc = lax.psum_scatter(
        jnp.concatenate([grad_b, grad_c], axis=1).astype(jnp.bfloat16),
        "head",
        scatter_dimension=0,
        tiled=True,
    )
    grad_hidden = (
        jnp.dot(d_bc, bc_weight.T, preferred_element_type=jnp.float32)
        + jnp.dot(d_step, dt_weight.T, preferred_element_type=jnp.float32)
    ).astype(jnp.bfloat16)
    seq_total = length * lax.axis_size("seq")
    weight_bc = jnp.dot(hidden.T, d_bc, preferred_element_type=jnp.float32) / seq_total
    weight_dt = jnp.dot(hidden.T, d_step, preferred_element_type=jnp.float32) / seq_total
    stacked = jnp.stack([grad_bias, grad_alog, grad_skip]) / seq_total
    param_local = lax.dynamic_update_slice(
        jnp.zeros((3, heads_all), jnp.float32), stacked, (0, offset)
    )
    grad_bc_weight, grad_dt_weight, param_grads = lax.psum(
        (weight_bc, weight_dt, param_local), ("seq", "head")
    )
    return (mixer_out, grad_x, grad_hidden, grad_bc_weight, grad_dt_weight, param_grads)


def solution(mesh):
    in_specs = (
        P(("dp", "seq", "head"), None),
        P(("dp", "seq", "head"), None),
        P(("dp", "seq", "head"), None),
        P(),
        P(),
        P(),
        P(),
        P(),
    )
    out_specs = (
        P(("dp", "seq", "head"), None),
        P(("dp", "seq", "head"), None),
        P(("dp", "seq", "head"), None),
        P("dp", None),
        P("dp", None),
        P("dp", None),
    )
    return jax.shard_map(
        per_device, mesh=mesh, in_specs=in_specs, out_specs=out_specs, check_vma=False
    )
```

profile of v0, /device:TPU:32, one launch (start us, length us, event | category | flops | bytes accessed | tf_op | source)
XLA Modules:
  0.0 753.4 jit_solution(9546356608684292287)
XLA Ops:
  7.2 1.4 convolution_convert_fusion.1
  9.5 8.6 %all-to-all-start.1 = ((bf16[8,2,160]{2,1,0:T(2,128)(2,1)}), bf16[8,2,160]{2,1,0:T(2,128)(2,1)S(1)}, u32[]{:S(2)}, u32[]{:S(2)}) async-start(bf16[8,2,160]{2,1,0:T(2,128)(2,1)} %reshape.399), calls=%async_computation.1 | async-start | bytes 16384 | tf_op jit(solution)/shard_map/all_to_all | solution.py:150
  20.0 1.7 copy.316
  21.8 2.6 all-to-all-done.1
  24.3 4.8 all-to-all-start
  29.1 28.2 %all_gather.23 = bf16[256,256]{1,0:T(8,128)(2,1)S(1)} all-gather(bf16[32,256]{1,0:T(8,128)(2,1)S(1)} %convolution_convert_fusion), channel_id=1, replica_groups=mesh['seq'=16,'head'=8,'dp'=2] {'head'}, dimensions={0}, use_global_device_ids=true | all-gather | bytes 147456 | tf_op jit(solution)/shard_map/all_gather | solution.py:153
  59.3 5.6 all-to-all-start.3
  67.8 1.5 mul.420.clone
  70.6 1.5 copy.234
  72.1 1.5 mul.416
  75.6 1.5 mul.406
  79.6 3.5 multiply_reduce_fusion
  83.1 1.5 mul.419
  84.6 2.6 fusion.62
  87.3 1.5 mul.429
  88.9 2.0 fusion.56
  93.2 20.9 %all-gather.2 = bf16[16,1,10]{2,1,0:T(2,128)(2,1)S(1)} all-gather(bf16[1,1,10]{2,1,0:T(2,128)(2,1)S(1)} %bitcast.278), channel_id=1, replica_groups=mesh['seq'=16,'head'=8,'dp'=2] {'seq'}, dimensions={0}, use_global_device_ids=true | all-gather | bytes 340 | tf_op jit(solution)/shard_map/all_gather | solution.py:15
  114.1 21.2 %all-gather.3 = f32[16,1,10]{2,1,0:T(1,128)} all-gather(f32[1,1,10]{2,1,0:T(1,128)} %bitcast.276), channel_id=1, replica_groups=mesh['seq'=16,'head'=8,'dp'=2] {'seq'}, dimensions={0}, use_global_device_ids=true | all-gather | bytes 680 | tf_op jit(solution)/shard_map/all_gather | solution.py:39
  136.3 1.8 reshape.371
  139.2 1.8 reshape.373
  140.9 22.0 %while.21 = (s32[]{:T(128)}, f32[10,128,64]{2,1,0:T(8,128)S(1)}, s32[]{:T(128)}, bf16[16,10]{1,0:T(8,128)(2,1)S(1)}, bf16[16,10,128,64]{2,3,1,0:T(8,128)(2,1)}, /*index=5*/s32[]{:T(128)}, s32[]{:T(128)}) while((s32[]{:T(128)}, f32[10,128,64]{2,1,0:T(8,128)S(1)}, s32[]{:T(128)}, bf16[16,10]{1,0:T(8,128)(2,1)S(1)}, ...), condition=%wide.region_3.4_spmd.clone, body=%wide.region_2.3_spmd.clone.sunk | while | flops 409614 | bytes 1474765 | solution.py:32
  162.9 40.9 %all-gather.9.cloned.1.call-done = f32[160,128,64]{1,2,0:T(8,128)} async-done(((f32[10,128,64]{1,2,0:T(8,128)}), f32[160,128,64]{1,2,0:T(8,128)}) %all-gather.9.cloned.1.call-update) | async-done | bytes 5242896 | tf_op jit(solution)/shard_map/all_gather | solution.py:39
  203.9 57.5 %while.20 = (s32[]{:T(128)}, f32[10,128,64]{2,1,0:T(8,128)S(1)}, s32[]{:T(128)}, f32[16,10]{1,0:T(8,128)}, f32[16,10,128,64]{2,3,1,0:T(8,128)}, /*index=5*/s32[]{:T(128)}, s32[]{:T(128)}, s32[]{:T(128)}, s32[]{:T(128)}) while((s32[]{:T(128)}, f32[10,128,64]{2,1,0:T(8,128)S(1)}, s32[]{:T(128)}, f32[16,10]{1,0:T(8,128)}, ...), condition=%wide.region_5.6_spmd, body=%wide.region_4.5_spmd.sunk | while | flops 163846 | bytes 2294027 | solution.py:48
  203.9 1.7 constant_dynamic-slice_fusion.4
  207.7 1.7 constant_dynamic-slice_fusion.4
  211.5 1.7 constant_dynamic-slice_fusion.4
  215.4 1.7 constant_dynamic-slice_fusion.4
  219.2 1.7 constant_dynamic-slice_fusion.4
  223.0 1.7 constant_dynamic-slice_fusion.4
  226.8 1.7 constant_dynamic-slice_fusion.4
  230.6 1.7 constant_dynamic-slice_fusion.4
  234.4 1.7 constant_dynamic-slice_fusion.4
  238.3 1.7 constant_dynamic-slice_fusion.4
  242.1 1.7 constant_dynamic-slice_fusion.4
  245.9 1.7 constant_dynamic-slice_fusion.4
  249.7 1.7 constant_dynamic-slice_fusion.4
  253.6 1.7 constant_dynamic-slice_fusion.4
  257.4 1.7 constant_dynamic-slice_fusion.4
  266.2 2.1 fusion.71
  269.4 3.0 copy.262
  272.4 3.0 copy.251
  275.4 2.2 copy.254
  277.6 2.1 convolution_bitcast_fusion
  279.8 5.8 fusion.19
  285.6 3.9 multiply_reduce_fusion.3
  291.1 1.7 fusion.118
  294.6 2.7 reduce-window.42
  297.5 2.3 broadcast_multiply_fusion
  299.9 1.7 fusion.65
  304.2 7.5 all-to-all-start.5
  312.5 5.4 all-to-all-done.5
  319.2 28.4 %reduce-scatter.4.cloned.1.call-done = bf16[32,256]{1,0:T(8,128)(2,1)} async-done(((bf16[256,256]{1,0:T(8,128)(2,1)}), bf16[32,256]{1,0:T(8,128)(2,1)}) %reduce-scatter.4.cloned.1.call-update) | async-done | bytes 16400
  347.6 2.7 fusion.1
  351.2 3.6 broadcast_multiply_fusion.1
  355.5 6.0 fusion.48
  361.6 2.4 copy.238
  365.3 2.4 copy.252
  367.7 1.3 reshape.363
  369.0 2.5 add_convert_fusion
  371.6 5.5 all-to-all-start.2
  377.4 13.1 %all-to-all-done.2 = bf16[8,32,640]{2,1,0:T(8,128)(2,1)S(1)} async-done(((bf16[8,32,640]{2,1,0:T(8,128)(2,1)}), bf16[8,32,640]{2,1,0:T(8,128)(2,1)S(1)}, u32[]{:S(2)}, u32[]{:S(2)}) %all-to-all-start.2) | async-done | bytes 327712 | tf_op jit(solution)/shard_map/all_to_all | solution.py:189
  390.5 4.7 all-to-all-start.4
  395.5 344.0 %psum.23 = f32[3,80]{1,0:T(4,128)} all-reduce(f32[3,80]{1,0:T(4,128)S(1)} %dynamic_update_slice.19), channel_id=1, replica_groups=mesh['seq'=16,'head'=8,'dp'=2] {'seq','head'}, use_global_device_ids=true, to_apply=%region_25.26 | all-reduce | flops 240 | bytes 1920 | tf_op jit(solution)/shard_map/psum | solution.py:210
  742.4 3.3 copy.269
  (317 shorter events, 91.2 us)
Async XLA Ops:
  7.2 10.9 %copy-start = (bf16[2560,256]{1,0:T(8,128)(2,1)S(1)}, bf16[2560,256]{1,0:T(8,128)(2,1)}, u32[]{:S(2)}) copy-start(bf16[2560,256]{1,0:T(8,128)(2,1)} %param.15) | copy-start | bytes 3932164
  7.2 50.1 %copy-start.45 = (f32[80]{0:T(128)S(1)}, f32[80]{0:T(128)}, u32[]{:S(2)}) copy-start(f32[80]{0:T(128)} %param.17) | copy-start | bytes 964
  7.2 50.2 %copy-start.14 = (bf16[32,5120]{1,0:T(8,128)(2,1)S(1)}, bf16[32,5120]{1,0:T(8,128)(2,1)}, u32[]{:S(2)}) copy-start(bf16[32,5120]{1,0:T(8,128)(2,1)} %param.14) | copy-start | bytes 983044
  9.5 14.9 %all-to-all-start.1 = ((bf16[8,2,160]{2,1,0:T(2,128)(2,1)}), bf16[8,2,160]{2,1,0:T(2,128)(2,1)S(1)}, u32[]{:S(2)}, u32[]{:S(2)}) async-start(bf16[8,2,160]{2,1,0:T(2,128)(2,1)} %reshape.399), calls=%async_computation.1 | async-start | bytes 16384 | tf_op jit(solution)/shard_map/all_to_all | solution.py:150
  20.0 46.4 %copy-start.34 = (f32[10]{0:T(128)}, f32[10]{0:T(128)S(1)}, u32[]{:S(2)}) copy-start(f32[10]{0:T(128)S(1)} %fusion.113) | copy-start | bytes 124
  24.3 34.9 %all-to-all-start = ((bf16[32,8,640]{2,0,1:T(8,128)(2,1)}), bf16[32,8,640]{2,0,1:T(8,128)(2,1)S(1)}, u32[]{:S(2)}, u32[]{:S(2)}) async-start(bf16[32,8,640]{2,0,1:T(8,128)(2,1)} %bitcast.236), calls=%async_computation | async-start | bytes 655360 | tf_op jit(solution)/shard_map/all_to_all | solution.py:149
  57.4 9.1 %copy-start.36 = (f32[10]{0:T(128)}, f32[10]{0:T(128)S(1)}, u32[]{:S(2)}) copy-start(f32[10]{0:T(128)S(1)} %dynamic_slice.73) | copy-start | bytes 124
  58.2 8.2 %copy-start.15 = (bf16[8,10,32]{2,1,0:T(8,128)(2,1)}, bf16[8,10,32]{2,1,0:T(8,128)(2,1)S(1)}, u32[]{:S(2)}) copy-start(bf16[8,10,32]{2,1,0:T(8,128)(2,1)S(1)} %reshape.400) | copy-start | bytes 15364
  58.3 6.6 copy-start.22
  59.3 7.2 copy-start.1
  59.3 20.3 %all-to-all-start.3 = ((bf16[32,8,640]{2,0,1:T(8,128)(2,1)}), bf16[32,8,640]{2,0,1:T(8,128)(2,1)}, u32[]{:S(2)}, u32[]{:S(2)}) async-start(bf16[32,8,640]{2,0,1:T(8,128)(2,1)} %bitcast.235), calls=%async_computation.3 | async-start | bytes 655360 | tf_op jit(solution)/shard_map/all_to_all | solution.py:151
  64.9 76.1 %all-gather.7.cloned.1.call-start = ((), (), s32[]{:S(2)}) async-start(), calls=%async_computation.7 | async-start | bytes 2785280 | tf_op jit(solution)/shard_map/all_gather | solution.py:15
  65.0 1.4 copy-start.20
  65.7 0.7 copy-start.41
  66.4 0.6 copy-start.26
  87.3 116.5 %all-gather.9.cloned.1.call-start = ((), (), s32[]{:S(2)}) async-start(), calls=%async_computation.8 | async-start | bytes 5570560 | tf_op jit(solution)/shard_map/all_gather | solution.py:39
  92.3 176.0 %copy-start.3 = (f32[256,128]{1,0:T(8,128)}, f32[256,128]{1,0:T(8,128)S(1)}, u32[]{:S(2)}) copy-start(f32[256,128]{1,0:T(8,128)S(1)} %get-tuple-element.368) | copy-start | bytes 393220
  261.4 4.9 copy-start.5
  263.1 9.3 %copy-start.38 = (f32[10]{0:T(128)}, f32[10]{0:T(128)S(1)}, u32[]{:S(2)}) copy-start(f32[10]{0:T(128)S(1)} %slice_bitcast_fusion) | copy-start | bytes 124
  279.8 5.8 copy-start.11
  279.8 5.8 copy-start.12
  279.8 5.8 copy-start.17
  279.8 5.8 copy-start.25
  279.8 5.8 copy-start.28
  279.8 5.8 copy-start.32
  289.5 4.6 copy-start.31
  289.5 4.7 copy-start.30
  289.5 4.9 copy-start.43
  289.5 4.9 copy-start.39
  297.5 4.1 copy-start.4
  297.5 4.1 copy-start.9
  297.5 4.1 copy-start.13
  297.5 4.5 copy-start.6
  299.8 2.6 copy-start.23
  299.8 2.6 copy-start.33
  299.8 2.6 copy-start.35
  299.8 2.6 copy-start.37
  299.8 3.5 copy-start.16
  299.9 18.2 %copy-start.2 = (bf16[32,2560]{1,0:T(8,128)(2,1)S(1)}, bf16[32,2560]{1,0:T(8,128)(2,1)}, u32[]{:S(2)}) copy-start(bf16[32,2560]{1,0:T(8,128)(2,1)} %param.12) | copy-start | bytes 491524
  304.2 13.8 %all-to-all-start.5 = ((bf16[8,2,160]{2,1,0:T(2,128)(2,1)}), bf16[8,2,160]{2,1,0:T(2,128)(2,1)S(1)}, u32[]{:S(2)}, u32[]{:S(2)}) async-start(bf16[8,2,160]{2,1,0:T(2,128)(2,1)} %reshape.401), calls=%async_computation.5 | async-start | bytes 16384 | tf_op jit(solution)/shard_map/all_to_all | solution.py:191
  311.6 35.9 %reduce-scatter.4.cloned.1.call-start = ((), (), s32[]{:S(2)}) async-start(), calls=%async_computation.9 | async-start | bytes 147456
  312.5 429.9 %all-reduce.4.cloned.1.call-start = ((), (), s32[]{:S(2)}) async-start(), calls=%async_computation.10 | async-start | bytes 6881280 | tf_op jit(solution)/shard_map/psum | solution.py:210
  318.1 32.3 %copy-start.18 = (bf16[32,80]{0,1:T(8,128)(2,1)}, bf16[32,80]{0,1:T(8,128)(2,1)S(1)}, u32[]{:S(2)}) copy-start(bf16[32,80]{0,1:T(8,128)(2,1)S(1)} %all_to_all.80) | copy-start | bytes 15364
  319.2 31.1 %copy-start.46 = (f32[80]{0:T(128)S(1)}, f32[80]{0:T(128)}, u32[]{:S(2)}) copy-start(f32[80]{0:T(128)} %param.19) | copy-start | bytes 964
  350.3 0.9 copy-start.8
  351.2 4.3 copy-start.21
  351.2 4.3 copy-start.27
  367.7 9.4 %copy-start.29 = (f32[640]{0:T(1024)S(1)}, f32[640]{0:T(1024)}, u32[]{:S(2)}) copy-start(f32[640]{0:T(1024)} %get-tuple-element.533) | copy-start | bytes 7684
  367.7 9.6 %copy-start.42 = (f32[10]{0:T(128)S(1)}, f32[10]{0:T(128)}, u32[]{:S(2)}) copy-start(f32[10]{0:T(128)} %get-tuple-element.542) | copy-start | bytes 124
  367.7 9.6 %copy-start.44 = (f32[80]{0:T(128)S(1)}, f32[80]{0:T(128)}, u32[]{:S(2)}) copy-start(f32[80]{0:T(128)} %param.18) | copy-start | bytes 964
  369.0 26.2 %copy-start.40 = (f32[10]{0:T(128)S(1)}, f32[10]{0:T(128)}, u32[]{:S(2)}) copy-start(f32[10]{0:T(128)} %get-tuple-element.530) | copy-start | bytes 124
  369.0 370.4 %copy-start.24 = (bf16[32,256]{1,0:T(8,128)(2,1)S(1)}, bf16[32,256]{1,0:T(8,128)(2,1)}, u32[]{:S(2)}) copy-start(bf16[32,256]{1,0:T(8,128)(2,1)} %reduce-scatter.4.cloned.1.call-done) | copy-start | bytes 49156
  369.0 370.9 %copy-start.7 = (bf16[2560,80]{0,1:T(8,128)(2,1)S(1)}, bf16[2560,80]{0,1:T(8,128)(2,1)}, u32[]{:S(2)}) copy-start(bf16[2560,80]{0,1:T(8,128)(2,1)} %param.16) | copy-start | bytes 1228804
  369.0 370.9 %copy-start.19 = (bf16[32,80]{0,1:T(8,128)(2,1)S(1)}, bf16[32,80]{0,1:T(8,128)(2,1)}, u32[]{:S(2)}) copy-start(bf16[32,80]{0,1:T(8,128)(2,1)} %copy-done.18) | copy-start | bytes 15364
  371.6 18.9 %all-to-all-start.2 = ((bf16[8,32,640]{2,1,0:T(8,128)(2,1)}), bf16[8,32,640]{2,1,0:T(8,128)(2,1)S(1)}, u32[]{:S(2)}, u32[]{:S(2)}) async-start(bf16[8,32,640]{2,1,0:T(8,128)(2,1)} %get-tuple-element.546), calls=%async_computation.2 | async-start | bytes 655360 | tf_op jit(solution)/shard_map/all_to_all | solution.py:189
  390.5 351.1 %all-to-all-start.4 = ((bf16[8,32,640]{2,1,0:T(8,128)(2,1)}), bf16[8,32,640]{2,1,0:T(8,128)(2,1)S(1)}, u32[]{:S(2)}, u32[]{:S(2)}) async-start(bf16[8,32,640]{2,1,0:T(8,128)(2,1)} %get-tuple-element.545), calls=%async_computation.4 | async-start | bytes 655360 | tf_op jit(solution)/shard_map/all_to_all | solution.py:190
  742.4 3.3 copy-start.10
Sparse Core Ops, SparseCore 0:
  87.4 52.5 all-gather.6
  143.0 60.7 all-gather.8
  315.5 32.0 reduce-scatter.3
  354.6 236.8 all-reduce.3
where the time goes:
time: 768 us; the launch traced here: 753 us
  blocking collectives  414 us (54%)
  local copies, waits for them, and re-layouts  124 us (16%)
  waiting for transfers between devices  90.5 us (12%)
  matrix products  38.5 us (5%)
  starting transfers between devices  36.7 us (5%)
  other arithmetic  32.9 us (4%)
  between operations  14.9 us (2%)
    psum x1, blocking collectives, per_device(): lax.psum((weight_bc, weight_dt, param_local), ('seq', 'head'))  344 us
    dynamic_slice x30, local copies, waits for them, and re-layouts, one(): lax.dynamic_index_in_dim(a, source, 0, False)  44 us
    all_gather x1, waiting for transfers between devices, prefix_3(): gathered = jax.tree.map(lambda a: lax.all_gather(a, axis), part)  40.9 us
    unnamed x5, waiting for transfers between devices  28.4 us
    all_gather x1, blocking collectives, per_device(): bc_local = lax.all_gather(proj_bc, 'head', axis=0, tiled=True)  28.2 us
    all_gather x1, blocking collectives, prefix_3(): gathered = jax.tree.map(lambda a: lax.all_gather(a, axis), part)  21.2 us
    all_gather x1, blocking collectives, prefix_2(): lax.all_gather(part.astype(kind), axis)  20.9 us
    dynamic_slice x32, local copies, waits for them, and re-layouts, step(): part[k].astype(own.dtype)  18.6 us
  transfers between devices with their start and end apart: 10, of which 5 were waited for; matrix products, arithmetic and copies ran while one was open for 10% of the time, Pallas kernels for 0%

commit v1 on v0

v1 whole, which is shorter than its diff:
```python
import functools

import jax
import jax.numpy as jnp
from jax import lax
from jax.experimental import pallas as pl
from jax.experimental.pallas import tpu as pltpu
from jax.sharding import PartitionSpec as P

F32 = jnp.float32
BF16 = jnp.bfloat16
LANES = 128
LIMIT = 48 * 2**20

SEQ, HEAD = 16, 8
D, H, WIDTH, N = 2560, 80, 64, 128
TOKENS = 32
SPAN = TOKENS * HEAD
HEADS = H // HEAD
CH = HEADS * WIDTH
TOTAL = SPAN * SEQ
COLS = D // SEQ
PACK = 2 * CH + 2 * N + LANES
DPACK = 2 * N + LANES
SLAB = N // SEQ
STEP = 2 * CH + 2 * N


def dot(a, b, ca=1, cb=0):
    return lax.dot_general(a, b, (((ca,), (cb,)), ((), ())), preferred_element_type=F32)


def iota(shape, dim):
    return lax.broadcasted_iota(jnp.int32, shape, dim)


def split(v, parts):
    out = []
    for _ in range(parts):
        top = v.astype(BF16)
        out.append(top)
        v = v - top.astype(F32)
    return out


def one_hot(shift=0):
    return (iota((LANES, CH), 0) - shift == iota((LANES, CH), 1) // WIDTH).astype(F32).astype(BF16)


def spread(v, hot):
    hi, lo = split(v, 2)
    return dot(hi, hot) + dot(lo, hot)


def gather_heads(v, hot, parts=2):
    return sum(dot(part, hot, 1, 1) for part in split(v, parts))


def triangle(dim):
    return (iota((SPAN, SPAN), dim) >= iota((SPAN, SPAN), 1 - dim)).astype(F32).astype(BF16)


def running_sum(tri, v):
    return sum(dot(tri, part) for part in split(v, 3))


def head_params(prm_ref):
    prm = pltpu.roll(prm_ref[...], lax.rem(LANES - HEADS * lax.axis_index("head"), LANES), 1)
    return prm[0:1], -jnp.exp(prm[1:2]), prm[2:3]


def step_sizes(r_ref, prm_ref):
    bias, rate, skip = head_params(prm_ref)
    pre = r_ref[:, STEP:].astype(F32) + bias
    step = jnp.maximum(pre, 0.0) + jnp.log1p(jnp.exp(-jnp.abs(pre)))
    cum = running_sum(triangle(0), step * rate)
    return pre, step, cum, rate, skip


def project_kernel(hid_ref, wbc_ref, wdt_ref, x_ref, g_ref, send_ref, hs_ref):
    hid = hid_ref[...]
    bc = dot(hid, wbc_ref[...]).astype(BF16)
    raw = dot(hid, wdt_ref[...]).astype(BF16).astype(F32)
    raw = jnp.concatenate([raw, jnp.zeros((TOKENS, LANES - H), F32)], axis=1)
    lane = iota((TOKENS, LANES), 1)
    for k in range(HEAD):
        send_ref[k, :, :CH] = x_ref[:, k * CH : (k + 1) * CH]
        send_ref[k, :, CH : 2 * CH] = g_ref[:, k * CH : (k + 1) * CH]
        send_ref[k, :, 2 * CH : STEP] = bc
        mine = pltpu.roll(raw, (LANES - HEADS * k) % LANES, 1)
        send_ref[k, :, STEP:] = jnp.where(lane < HEADS, mine, 0.0).astype(BF16)
    half = TOKENS // 2
    wide = hid.astype(F32)
    pad = jnp.zeros((half, 3 * LANES - 2 * COLS), F32)
    for s in range(SEQ):
        part = wide[:, s * COLS : (s + 1) * COLS]
        hs_ref[s] = jnp.concatenate([part[:half], part[half:], pad], axis=1).astype(BF16)


def totals_kernel(r_ref, prm_ref, hs_ref, send_ref):
    pre, step, cum, rate, skip = step_sizes(r_ref, prm_ref)
    hot = one_hot()
    total = cum[SPAN - 1 :]
    to_end = spread(step * jnp.exp(total - cum), hot)
    from_start = spread(jnp.exp(cum), hot)
    x = r_ref[:, :CH].astype(F32)
    g = r_ref[:, CH : 2 * CH].astype(F32)
    b = r_ref[:, 2 * CH : 2 * CH + N]
    c = r_ref[:, 2 * CH + N : STEP]
    fresh = dot(b, (x * to_end).astype(BF16), 0, 0)
    back = dot(c, (g * from_start).astype(BF16), 0, 0)
    both = jnp.concatenate(
        [fresh.reshape(SEQ, SLAB, CH), back.reshape(SEQ, SLAB, CH)], axis=1
    )
    send_ref[:, :, :CH] = both.astype(BF16)
    hi, lo = split(jnp.exp(total), 2)
    row = iota((2 * SLAB, LANES), 0)
    lane = iota((2 * SLAB, LANES), 1)
    decay = jnp.where(row == 0, hi.astype(F32), jnp.where(row == 1, lo.astype(F32), 0.0))
    decay = pltpu.roll(jnp.where(lane < HEADS, decay, 0.0), WIDTH, 1)
    send_ref[:, :, CH : CH + 2 * LANES] = hs_ref[:, :, : 2 * LANES]
    tail = hs_ref[:, :, 2 * LANES :].astype(F32) + decay[None]
    send_ref[:, :, CH + 2 * LANES :] = tail.astype(BF16)


def prefix_kernel(r_ref, out_ref):
    hot = one_hot(WIDTH)
    tail = r_ref[:, :, CH + 2 * LANES :].astype(F32)
    decay = dot(tail[:, 0, :].astype(BF16), hot) + dot(tail[:, 1, :].astype(BF16), hot)
    ahead, behind = [], [None] * SEQ
    state = jnp.zeros((SLAB, CH), F32)
    for s in range(SEQ):
        ahead.append(state)
        state = decay[s : s + 1] * state + r_ref[s, :, :CH].astype(F32)[:SLAB]
    state = jnp.zeros((SLAB, CH), F32)
    for s in reversed(range(SEQ)):
        behind[s] = state
        state = decay[s : s + 1] * state + r_ref[s, :, :CH].astype(F32)[SLAB:]
    for s in range(SEQ):
        out_ref[s] = jnp.concatenate([ahead[s], behind[s]], axis=0).astype(BF16)


def inner_kernel(r_ref, prm_ref, y_ref, du_ref, db_ref, dc_ref, e_ref, ds_ref):
    pre, step, cum, rate, skip = step_sizes(r_ref, prm_ref)
    hot = one_hot()
    cum_t = cum.T
    b = r_ref[:, 2 * CH : 2 * CH + N]
    c = r_ref[:, 2 * CH + N : STEP]
    scores = dot(c, b, 1, 1)
    causal = iota((SPAN, SPAN), 0) >= iota((SPAN, SPAN), 1)
    step_x = spread(step, hot)
    low = iota((SPAN, LANES), 1) < WIDTH
    zero = jnp.zeros((SPAN, LANES), BF16)
    products = []
    for j in range(HEADS // 2):
        at = slice(j * LANES, (j + 1) * LANES)
        g = r_ref[:, CH + j * LANES : CH + (j + 1) * LANES]
        u = (r_ref[:, at].astype(F32) * step_x[:, at]).astype(BF16)
        g_t = g.astype(F32).T.astype(BF16)
        y = jnp.zeros((SPAN, LANES), F32)
        du_t = []
        for i in range(2):
            h = 2 * j + i
            mine = low if i == 0 else jnp.logical_not(low)
            gap = jnp.where(causal, cum[:, h : h + 1] - cum_t[h : h + 1, :], -1e30)
            decay = jnp.exp(gap)
            mixer = (decay * scores).astype(BF16)
            y += dot(mixer, jnp.where(mine, u, zero))
            du_t.append(dot(g_t[i * WIDTH : (i + 1) * WIDTH], mixer))
            d_mixer = dot(jnp.where(mine, g, zero), u, 1, 1) * decay
            if h == 0:
                ds_ref[...] = d_mixer
            else:
                ds_ref[...] += d_mixer
        du = jnp.concatenate(du_t, axis=0).T
        y_ref[:, at] = y
        du_ref[:, at] = du
        products.append(g.astype(F32) * y - u.astype(F32) * du)
    e_ref[...] = gather_heads(jnp.concatenate(products, axis=1), hot, 3)
    ds = ds_ref[...]
    dc_ref[...] = dot(ds.astype(BF16), b)
    db_ref[...] = dot(ds.T.astype(BF16), c)


def carry_kernel(r_ref, prm_ref, st_ref, y_ref, du_ref, db_ref, dc_ref, e_ref, send_ref):
    pre, step, cum, rate, skip = step_sizes(r_ref, prm_ref)
    hot = one_hot()
    total = cum[SPAN - 1 :]
    step_x = spread(step, hot)
    to_end = spread(jnp.exp(total - cum), hot)
    from_start = spread(jnp.exp(cum), hot)
    skip_x = spread(jnp.broadcast_to(skip, (8, LANES)), hot)[:1]
    states = st_ref[...].astype(F32)
    state_in = states[:, :SLAB].reshape(N, CH)
    state_gr = states[:, SLAB:].reshape(N, CH)
    x = r_ref[:, :CH].astype(F32)
    g = r_ref[:, CH : 2 * CH].astype(F32)
    b = r_ref[:, 2 * CH : 2 * CH + N]
    c = r_ref[:, 2 * CH + N : STEP]
    s_b = state_in.astype(BF16)
    q_b = state_gr.astype(BF16)
    u = x * step_x
    carried = dot(c, s_b) * from_start
    late = dot(b, q_b) * to_end
    y = y_ref[...] + carried + skip_x * x
    du = du_ref[...] + late
    gx = step_x * du + skip_x * g
    d_c = dc_ref[...] + dot((g * from_start).astype(BF16), s_b, 1, 1)
    d_b = db_ref[...] + dot((u * to_end).astype(BF16), q_b, 1, 1)
    e = e_ref[...] + gather_heads(g * carried, hot)
    f = gather_heads(u * late, hot)
    xdu = gather_heads(x * du, hot)
    sums = jnp.concatenate(
        [
            jnp.sum(state_in * state_gr, axis=0, keepdims=True),
            jnp.sum(g * x, axis=0, keepdims=True),
            jnp.zeros((6, CH), F32),
        ],
        axis=0,
    )
    sums = gather_heads(sums, hot, 3)
    edge = jnp.exp(total) * sums[0:1]
    d_rate = running_sum(triangle(1), e) + running_sum(triangle(0), f) - f + edge
    d_raw = (rate * d_rate + xdu) / (1.0 + jnp.exp(-pre))
    d_bias = jnp.sum(d_raw, axis=0, keepdims=True)
    d_log = rate * jnp.sum(step * d_rate, axis=0, keepdims=True)
    hi, lo = split(jnp.concatenate([d_bias, d_log, sums[1:2]], axis=0), 2)
    row = jnp.concatenate(
        [hi.astype(F32), lo.astype(F32), jnp.zeros((TOKENS - 6, LANES), F32)], axis=0
    )
    lane = iota((TOKENS, LANES), 1)
    row = pltpu.roll(jnp.where(lane < HEADS, row, 0.0), 16, 1)
    for k in range(HEAD):
        at = slice(k * TOKENS, (k + 1) * TOKENS)
        send_ref[k, :, :CH] = y[at].astype(BF16)
        send_ref[k, :, CH : 2 * CH] = gx[at].astype(BF16)
        send_ref[k, :, 2 * CH : 2 * CH + N] = d_b[at].astype(BF16)
        send_ref[k, :, 2 * CH + N : STEP] = d_c[at].astype(BF16)
        send_ref[k, :, STEP:] = (jnp.where(lane < HEADS, d_raw[at], 0.0) + row).astype(BF16)


def reduce_kernel(r_ref, send_ref):
    d_bc = jnp.sum(r_ref[:, :, 2 * CH : STEP].astype(F32), axis=0).astype(BF16)
    lane = iota((TOKENS, LANES), 1)
    steps = jnp.zeros((TOKENS, LANES), F32)
    rows = [[], []]
    low = iota((8, LANES), 1)
    for k in range(HEAD):
        tile = r_ref[k, :, STEP:].astype(F32)
        steps += pltpu.roll(jnp.where(lane < HEADS, tile, 0.0), HEADS * k, 1)
        mine = jnp.where(jnp.logical_and(low >= 16, low < 16 + HEADS), tile[:8], 0.0)
        rows[k // 4].append(pltpu.roll(mine, H - 16 if k < 4 else H, 1))
    tail = steps + jnp.concatenate(rows[0], axis=0) + jnp.concatenate(rows[1], axis=0)
    tail = tail.astype(BF16)
    for s in range(SEQ):
        send_ref[s, :, : 2 * N] = d_bc
        send_ref[s, :, 2 * N :] = tail


def finish_kernel(r_ref, d_ref, wbc_ref, wdt_ref, y_ref, gx_ref, gh_ref):
    for k in range(HEAD):
        y_ref[:, k * CH : (k + 1) * CH] = r_ref[k, :, :CH]
        gx_ref[:, k * CH : (k + 1) * CH] = r_ref[k, :, CH : 2 * CH]
    d_bc = d_ref[0, :, : 2 * N]
    d_step = d_ref[0, :, 2 * N :][:, :H]
    gh = dot(d_bc, wbc_ref[...], 1, 1) + dot(d_step, wdt_ref[...], 1, 1)
    gh_ref[...] = gh.astype(BF16)


def weight_kernel(d_ref, h_ref, send_ref, par_ref):
    half = TOKENS // 2
    d = d_ref[...]
    h = h_ref[:, :, CH:].astype(F32)
    grad = jnp.zeros((COLS, DPACK), F32)
    for i in range(2):
        rows = h[:, :, i * COLS : (i + 1) * COLS].reshape(SEQ * half, COLS).astype(BF16)
        grad += dot(rows, d[:, i * half : (i + 1) * half].reshape(SEQ * half, DPACK), 0, 0)
    grad = grad.astype(BF16)
    for k in range(HEAD):
        send_ref[k] = grad
    tail = jnp.sum(d[:, :, 2 * N :].astype(F32), axis=0)
    low = iota((8, LANES), 1)
    out = jnp.zeros((8, LANES), F32)
    for k in range(HEAD):
        at = H if k < 4 else H + 16
        rolled = pltpu.roll(tail[8 * (k % 4) : 8 * (k % 4) + 8], (HEADS * k - at) % LANES, 1)
        mine = jnp.logical_and(low >= HEADS * k, low < HEADS * (k + 1))
        out += jnp.where(mine, rolled, 0.0)
    par_ref[...] = ((out[0:3] + out[3:6]) / TOTAL)[:, :H]


def sum_kernel(r_ref, send_ref):
    grad = (jnp.sum(r_ref[...].astype(F32), axis=0) / TOTAL).astype(BF16)
    for s in range(SEQ):
        send_ref[s] = grad


def unpack_kernel(r_ref, bc_ref, dt_ref):
    for s in range(r_ref.shape[0]):
        at = slice(s * COLS, (s + 1) * COLS)
        bc_ref[at, :] = r_ref[s, :, : 2 * N].astype(F32)
        dt_ref[at, :] = r_ref[s, :, 2 * N :].astype(F32)[:, :H]


def call(kernel, outs, *args, scratch=()):
    return pl.pallas_call(
        kernel,
        out_shape=[jax.ShapeDtypeStruct(shape, kind) for shape, kind in outs],
        in_specs=[pl.BlockSpec(memory_space=pltpu.VMEM)] * len(args),
        out_specs=[pl.BlockSpec(memory_space=pltpu.VMEM)] * len(outs),
        scratch_shapes=list(scratch),
        compiler_params=pltpu.CompilerParams(vmem_limit_bytes=LIMIT),
    )(*args)


def exchange(v, axis):
    return lax.all_to_all(v, axis, split_axis=0, concat_axis=0, tiled=True)


def per_device(hidden, x_input, grad_out, bc_weight, dt_weight, dt_bias, a_log, d_skip):
    prm = jnp.pad(jnp.stack([dt_bias, a_log, d_skip]), ((0, 5), (0, LANES - H)))
    packed, hid_send = call(
        project_kernel,
        [((HEAD, TOKENS, PACK), BF16), ((SEQ, TOKENS // 2, 3 * LANES), BF16)],
        hidden, bc_weight, dt_weight, x_input, grad_out,
    )
    mine = exchange(packed, "head").reshape(SPAN, PACK)
    [sent] = call(
        totals_kernel, [((SEQ, 2 * SLAB, CH + 3 * LANES), BF16)], mine, prm, hid_send
    )
    totals = exchange(sent, "seq")
    y, du, db, dc, e = call(
        inner_kernel,
        [((SPAN, CH), F32), ((SPAN, CH), F32), ((SPAN, N), F32), ((SPAN, N), F32), ((SPAN, LANES), F32)],
        mine, prm,
        scratch=[pltpu.VMEM((SPAN, SPAN), F32)],
    )
    [states] = call(prefix_kernel, [((SEQ, 2 * SLAB, CH), BF16)], totals)
    states = exchange(states, "seq")
    [results] = call(
        carry_kernel, [((HEAD, TOKENS, PACK), BF16)], mine, prm, states, y, du, db, dc, e
    )
    results = exchange(results, "head")
    [d_send] = call(reduce_kernel, [((SEQ, TOKENS, DPACK), BF16)], results)
    d_all = exchange(d_send, "seq")
    mixer_out, grad_x, grad_hidden = call(
        finish_kernel,
        [((TOKENS, H * WIDTH), BF16), ((TOKENS, H * WIDTH), BF16), ((TOKENS, D), BF16)],
        results, d_send, bc_weight, dt_weight,
    )
    w_send, param_grads = call(
        weight_kernel, [((HEAD, COLS, DPACK), BF16), ((3, H), F32)], d_all, totals
    )
    w_parts = exchange(w_send, "head")
    [w_sum] = call(sum_kernel, [((SEQ, COLS, DPACK), BF16)], w_parts)
    w_all = exchange(w_sum, "seq")
    grad_bc_weight, grad_dt_weight = call(
        unpack_kernel, [((D, 2 * N), F32), ((D, H), F32)], w_all
    )
    return (mixer_out, grad_x, grad_hidden, grad_bc_weight, grad_dt_weight, param_grads)


def solution(mesh):
    rows = P(("dp", "seq", "head"), None)
    return jax.shard_map(
        per_device,
        mesh=mesh,
        in_specs=(rows, rows, rows, P(), P(), P(), P(), P()),
        out_specs=(rows, rows, rows, P("dp", None), P("dp", None), P("dp", None)),
        check_vma=False,
    )
```

time: 768 us -> 173 us (0.23); the launches traced: 753 us -> 170 us
  blocking collectives: 414 us -> 81.2 us
  local copies, waits for them, and re-layouts: 124 us -> 12.3 us
  waiting for transfers between devices: 90.5 us -> 47.3 us
  matrix products: 38.5 us -> 0 us
  other arithmetic: 32.9 us -> 0.01 us
  starting transfers between devices: 36.7 us -> 15.8 us
  between operations: 14.9 us -> 0.76 us
  Pallas kernels: 0 us -> 12.6 us
    psum x1 -> x0, blocking collectives: 344 us -> none  [per_device(): lax.psum((weight_bc, weight_dt, param_local), ('seq', 'head'))]
    all_to_all x0 -> x4, blocking collectives: none -> 81.2 us  [exchange(): return lax.all_to_all(v, axis, split_axis=0, concat_axis=0, tiled=True)]
    all_gather x3 -> x0, blocking collectives: 70.3 us -> none  [the longest x1 28.2 us: per_device(): bc_local = lax.all_gather(proj_bc, 'head', axis=0, tiled=True)]
    dynamic_slice x64 -> x0, local copies, waits for them, and re-layouts: 62.7 us -> none  [the longest x30 44 us: one(): lax.dynamic_index_in_dim(a, source, 0, False)]
    all_gather x2 -> x0, waiting for transfers between devices: 40.9 us -> none  [the longest x1 40.9 us: prefix_3(): gathered = jax.tree.map(lambda a: lax.all_gather(a, axis), part)]
    dot_general x18 -> x0, matrix products: 36.3 us -> none  [the longest x3 15.7 us: span_advance(): jnp.einsum('qkh,khp->qhp', decay * scores[:, :, None], scaled_x, precisio...]
    unnamed x5 -> x0, waiting for transfers between devices: 28.4 us -> none
    all_to_all x6 -> x3, waiting for transfers between devices: 21.1 us -> 47.3 us  [exchange(): return lax.all_to_all(v, axis, split_axis=0, concat_axis=0, tiled=True)]
  transfers between devices with their start and end apart: 10 -> 3, of which waited for: 5 -> 3; matrix products, arithmetic and copies ran while one was open for 10% -> 0% of each run, Pallas kernels for 0% -> 2%
where the time goes in v1:
time: 173 us; the launch traced here: 170 us
  blocking collectives  81.2 us (47%)
  waiting for transfers between devices  47.3 us (27%)
  starting transfers between devices  15.8 us (9%)
  Pallas kernels  12.6 us (7%)
  local copies, waits for them, and re-layouts  12.3 us (7%)
    all_to_all x4, blocking collectives, exchange(): return lax.all_to_all(v, axis, split_axis=0, concat_axis=0, tiled=True)  81.2 us
    all_to_all x3, waiting for transfers between devices, exchange(): return lax.all_to_all(v, axis, split_axis=0, concat_axis=0, tiled=True)  47.3 us
    all_to_all x3, starting transfers between devices, exchange(): return lax.all_to_all(v, axis, split_axis=0, concat_axis=0, tiled=True)  15.8 us
    pallas_call x10, Pallas kernels, call(): pl.pallas_call(kernel, out_shape=[jax.ShapeDtypeStruct(shape, kind) for s...  12.6 us
    unnamed x28, local copies, waits for them, and re-layouts  12.3 us
  transfers between devices with their start and end apart: 3, of which 3 were waited for; matrix products, arithmetic and copies ran while one was open for 0% of the time, Pallas kernels for 2%

profile of v1, /device:TPU:32, one launch (start us, length us, event | category | flops | bytes accessed | tf_op | source)
XLA Modules:
  0.0 170.0 jit_solution(7146555113498504120)
XLA Ops:
  0.6 1.3 copy.14.wdt_ref
  2.0 0.0 copy-start.1
  2.0 1.3 copy-done.1
  3.3 0.0 copy-start.7
  3.3 1.0 copy-done.7
  4.3 0.0 copy-start.8
  4.3 1.0 copy-done.8
  5.2 0.0 copy-start.9
  5.2 0.9 copy-done.9
  6.1 0.0 copy-start.10
  6.1 0.0 copy-start.11
  6.2 0.0 copy-start.12
  6.2 1.4 shard_map.127
  7.5 8.6 %all-to-all-start = ((bf16[8,32,1664]{2,1,0:T(8,128)(2,1)}), bf16[8,32,1664]{2,1,0:T(8,128)(2,1)S(1)}, u32[]{:S(2)}, u32[]{:S(2)}) async-start(bf16[8,32,1664]{2,1,0:T(8,128)(2,1)} %get-tuple-element.20), calls=%async_computation | async-start | bytes 1703936 | tf_op jit(solution)/shard_map/all_to_all | solution.py:317
  16.1 0.0 copy-done.10
  16.1 0.0 copy-done.11
  16.1 0.0 copy-done.12
  16.1 23.0 %all-to-all-done = bf16[8,32,1664]{2,1,0:T(8,128)(2,1)S(1)} async-done(((bf16[8,32,1664]{2,1,0:T(8,128)(2,1)}), bf16[8,32,1664]{2,1,0:T(8,128)(2,1)S(1)}, u32[]{:S(2)}, u32[]{:S(2)}) %all-to-all-start) | async-done | bytes 852000 | tf_op jit(solution)/shard_map/all_to_all | solution.py:317
  39.1 1.1 shard_map.128
  40.2 17.0 %all_to_all.35.r_ref.h_ref = bf16[16,16,1024]{2,1,0:T(8,128)(2,1)S(1)} all-to-all(bf16[16,16,1024]{2,1,0:T(8,128)(2,1)S(1)} %shard_map.128), channel_id=1, replica_groups=mesh['seq'=16,'head'=8,'dp'=2] {'seq'}, dimensions={0} | all-to-all | bytes 1048576 | tf_op jit(solution)/shard_map/all_to_all | solution.py:317
  57.2 1.0 shard_map.129
  58.2 3.5 %all-to-all-start.2 = ((bf16[16,16,640]{2,1,0:T(8,128)(2,1)}), bf16[16,16,640]{2,1,0:T(8,128)(2,1)S(1)}, u32[]{:S(2)}, u32[]{:S(2)}) async-start(bf16[16,16,640]{2,1,0:T(8,128)(2,1)} %shard_map.129), calls=%async_computation.2 | async-start | bytes 655360 | tf_op jit(solution)/shard_map/all_to_all | solution.py:317
  61.7 2.3 %shard_map.130 = (f32[256,640]{1,0:T(8,128)S(1)}, f32[256,640]{1,0:T(8,128)S(1)}, f32[256,128]{1,0:T(8,128)S(1)}, f32[256,128]{1,0:T(8,128)S(1)}, f32[256,128]{1,0:T(8,128)S(1)}) custom-call(bf16[256,1664]{1,0:T(8,128)(2,1)S(1)} %bitcast.5, f32[8,128]{1,0:T(8,128)S(1)} %select_maximum_fusion.prm_ref), custom_call_target="tpu_custom_call" | custom-call | tf_op jit(solution)/shard_map/pallas_call | solution.py:306
  64.0 0.0 copy-start.5
  64.0 0.8 copy-done.5
  64.9 5.9 %all-to-all-done.2.st_ref = bf16[16,16,640]{2,1,0:T(8,128)(2,1)S(1)} async-done(((bf16[16,16,640]{2,1,0:T(8,128)(2,1)}), bf16[16,16,640]{2,1,0:T(8,128)(2,1)S(1)}, u32[]{:S(2)}, u32[]{:S(2)}) %all-to-all-start.2) | async-done | bytes 327712 | tf_op jit(solution)/shard_map/all_to_all | solution.py:317
  70.7 0.0 copy-start.6
  70.8 1.1 copy-done.6
  71.8 2.6 %shard_map.131 = bf16[8,32,1664]{2,1,0:T(8,128)(2,1)S(1)} custom-call(bf16[256,1664]{1,0:T(8,128)(2,1)S(1)} %bitcast.6, f32[8,128]{1,0:T(8,128)S(1)} %select_maximum_fusion.prm_ref, bf16[16,16,640]{2,1,0:T(8,128)(2,1)S(1)} %all-to-all-done.2.st_ref, f32[256,640]{1,0:T(8,128)S(1)} %get-tuple-element.22.y_ref, f32[256,640]{1,0:T(8,128)S(1)} %copy-done.6, ...), custom_call_target="tpu_custom_call" | custom-call | tf_op jit(solution)/shard_map/pallas_call | solution.py:306
  74.4 26.6 %all_to_all.36.r_ref = bf16[8,32,1664]{2,1,0:T(8,128)(2,1)S(1)} all-to-all(bf16[8,32,1664]{2,1,0:T(8,128)(2,1)S(1)} %shard_map.131), channel_id=1, replica_groups=mesh['seq'=16,'head'=8,'dp'=2] {'head'}, dimensions={0} | all-to-all | bytes 1703936 | tf_op jit(solution)/shard_map/all_to_all | solution.py:317
  101.0 0.1 shard_map.132.d_ref
  101.1 0.0 copy-start.3
  101.1 12.3 %all_to_all.37.d_ref = bf16[16,32,384]{2,1,0:T(8,128)(2,1)S(1)} all-to-all(bf16[16,32,384]{2,1,0:T(8,128)(2,1)S(1)} %shard_map.132.d_ref), channel_id=1, replica_groups=mesh['seq'=16,'head'=8,'dp'=2] {'seq'}, dimensions={0} | all-to-all | bytes 786432 | tf_op jit(solution)/shard_map/all_to_all | solution.py:317
  113.4 0.9 shard_map.134
  114.3 25.3 %all_to_all.38.r_ref = bf16[8,160,384]{2,1,0:T(8,128)(2,1)S(1)} all-to-all(bf16[8,160,384]{2,1,0:T(8,128)(2,1)S(1)} %get-tuple-element.30), channel_id=1, replica_groups=mesh['seq'=16,'head'=8,'dp'=2] {'head'}, dimensions={0} | all-to-all | bytes 1966080 | tf_op jit(solution)/shard_map/all_to_all | solution.py:317
  139.6 0.2 shard_map.135
  139.8 0.0 copy-done.3
  139.8 0.0 copy-start
  139.8 1.3 copy-done
  141.1 3.7 %all-to-all-start.6 = ((bf16[16,160,384]{2,1,0:T(8,128)(2,1)}), bf16[16,160,384]{2,1,0:T(8,128)(2,1)S(1)}, u32[]{:S(2)}, u32[]{:S(2)}) async-start(bf16[16,160,384]{2,1,0:T(8,128)(2,1)} %copy-done), calls=%async_computation.6 | async-start | bytes 3932160 | tf_op jit(solution)/shard_map/all_to_all | solution.py:317
  144.8 0.0 copy-start.2
  144.8 1.3 copy-done.2
  146.1 0.0 copy-start.4
  146.1 1.0 copy-done.4
  147.1 1.5 shard_map.133
  148.6 18.4 %all-to-all-done.6.r_ref = bf16[16,160,384]{2,1,0:T(8,128)(2,1)S(1)} async-done(((bf16[16,160,384]{2,1,0:T(8,128)(2,1)}), bf16[16,160,384]{2,1,0:T(8,128)(2,1)S(1)}, u32[]{:S(2)}, u32[]{:S(2)}) %all-to-all-start.6) | async-done | bytes 1966112 | tf_op jit(solution)/shard_map/all_to_all | solution.py:317
  167.0 1.7 shard_map.136
  168.7 1.3 copy.16
  (1 shorter events, 0.0 us)
Async XLA Ops:
  2.0 1.3 copy-start.1
  3.3 1.0 copy-start.7
  4.3 1.0 copy-start.8
  5.2 0.9 copy-start.9
  6.1 9.9 %copy-start.10 = (f32[80]{0:T(128)S(1)}, f32[80]{0:T(128)}, u32[]{:S(2)}) copy-start(f32[80]{0:T(128)} %param.15) | copy-start | bytes 964
  6.1 9.9 %copy-start.11 = (f32[80]{0:T(128)S(1)}, f32[80]{0:T(128)}, u32[]{:S(2)}) copy-start(f32[80]{0:T(128)} %param.14) | copy-start | bytes 964
  6.2 9.9 %copy-start.12 = (f32[80]{0:T(128)S(1)}, f32[80]{0:T(128)}, u32[]{:S(2)}) copy-start(f32[80]{0:T(128)} %param.13) | copy-start | bytes 964
  7.5 31.6 %all-to-all-start = ((bf16[8,32,1664]{2,1,0:T(8,128)(2,1)}), bf16[8,32,1664]{2,1,0:T(8,128)(2,1)S(1)}, u32[]{:S(2)}, u32[]{:S(2)}) async-start(bf16[8,32,1664]{2,1,0:T(8,128)(2,1)} %get-tuple-element.20), calls=%async_computation | async-start | bytes 1703936 | tf_op jit(solution)/shard_map/all_to_all | solution.py:317
  58.2 12.6 %all-to-all-start.2 = ((bf16[16,16,640]{2,1,0:T(8,128)(2,1)}), bf16[16,16,640]{2,1,0:T(8,128)(2,1)S(1)}, u32[]{:S(2)}, u32[]{:S(2)}) async-start(bf16[16,16,640]{2,1,0:T(8,128)(2,1)} %shard_map.129), calls=%async_computation.2 | async-start | bytes 655360 | tf_op jit(solution)/shard_map/all_to_all | solution.py:317
  64.0 0.8 copy-start.5
  70.7 1.1 copy-start.6
  101.1 38.7 %copy-start.3 = (bf16[16,32,384]{2,1,0:T(8,128)(2,1)}, bf16[16,32,384]{2,1,0:T(8,128)(2,1)S(1)}, u32[]{:S(2)}) copy-start(bf16[16,32,384]{2,1,0:T(8,128)(2,1)S(1)} %shard_map.132.d_ref) | copy-start | bytes 1179652
  139.8 1.3 copy-start
  141.1 26.0 %all-to-all-start.6 = ((bf16[16,160,384]{2,1,0:T(8,128)(2,1)}), bf16[16,160,384]{2,1,0:T(8,128)(2,1)S(1)}, u32[]{:S(2)}, u32[]{:S(2)}) async-start(bf16[16,160,384]{2,1,0:T(8,128)(2,1)} %copy-done), calls=%async_computation.6 | async-start | bytes 3932160 | tf_op jit(solution)/shard_map/all_to_all | solution.py:317
  144.8 1.3 copy-start.2
  146.1 1.0 copy-start.4

commit v2 on v1

--- a/solution.py
+++ b/solution.py
@@ -10,7 +10,8 @@
 F32 = jnp.float32
 BF16 = jnp.bfloat16
 LANES = 128
-LIMIT = 48 * 2**20
+LIMIT = 24 * 2**20
+FULL = 60 * 2**20
 
 SEQ, HEAD = 16, 8
 D, H, WIDTH, N = 2560, 80, 64, 128
@@ -22,6 +23,7 @@
 COLS = D // SEQ
 PACK = 2 * CH + 2 * N + LANES
 DPACK = 2 * N + LANES
+STAGES = 4
 SLAB = N // SEQ
 STEP = 2 * CH + 2 * N
 
@@ -77,20 +79,45 @@
     return pre, step, cum, rate, skip
 
 
-def project_kernel(hid_ref, wbc_ref, wdt_ref, x_ref, g_ref, send_ref, hs_ref):
+def project_kernel(
+    hid_hbm, wbc_hbm, wdt_hbm, x_hbm, g_hbm, send_ref, hid_ref, wbc_ref, wdt_ref, sems
+):
+    first = [
+        pltpu.make_async_copy(hid_hbm, hid_ref, sems.at[0]),
+        pltpu.make_async_copy(wdt_hbm, wdt_ref, sems.at[1]),
+        pltpu.make_async_copy(wbc_hbm, wbc_ref, sems.at[2]),
+    ]
+    rest = []
+    for k in range(HEAD):
+        for i, ref in enumerate((x_hbm, g_hbm)):
+            rest.append(
+                pltpu.make_async_copy(
+                    ref.at[:, k * CH : (k + 1) * CH],
+                    send_ref.at[k, :, i * CH : (i + 1) * CH],
+                    sems.at[3 + 2 * k + i],
+                )
+            )
+    for copy in first + rest:
+        copy.start()
+    first[0].wait()
     hid = hid_ref[...]
+    first[1].wait()
+    raw = dot(hid, wdt_ref[...], 1, 1).astype(BF16).astype(F32)
+    raw = jnp.concatenate([raw, jnp.zeros((TOKENS, LANES - H), F32)], axis=1)
+    first[2].wait()
     bc = dot(hid, wbc_ref[...]).astype(BF16)
-    raw = dot(hid, wdt_ref[...]).astype(BF16).astype(F32)
-    raw = jnp.concatenate([raw, jnp.zeros((TOKENS, LANES - H), F32)], axis=1)
     lane = iota((TOKENS, LANES), 1)
     for k in range(HEAD):
-        send_ref[k, :, :CH] = x_ref[:, k * CH : (k + 1) * CH]
-        send_ref[k, :, CH : 2 * CH] = g_ref[:, k * CH : (k + 1) * CH]
         send_ref[k, :, 2 * CH : STEP] = bc
         mine = pltpu.roll(raw, (LANES - HEADS * k) % LANES, 1)
         send_ref[k, :, STEP:] = jnp.where(lane < HEADS, mine, 0.0).astype(BF16)
+    for copy in rest:
+        copy.wait()
+
+
+def slab_kernel(hid_ref, hs_ref):
     half = TOKENS // 2
-    wide = hid.astype(F32)
+    wide = hid_ref[...].astype(F32)
     pad = jnp.zeros((half, 3 * LANES - 2 * COLS), F32)
     for s in range(SEQ):
         part = wide[:, s * COLS : (s + 1) * COLS]
@@ -140,7 +167,7 @@
         out_ref[s] = jnp.concatenate([ahead[s], behind[s]], axis=0).astype(BF16)
 
 
-def inner_kernel(r_ref, prm_ref, y_ref, du_ref, db_ref, dc_ref, e_ref, ds_ref):
+def inner_kernel(r_ref, prm_ref, out_ref, ds_ref):
     pre, step, cum, rate, skip = step_sizes(r_ref, prm_ref)
     hot = one_hot()
     cum_t = cum.T
@@ -173,16 +200,16 @@
             else:
                 ds_ref[...] += d_mixer
         du = jnp.concatenate(du_t, axis=0).T
-        y_ref[:, at] = y
-        du_ref[:, at] = du
+        out_ref[:, at] = y
+        out_ref[:, CH + j * LANES : CH + (j + 1) * LANES] = du
         products.append(g.astype(F32) * y - u.astype(F32) * du)
-    e_ref[...] = gather_heads(jnp.concatenate(products, axis=1), hot, 3)
+    out_ref[:, STEP:] = gather_heads(jnp.concatenate(products, axis=1), hot, 3)
     ds = ds_ref[...]
-    dc_ref[...] = dot(ds.astype(BF16), b)
-    db_ref[...] = dot(ds.T.astype(BF16), c)
-
-
-def carry_kernel(r_ref, prm_ref, st_ref, y_ref, du_ref, db_ref, dc_ref, e_ref, send_ref):
+    out_ref[:, 2 * CH : 2 * CH + N] = dot(ds.T.astype(BF16), c)
+    out_ref[:, 2 * CH + N : STEP] = dot(ds.astype(BF16), b)
+
+
+def carry_kernel(r_ref, prm_ref, st_ref, in_ref, send_ref, both_ref):
     pre, step, cum, rate, skip = step_sizes(r_ref, prm_ref)
     hot = one_hot()
     total = cum[SPAN - 1 :]
@@ -202,12 +229,12 @@
     u = x * step_x
     carried = dot(c, s_b) * from_start
     late = dot(b, q_b) * to_end
-    y = y_ref[...] + carried + skip_x * x
-    du = du_ref[...] + late
+    y = in_ref[:, :CH] + carried + skip_x * x
+    du = in_ref[:, CH : 2 * CH] + late
     gx = step_x * du + skip_x * g
-    d_c = dc_ref[...] + dot((g * from_start).astype(BF16), s_b, 1, 1)
-    d_b = db_ref[...] + dot((u * to_end).astype(BF16), q_b, 1, 1)
-    e = e_ref[...] + gather_heads(g * carried, hot)
+    d_c = in_ref[:, 2 * CH + N : STEP] + dot((g * from_start).astype(BF16), s_b, 1, 1)
+    d_b = in_ref[:, 2 * CH : 2 * CH + N] + dot((u * to_end).astype(BF16), q_b, 1, 1)
+    e = in_ref[:, STEP:] + gather_heads(g * carried, hot)
     f = gather_heads(u * late, hot)
     xdu = gather_heads(x * du, hot)
     sums = jnp.concatenate(
@@ -230,23 +257,29 @@
     )
     lane = iota((TOKENS, LANES), 1)
     row = pltpu.roll(jnp.where(lane < HEADS, row, 0.0), 16, 1)
+    both_ref[:, :CH] = y.astype(BF16)
+    both_ref[:, CH:] = gx.astype(BF16)
     for k in range(HEAD):
         at = slice(k * TOKENS, (k + 1) * TOKENS)
-        send_ref[k, :, :CH] = y[at].astype(BF16)
-        send_ref[k, :, CH : 2 * CH] = gx[at].astype(BF16)
-        send_ref[k, :, 2 * CH : 2 * CH + N] = d_b[at].astype(BF16)
-        send_ref[k, :, 2 * CH + N : STEP] = d_c[at].astype(BF16)
-        send_ref[k, :, STEP:] = (jnp.where(lane < HEADS, d_raw[at], 0.0) + row).astype(BF16)
+        send_ref[k, :, :N] = d_b[at].astype(BF16)
+        send_ref[k, :, N : 2 * N] = d_c[at].astype(BF16)
+        send_ref[k, :, 2 * N :] = (jnp.where(lane < HEADS, d_raw[at], 0.0) + row).astype(BF16)
+
+
+def rotate_kernel(both_ref, *blocks):
+    for k in range(HEAD):
+        to = lax.rem(lax.axis_index("head") + k, HEAD)
+        blocks[k][...] = both_ref[pl.ds(pl.multiple_of(to * TOKENS, TOKENS), TOKENS), :]
 
 
 def reduce_kernel(r_ref, send_ref):
-    d_bc = jnp.sum(r_ref[:, :, 2 * CH : STEP].astype(F32), axis=0).astype(BF16)
+    d_bc = jnp.sum(r_ref[:, :, : 2 * N].astype(F32), axis=0).astype(BF16)
     lane = iota((TOKENS, LANES), 1)
     steps = jnp.zeros((TOKENS, LANES), F32)
     rows = [[], []]
     low = iota((8, LANES), 1)
     for k in range(HEAD):
-        tile = r_ref[k, :, STEP:].astype(F32)
+        tile = r_ref[k, :, 2 * N :].astype(F32)
         steps += pltpu.roll(jnp.where(lane < HEADS, tile, 0.0), HEADS * k, 1)
         mine = jnp.where(jnp.logical_and(low >= 16, low < 16 + HEADS), tile[:8], 0.0)
         rows[k // 4].append(pltpu.roll(mine, H - 16 if k < 4 else H, 1))
@@ -257,14 +290,29 @@
         send_ref[s, :, 2 * N :] = tail
 
 
-def finish_kernel(r_ref, d_ref, wbc_ref, wdt_ref, y_ref, gx_ref, gh_ref):
-    for k in range(HEAD):
-        y_ref[:, k * CH : (k + 1) * CH] = r_ref[k, :, :CH]
-        gx_ref[:, k * CH : (k + 1) * CH] = r_ref[k, :, CH : 2 * CH]
+def hidden_kernel(d_ref, wbc_ref, wdt_ref, gh_ref):
     d_bc = d_ref[0, :, : 2 * N]
     d_step = d_ref[0, :, 2 * N :][:, :H]
-    gh = dot(d_bc, wbc_ref[...], 1, 1) + dot(d_step, wdt_ref[...], 1, 1)
+    gh = dot(d_bc, wbc_ref[...], 1, 1) + dot(d_step, wdt_ref[...])
     gh_ref[...] = gh.astype(BF16)
+
+
+def finish_kernel(*refs):
+    blocks, (y_hbm, gx_hbm), sems = refs[:HEAD], refs[HEAD : HEAD + 2], refs[HEAD + 2]
+    copies = []
+    for k in range(HEAD):
+        of = lax.rem(lax.axis_index("head") + HEAD - k, HEAD)
+        cols = pl.ds(pl.multiple_of(of * CH, LANES), CH)
+        for i, out in enumerate((y_hbm, gx_hbm)):
+            copies.append(
+                pltpu.make_async_copy(
+                    blocks[k].at[:, i * CH : (i + 1) * CH], out.at[:, cols], sems.at[k, i]
+                )
+            )
+    for copy in copies:
+        copy.start()
+    for copy in copies:
+        copy.wait()
 
 
 def weight_kernel(d_ref, h_ref, send_ref, par_ref):
@@ -295,22 +343,46 @@
         send_ref[s] = grad
 
 
-def unpack_kernel(r_ref, bc_ref, dt_ref):
-    for s in range(r_ref.shape[0]):
-        at = slice(s * COLS, (s + 1) * COLS)
-        bc_ref[at, :] = r_ref[s, :, : 2 * N].astype(F32)
-        dt_ref[at, :] = r_ref[s, :, 2 * N :].astype(F32)[:, :H]
-
-
-def call(kernel, outs, *args, scratch=()):
+def unpack_kernel(r_ref, bc_hbm, dt_hbm, bc_ref, dt_ref, sems):
+    parts = SEQ // STAGES
+    copies = []
+    for i in range(STAGES):
+        part = r_ref[i * parts : (i + 1) * parts]
+        at = slice(i * parts * COLS, (i + 1) * parts * COLS)
+        bc_ref[at] = part[:, :, : 2 * N].astype(F32).reshape(parts * COLS, 2 * N)
+        copies.append(pltpu.make_async_copy(bc_ref.at[at], bc_hbm.at[at], sems.at[i, 0]))
+        copies[-1].start()
+        dt_ref[:, at] = part[:, :, 2 * N :].astype(F32).reshape(parts * COLS, LANES).T[:H]
+        copies.append(pltpu.make_async_copy(dt_ref.at[:, at], dt_hbm.at[:, at], sems.at[i, 1]))
+        copies[-1].start()
+    for copy in copies:
+        copy.wait()
+
+
+def call(kernel, outs, *args, scratch=(), far=False, limit=LIMIT):
     return pl.pallas_call(
         kernel,
         out_shape=[jax.ShapeDtypeStruct(shape, kind) for shape, kind in outs],
-        in_specs=[pl.BlockSpec(memory_space=pltpu.VMEM)] * len(args),
+        in_specs=[pl.BlockSpec(memory_space=pltpu.HBM if far else pltpu.VMEM)] * len(args),
         out_specs=[pl.BlockSpec(memory_space=pltpu.VMEM)] * len(outs),
         scratch_shapes=list(scratch),
+        compiler_params=pltpu.CompilerParams(vmem_limit_bytes=limit),
+    )(*args)
+
+
+def unpack(w_all):
+    return pl.pallas_call(
+        unpack_kernel,
+        out_shape=[jax.ShapeDtypeStruct((D, 2 * N), F32), jax.ShapeDtypeStruct((H, D), F32)],
+        in_specs=[pl.BlockSpec(memory_space=pltpu.VMEM)],
+        out_specs=[pl.BlockSpec(memory_space=pltpu.HBM)] * 2,
+        scratch_shapes=[
+            pltpu.VMEM((D, 2 * N), F32),
+            pltpu.VMEM((H, D), F32),
+            pltpu.SemaphoreType.DMA((STAGES, 2)),
+        ],
         compiler_params=pltpu.CompilerParams(vmem_limit_bytes=LIMIT),
-    )(*args)
+    )(w_all)
 
 
 def exchange(v, axis):
@@ -319,45 +391,67 @@
 
 def per_device(hidden, x_input, grad_out, bc_weight, dt_weight, dt_bias, a_log, d_skip):
     prm = jnp.pad(jnp.stack([dt_bias, a_log, d_skip]), ((0, 5), (0, LANES - H)))
-    packed, hid_send = call(
+    [packed] = call(
         project_kernel,
-        [((HEAD, TOKENS, PACK), BF16), ((SEQ, TOKENS // 2, 3 * LANES), BF16)],
-        hidden, bc_weight, dt_weight, x_input, grad_out,
+        [((HEAD, TOKENS, PACK), BF16)],
+        hidden, bc_weight, dt_weight.T, x_input, grad_out,
+        scratch=[
+            pltpu.VMEM((TOKENS, D), BF16),
+            pltpu.VMEM((D, 2 * N), BF16),
+            pltpu.VMEM((H, D), BF16),
+            pltpu.SemaphoreType.DMA((3 + 2 * HEAD,)),
+        ],
+        far=True,
+        limit=FULL,
     )
     mine = exchange(packed, "head").reshape(SPAN, PACK)
+    [hid_send] = call(slab_kernel, [((SEQ, TOKENS // 2, 3 * LANES), BF16)], hidden)
     [sent] = call(
         totals_kernel, [((SEQ, 2 * SLAB, CH + 3 * LANES), BF16)], mine, prm, hid_send
     )
     totals = exchange(sent, "seq")
-    y, du, db, dc, e = call(
+    [inner] = call(
         inner_kernel,
-        [((SPAN, CH), F32), ((SPAN, CH), F32), ((SPAN, N), F32), ((SPAN, N), F32), ((SPAN, LANES), F32)],
+        [((SPAN, PACK), F32)],
         mine, prm,
         scratch=[pltpu.VMEM((SPAN, SPAN), F32)],
     )
+    totals, inner = lax.optimization_barrier((totals, inner))
     [states] = call(prefix_kernel, [((SEQ, 2 * SLAB, CH), BF16)], totals)
     states = exchange(states, "seq")
-    [results] = call(
-        carry_kernel, [((HEAD, TOKENS, PACK), BF16)], mine, prm, states, y, du, db, dc, e
-    )
-    results = exchange(results, "head")
-    [d_send] = call(reduce_kernel, [((SEQ, TOKENS, DPACK), BF16)], results)
+    d_part, both = call(
+        carry_kernel,
+        [((HEAD, TOKENS, DPACK), BF16), ((SPAN, 2 * CH), BF16)],
+        mine, prm, states, inner,
+    )
+    d_part = exchange(d_part, "head")
+    [d_send] = call(reduce_kernel, [((SEQ, TOKENS, DPACK), BF16)], d_part)
     d_all = exchange(d_send, "seq")
-    mixer_out, grad_x, grad_hidden = call(
-        finish_kernel,
-        [((TOKENS, H * WIDTH), BF16), ((TOKENS, H * WIDTH), BF16), ((TOKENS, D), BF16)],
-        results, d_send, bc_weight, dt_weight,
-    )
+    [grad_hidden] = call(
+        hidden_kernel, [((TOKENS, D), BF16)], d_send, bc_weight, dt_weight.T
+    )
+    d_all, grad_hidden = lax.optimization_barrier((d_all, grad_hidden))
     w_send, param_grads = call(
         weight_kernel, [((HEAD, COLS, DPACK), BF16), ((3, H), F32)], d_all, totals
     )
     w_parts = exchange(w_send, "head")
     [w_sum] = call(sum_kernel, [((SEQ, COLS, DPACK), BF16)], w_parts)
+    w_sum, both = lax.optimization_barrier((w_sum, both))
     w_all = exchange(w_sum, "seq")
-    grad_bc_weight, grad_dt_weight = call(
-        unpack_kernel, [((D, 2 * N), F32), ((D, H), F32)], w_all
-    )
-    return (mixer_out, grad_x, grad_hidden, grad_bc_weight, grad_dt_weight, param_grads)
+    blocks = list(call(rotate_kernel, [((TOKENS, 2 * CH), BF16)] * HEAD, both))
+    for k in range(1, HEAD):
+        ring = [(i, (i + k) % HEAD) for i in range(HEAD)]
+        blocks[k] = lax.ppermute(blocks[k], "head", ring)
+    mixer_out, grad_x = pl.pallas_call(
+        finish_kernel,
+        out_shape=[jax.ShapeDtypeStruct((TOKENS, H * WIDTH), BF16)] * 2,
+        in_specs=[pl.BlockSpec(memory_space=pl.ANY)] * HEAD,
+        out_specs=[pl.BlockSpec(memory_space=pltpu.HBM)] * 2,
+        scratch_shapes=[pltpu.SemaphoreType.DMA((HEAD, 2))],
+        compiler_params=pltpu.CompilerParams(vmem_limit_bytes=LIMIT),
+    )(*blocks)
+    grad_bc_weight, grad_dt_weight = unpack(w_all)
+    return (mixer_out, grad_x, grad_hidden, grad_bc_weight, grad_dt_weight.T, param_grads)
 
 
 def solution(mesh):

time: 173 us -> 157 us (0.908)
  blocking collectives: 81.2 us -> 51.7 us
  starting transfers between devices: 15.8 us -> 35.7 us
  local copies, waits for them, and re-layouts: 12.3 us -> 2.13 us
  Pallas kernels: 12.6 us -> 17.4 us
    all_to_all x4 -> x3, blocking collectives: 81.2 us -> 51.7 us  [exchange(): return lax.all_to_all(v, axis, split_axis=0, concat_axis=0, tiled=True)]
    ppermute x0 -> x7, starting transfers between devices: none -> 12.7 us  [per_device(): blocks[k] = lax.ppermute(blocks[k], 'head', ring)]
    unnamed x28 -> x18, local copies, waits for them, and re-layouts: 12.3 us -> 2.13 us
    all_to_all x3 -> x4, starting transfers between devices: 15.8 us -> 23 us  [exchange(): return lax.all_to_all(v, axis, split_axis=0, concat_axis=0, tiled=True)]
    all_to_all x3 -> x4, waiting for transfers between devices: 47.3 us -> 41.2 us  [exchange(): return lax.all_to_all(v, axis, split_axis=0, concat_axis=0, tiled=True)]
    ppermute x0 -> x7, waiting for transfers between devices: none -> 5.86 us  [per_device(): blocks[k] = lax.ppermute(blocks[k], 'head', ring)]
    pallas_call x0 -> x2, Pallas kernels: none -> 2.89 us  [the longest x1 1.94 us: unpack(): pl.pallas_call(unpack_kernel, out_shape=[jax.ShapeDtypeStruct((D, 2 * N),...]
    pallas_call x10 -> x11, Pallas kernels: 12.6 us -> 14.5 us  [call(): pl.pallas_call(kernel, out_shape=[jax.ShapeDtypeStruct(shape, kind) for s...]
  transfers between devices with their start and end apart: 3 -> 11, of which waited for: 3 -> 7; matrix products, arithmetic and copies ran while one was open for 0% -> 0% of each run, Pallas kernels for 2% -> 4%
where the time goes in v2:
time: 157 us; the launch traced here: 155 us
  blocking collectives  51.7 us (33%)
  waiting for transfers between devices  47.1 us (30%)
  starting transfers between devices  35.7 us (23%)
  Pallas kernels  17.4 us (11%)
  local copies, waits for them, and re-layouts  2.13 us (1%)
    all_to_all x3, blocking collectives, exchange(): return lax.all_to_all(v, axis, split_axis=0, concat_axis=0, tiled=True)  51.7 us
    all_to_all x4, waiting for transfers between devices, exchange(): return lax.all_to_all(v, axis, split_axis=0, concat_axis=0, tiled=True)  41.2 us
    all_to_all x4, starting transfers between devices, exchange(): return lax.all_to_all(v, axis, split_axis=0, concat_axis=0, tiled=True)  23 us
    pallas_call x11, Pallas kernels, call(): pl.pallas_call(kernel, out_shape=[jax.ShapeDtypeStruct(shape, kind) for s...  14.5 us
    ppermute x7, starting transfers between devices, per_device(): blocks[k] = lax.ppermute(blocks[k], 'head', ring)  12.7 us
    ppermute x7, waiting for transfers between devices, per_device(): blocks[k] = lax.ppermute(blocks[k], 'head', ring)  5.86 us
  transfers between devices with their start and end apart: 11, of which 7 were waited for; matrix products, arithmetic and copies ran while one was open for 0% of the time, Pallas kernels for 4%

profile of v2, /device:TPU:32, one launch (start us, length us, event | category | flops | bytes accessed | tf_op | source)
XLA Modules:
  0.0 154.9 jit_solution(14894258927693799451)
XLA Ops:
  0.6 0.0 copy-start.3
  0.6 0.0 copy-start.6
  0.7 0.0 copy-start.7
  0.7 0.0 copy-start.8
  0.7 3.1 %shard_map.127 = bf16[8,32,1664]{2,1,0:T(8,128)(2,1)} custom-call(bf16[32,2560]{1,0:T(8,128)(2,1)} %hid_ref.1, bf16[2560,256]{1,0:T(8,128)(2,1)} %wbc_ref.1, bf16[80,2560]{1,0:T(8,128)(2,1)} %bitcast.9, bf16[32,5120]{1,0:T(8,128)(2,1)} %x_hbm.1, bf16[32,5120]{1,0:T(8,128)(2,1)} %g_hbm.1), custom_call_target="tpu_custom_call" | custom-call | tf_op jit(solution)/shard_map/pallas_call | solution.py:363
  3.8 8.6 %all-to-all-start = ((bf16[8,32,1664]{2,1,0:T(8,128)(2,1)}), bf16[8,32,1664]{2,1,0:T(8,128)(2,1)S(1)}, u32[]{:S(2)}, u32[]{:S(2)}) async-start(bf16[8,32,1664]{2,1,0:T(8,128)(2,1)} %shard_map.127), calls=%async_computation | async-start | bytes 1703936 | tf_op jit(solution)/shard_map/all_to_all | solution.py:389
  12.4 0.0 copy-done.3
  12.4 0.1 shard_map.128.hs_ref
  12.5 0.0 copy-done.6
  12.5 0.0 copy-done.7
  12.5 0.0 copy-done.8
  12.5 22.9 %all-to-all-done = bf16[8,32,1664]{2,1,0:T(8,128)(2,1)S(1)} async-done(((bf16[8,32,1664]{2,1,0:T(8,128)(2,1)}), bf16[8,32,1664]{2,1,0:T(8,128)(2,1)S(1)}, u32[]{:S(2)}, u32[]{:S(2)}) %all-to-all-start) | async-done | bytes 852000 | tf_op jit(solution)/shard_map/all_to_all | solution.py:389
  35.4 1.9 %shard_map.129 = bf16[16,16,1024]{2,1,0:T(8,128)(2,1)} custom-call(bf16[256,1664]{1,0:T(8,128)(2,1)S(1)} %bitcast.6, f32[8,128]{1,0:T(8,128)S(1)} %select_maximum_fusion.prm_ref, bf16[16,16,384]{2,1,0:T(8,128)(2,1)S(1)} %shard_map.128.hs_ref), custom_call_target="tpu_custom_call" | custom-call | tf_op jit(solution)/shard_map/pallas_call | solution.py:363
  37.3 7.0 %all-to-all-start.1 = ((bf16[16,16,1024]{2,1,0:T(8,128)(2,1)}), bf16[16,16,1024]{2,1,0:T(8,128)(2,1)S(1)}, u32[]{:S(2)}, u32[]{:S(2)}) async-start(bf16[16,16,1024]{2,1,0:T(8,128)(2,1)} %shard_map.129), calls=%async_computation.1 | async-start | bytes 1048576 | tf_op jit(solution)/shard_map/all_to_all | solution.py:389
  44.3 2.3 %shard_map.130.in_ref = f32[256,1664]{1,0:T(8,128)S(1)} custom-call(bf16[256,1664]{1,0:T(8,128)(2,1)S(1)} %bitcast.7, f32[8,128]{1,0:T(8,128)S(1)} %select_maximum_fusion.prm_ref), custom_call_target="tpu_custom_call" | custom-call | tf_op jit(solution)/shard_map/pallas_call | solution.py:363
  46.6 7.8 %all-to-all-done.1.r_ref.h_ref = bf16[16,16,1024]{2,1,0:T(8,128)(2,1)S(1)} async-done(((bf16[16,16,1024]{2,1,0:T(8,128)(2,1)}), bf16[16,16,1024]{2,1,0:T(8,128)(2,1)S(1)}, u32[]{:S(2)}, u32[]{:S(2)}) %all-to-all-start.1) | async-done | bytes 524320 | tf_op jit(solution)/shard_map/all_to_all | solution.py:389
  54.5 0.2 shard_map.131
  54.7 12.0 %all_to_all.35.st_ref = bf16[16,16,640]{2,1,0:T(8,128)(2,1)S(1)} all-to-all(bf16[16,16,640]{2,1,0:T(8,128)(2,1)S(1)} %shard_map.131), channel_id=1, replica_groups=mesh['seq'=16,'head'=8,'dp'=2] {'seq'}, dimensions={0} | all-to-all | bytes 655360 | tf_op jit(solution)/shard_map/all_to_all | solution.py:389
  66.7 0.0 copy-start.2
  66.7 2.6 %shard_map.132 = (bf16[8,32,384]{2,1,0:T(8,128)(2,1)S(1)}, bf16[256,1280]{1,0:T(8,128)(2,1)S(1)}) custom-call(bf16[256,1664]{1,0:T(8,128)(2,1)S(1)} %bitcast.8, f32[8,128]{1,0:T(8,128)S(1)} %select_maximum_fusion.prm_ref, bf16[16,16,640]{2,1,0:T(8,128)(2,1)S(1)} %all_to_all.35.st_ref, f32[256,1664]{1,0:T(8,128)S(1)} %shard_map.130.in_ref), custom_call_target="tpu_custom_call" | custom-call | tf_op jit(solution)/shard_map/pallas_call | solution.py:363
  69.4 0.0 copy-start.4
  69.4 0.8 copy-done.4
  70.2 0.0 copy-start.1
  70.2 13.7 %all_to_all.36.r_ref = bf16[8,32,384]{2,1,0:T(8,128)(2,1)S(1)} all-to-all(bf16[8,32,384]{2,1,0:T(8,128)(2,1)S(1)} %get-tuple-element.30), channel_id=1, replica_groups=mesh['seq'=16,'head'=8,'dp'=2] {'head'}, dimensions={0} | all-to-all | bytes 393216 | tf_op jit(solution)/shard_map/all_to_all | solution.py:389
  83.9 0.9 shard_map.133.d_ref
  84.8 3.6 %all-to-all-start.4 = ((bf16[16,32,384]{2,1,0:T(8,128)(2,1)}), bf16[16,32,384]{2,1,0:T(8,128)(2,1)S(1)}, u32[]{:S(2)}, u32[]{:S(2)}) async-start(bf16[16,32,384]{2,1,0:T(8,128)(2,1)} %shard_map.133.d_ref), calls=%async_computation.4 | async-start | bytes 786432 | tf_op jit(solution)/shard_map/all_to_all | solution.py:389
  88.4 0.0 copy-done.2
  88.4 0.0 copy-done.1
  88.4 2.3 %shard_map.134 = bf16[32,2560]{1,0:T(8,128)(2,1)} custom-call(bf16[16,32,384]{2,1,0:T(8,128)(2,1)} %shard_map.133.d_ref, bf16[2560,256]{1,0:T(8,128)(2,1)S(1)} %copy-done.1, bf16[80,2560]{1,0:T(8,128)(2,1)S(1)} %bitcast.10), custom_call_target="tpu_custom_call" | custom-call | tf_op jit(solution)/shard_map/pallas_call | solution.py:363
  90.6 7.1 %all-to-all-done.4.d_ref = bf16[16,32,384]{2,1,0:T(8,128)(2,1)S(1)} async-done(((bf16[16,32,384]{2,1,0:T(8,128)(2,1)}), bf16[16,32,384]{2,1,0:T(8,128)(2,1)S(1)}, u32[]{:S(2)}, u32[]{:S(2)}) %all-to-all-start.4) | async-done | bytes 393248 | tf_op jit(solution)/shard_map/all_to_all | solution.py:389
  97.7 0.9 shard_map.135
  98.6 26.0 %all_to_all.37.r_ref = bf16[8,160,384]{2,1,0:T(8,128)(2,1)S(1)} all-to-all(bf16[8,160,384]{2,1,0:T(8,128)(2,1)S(1)} %get-tuple-element.32), channel_id=1, replica_groups=mesh['seq'=16,'head'=8,'dp'=2] {'head'}, dimensions={0} | all-to-all | bytes 1966080 | tf_op jit(solution)/shard_map/all_to_all | solution.py:389
  124.6 0.2 shard_map.136
  124.8 0.0 copy-start
  124.8 1.3 copy-done
  126.1 0.0 copy-start.5
  126.1 3.8 %all-to-all-start.6 = ((bf16[16,160,384]{2,1,0:T(8,128)(2,1)}), bf16[16,160,384]{2,1,0:T(8,128)(2,1)S(1)}, u32[]{:S(2)}, u32[]{:S(2)}) async-start(bf16[16,160,384]{2,1,0:T(8,128)(2,1)} %copy-done), calls=%async_computation.6 | async-start | bytes 3932160 | tf_op jit(solution)/shard_map/all_to_all | solution.py:389
  129.9 0.0 copy-done.5
  129.9 0.1 shard_map.137
  130.0 0.2 collective-permute-start
  130.2 1.0 collective-permute-start.1
  131.2 1.7 %collective-permute-start.2 = (bf16[32,1280]{1,0:T(8,128)(2,1)S(1)}, bf16[32,1280]{1,0:T(8,128)(2,1)S(1)}, u32[]{:S(2)}, u32[]{:S(2)}) collective-permute-start(bf16[32,1280]{1,0:T(8,128)(2,1)S(1)} %get-tuple-element.38), channel_id=1, source_target_pairs={{0,6},{2,8},{4,10},{6,12},{8,14},{10,0},{12,2},{14,4},{1,7},{3,9},... | collective-permute-start | bytes 245768 | tf_op jit(solution)/shard_map/ppermute | solution.py:444
  132.9 4.0 %collective-permute-start.3 = (bf16[32,1280]{1,0:T(8,128)(2,1)S(1)}, bf16[32,1280]{1,0:T(8,128)(2,1)S(1)}, u32[]{:S(2)}, u32[]{:S(2)}) collective-permute-start(bf16[32,1280]{1,0:T(8,128)(2,1)S(1)} %get-tuple-element.39), channel_id=1, source_target_pairs={{0,8},{2,10},{4,12},{6,14},{8,0},{10,2},{12,4},{14,6},{1,9},{3,11}... | collective-permute-start | bytes 245768 | tf_op jit(solution)/shard_map/ppermute | solution.py:444
  136.9 4.7 %collective-permute-start.4 = (bf16[32,1280]{1,0:T(8,128)(2,1)S(1)}, bf16[32,1280]{1,0:T(8,128)(2,1)S(1)}, u32[]{:S(2)}, u32[]{:S(2)}) collective-permute-start(bf16[32,1280]{1,0:T(8,128)(2,1)S(1)} %get-tuple-element.40), channel_id=1, source_target_pairs={{0,10},{2,12},{4,14},{6,0},{8,2},{10,4},{12,6},{14,8},{1,11},{3,13... | collective-permute-start | bytes 245768 | tf_op jit(solution)/shard_map/ppermute | solution.py:444
  141.6 0.0 collective-permute-done.refs_1_
  141.6 0.0 collective-permute-start.5
  141.6 0.0 collective-permute-done.1.refs_2_
  141.6 1.1 collective-permute-start.6
  142.7 0.0 collective-permute-done.2.refs_3_
  142.7 0.6 collective-permute-done.3.refs_4_
  143.4 3.8 %collective-permute-done.4.refs_5_ = bf16[32,1280]{1,0:T(8,128)(2,1)S(1)} collective-permute-done((bf16[32,1280]{1,0:T(8,128)(2,1)S(1)}, bf16[32,1280]{1,0:T(8,128)(2,1)S(1)}, u32[]{:S(2)}, u32[]{:S(2)}) %collective-permute-start.4) | collective-permute-done | bytes 81952 | tf_op jit(solution)/shard_map/ppermute | solution.py:444
  147.1 0.0 collective-permute-done.5.refs_6_
  147.2 1.4 collective-permute-done.6.refs_7_
  148.6 1.0 shard_map.138
  149.5 3.4 %all-to-all-done.6.r_ref = bf16[16,160,384]{2,1,0:T(8,128)(2,1)S(1)} async-done(((bf16[16,160,384]{2,1,0:T(8,128)(2,1)}), bf16[16,160,384]{2,1,0:T(8,128)(2,1)S(1)}, u32[]{:S(2)}, u32[]{:S(2)}) %all-to-all-start.6) | async-done | bytes 1966112 | tf_op jit(solution)/shard_map/all_to_all | solution.py:389
  152.9 1.9 %shard_map.139 = (f32[2560,256]{1,0:T(8,128)}, f32[80,2560]{1,0:T(8,128)}) custom-call(bf16[16,160,384]{2,1,0:T(8,128)(2,1)S(1)} %all-to-all-done.6.r_ref), custom_call_target="tpu_custom_call" | custom-call | tf_op jit(solution)/shard_map/pallas_call | solution.py:374
  (1 shorter events, 0.0 us)
Async XLA Ops:
  0.6 11.7 %copy-start.3 = (bf16[32,2560]{1,0:T(8,128)(2,1)S(1)}, bf16[32,2560]{1,0:T(8,128)(2,1)}, u32[]{:S(2)}) copy-start(bf16[32,2560]{1,0:T(8,128)(2,1)} %hid_ref.1) | copy-start | bytes 491524
  0.6 11.9 %copy-start.6 = (f32[80]{0:T(128)S(1)}, f32[80]{0:T(128)}, u32[]{:S(2)}) copy-start(f32[80]{0:T(128)} %param.15) | copy-start | bytes 964
  0.7 11.9 %copy-start.7 = (f32[80]{0:T(128)S(1)}, f32[80]{0:T(128)}, u32[]{:S(2)}) copy-start(f32[80]{0:T(128)} %param.14) | copy-start | bytes 964
  0.7 11.9 %copy-start.8 = (f32[80]{0:T(128)S(1)}, f32[80]{0:T(128)}, u32[]{:S(2)}) copy-start(f32[80]{0:T(128)} %param.13) | copy-start | bytes 964
  3.8 31.6 %all-to-all-start = ((bf16[8,32,1664]{2,1,0:T(8,128)(2,1)}), bf16[8,32,1664]{2,1,0:T(8,128)(2,1)S(1)}, u32[]{:S(2)}, u32[]{:S(2)}) async-start(bf16[8,32,1664]{2,1,0:T(8,128)(2,1)} %shard_map.127), calls=%async_computation | async-start | bytes 1703936 | tf_op jit(solution)/shard_map/all_to_all | solution.py:389
  37.3 17.2 %all-to-all-start.1 = ((bf16[16,16,1024]{2,1,0:T(8,128)(2,1)}), bf16[16,16,1024]{2,1,0:T(8,128)(2,1)S(1)}, u32[]{:S(2)}, u32[]{:S(2)}) async-start(bf16[16,16,1024]{2,1,0:T(8,128)(2,1)} %shard_map.129), calls=%async_computation.1 | async-start | bytes 1048576 | tf_op jit(solution)/shard_map/all_to_all | solution.py:389
  66.7 21.6 %copy-start.2 = (bf16[2560,80]{0,1:T(8,128)(2,1)S(1)}, bf16[2560,80]{0,1:T(8,128)(2,1)}, u32[]{:S(2)}) copy-start(bf16[2560,80]{0,1:T(8,128)(2,1)} %param.12) | copy-start | bytes 1228804
  69.4 0.8 copy-start.4
  70.2 18.1 %copy-start.1 = (bf16[2560,256]{1,0:T(8,128)(2,1)S(1)}, bf16[2560,256]{1,0:T(8,128)(2,1)}, u32[]{:S(2)}) copy-start(bf16[2560,256]{1,0:T(8,128)(2,1)} %wbc_ref.1) | copy-start | bytes 3932164
  84.8 12.9 %all-to-all-start.4 = ((bf16[16,32,384]{2,1,0:T(8,128)(2,1)}), bf16[16,32,384]{2,1,0:T(8,128)(2,1)S(1)}, u32[]{:S(2)}, u32[]{:S(2)}) async-start(bf16[16,32,384]{2,1,0:T(8,128)(2,1)} %shard_map.133.d_ref), calls=%async_computation.4 | async-start | bytes 786432 | tf_op jit(solution)/shard_map/all_to_all | solution.py:389
  124.8 1.3 copy-start
  126.1 3.9 %copy-start.5 = (bf16[256,1280]{1,0:T(8,128)(2,1)S(1)}, bf16[256,1280]{1,0:T(8,128)(2,1)}, u32[]{:S(2)}) copy-start(bf16[256,1280]{1,0:T(8,128)(2,1)} %copy-done.4) | copy-start | bytes 1966084
  126.1 26.9 %all-to-all-start.6 = ((bf16[16,160,384]{2,1,0:T(8,128)(2,1)}), bf16[16,160,384]{2,1,0:T(8,128)(2,1)S(1)}, u32[]{:S(2)}, u32[]{:S(2)}) async-start(bf16[16,160,384]{2,1,0:T(8,128)(2,1)} %copy-done), calls=%async_computation.6 | async-start | bytes 3932160 | tf_op jit(solution)/shard_map/all_to_all | solution.py:389
  130.0 11.6 %collective-permute-start = (bf16[32,1280]{1,0:T(8,128)(2,1)S(1)}, bf16[32,1280]{1,0:T(8,128)(2,1)S(1)}, u32[]{:S(2)}, u32[]{:S(2)}) collective-permute-start(bf16[32,1280]{1,0:T(8,128)(2,1)S(1)} %get-tuple-element.36), channel_id=1, source_target_pairs={{0,2},{2,4},{4,6},{6,8},{8,10},{10,12},{12,14},{14,0},{1,3},{3,5},... | collective-permute-start | bytes 245768 | tf_op jit(solution)/shard_map/ppermute | solution.py:444
  130.2 11.4 %collective-permute-start.1 = (bf16[32,1280]{1,0:T(8,128)(2,1)S(1)}, bf16[32,1280]{1,0:T(8,128)(2,1)S(1)}, u32[]{:S(2)}, u32[]{:S(2)}) collective-permute-start(bf16[32,1280]{1,0:T(8,128)(2,1)S(1)} %get-tuple-element.37), channel_id=1, source_target_pairs={{0,4},{2,6},{4,8},{6,10},{8,12},{10,14},{12,0},{14,2},{1,5},{3,7},... | collective-permute-start | bytes 245768 | tf_op jit(solution)/shard_map/ppermute | solution.py:444
  131.2 11.5 %collective-permute-start.2 = (bf16[32,1280]{1,0:T(8,128)(2,1)S(1)}, bf16[32,1280]{1,0:T(8,128)(2,1)S(1)}, u32[]{:S(2)}, u32[]{:S(2)}) collective-permute-start(bf16[32,1280]{1,0:T(8,128)(2,1)S(1)} %get-tuple-element.38), channel_id=1, source_target_pairs={{0,6},{2,8},{4,10},{6,12},{8,14},{10,0},{12,2},{14,4},{1,7},{3,9},... | collective-permute-start | bytes 245768 | tf_op jit(solution)/shard_map/ppermute | solution.py:444
  132.9 10.5 %collective-permute-start.3 = (bf16[32,1280]{1,0:T(8,128)(2,1)S(1)}, bf16[32,1280]{1,0:T(8,128)(2,1)S(1)}, u32[]{:S(2)}, u32[]{:S(2)}) collective-permute-start(bf16[32,1280]{1,0:T(8,128)(2,1)S(1)} %get-tuple-element.39), channel_id=1, source_target_pairs={{0,8},{2,10},{4,12},{6,14},{8,0},{10,2},{12,4},{14,6},{1,9},{3,11}... | collective-permute-start | bytes 245768 | tf_op jit(solution)/shard_map/ppermute | solution.py:444
  136.9 10.3 %collective-permute-start.4 = (bf16[32,1280]{1,0:T(8,128)(2,1)S(1)}, bf16[32,1280]{1,0:T(8,128)(2,1)S(1)}, u32[]{:S(2)}, u32[]{:S(2)}) collective-permute-start(bf16[32,1280]{1,0:T(8,128)(2,1)S(1)} %get-tuple-element.40), channel_id=1, source_target_pairs={{0,10},{2,12},{4,14},{6,0},{8,2},{10,4},{12,6},{14,8},{1,11},{3,13... | collective-permute-start | bytes 245768 | tf_op jit(solution)/shard_map/ppermute | solution.py:444
  141.6 5.6 %collective-permute-start.5 = (bf16[32,1280]{1,0:T(8,128)(2,1)S(1)}, bf16[32,1280]{1,0:T(8,128)(2,1)S(1)}, u32[]{:S(2)}, u32[]{:S(2)}) collective-permute-start(bf16[32,1280]{1,0:T(8,128)(2,1)S(1)} %get-tuple-element.41), channel_id=1, source_target_pairs={{0,12},{2,14},{4,0},{6,2},{8,4},{10,6},{12,8},{14,10},{1,13},{3,15... | collective-permute-start | bytes 245768 | tf_op jit(solution)/shard_map/ppermute | solution.py:444
  141.6 7.0 %collective-permute-start.6 = (bf16[32,1280]{1,0:T(8,128)(2,1)S(1)}, bf16[32,1280]{1,0:T(8,128)(2,1)S(1)}, u32[]{:S(2)}, u32[]{:S(2)}) collective-permute-start(bf16[32,1280]{1,0:T(8,128)(2,1)S(1)} %get-tuple-element.42), channel_id=1, source_target_pairs={{0,14},{2,0},{4,2},{6,4},{8,6},{10,8},{12,10},{14,12},{1,15},{3,1}... | collective-permute-start | bytes 245768 | tf_op jit(solution)/shard_map/ppermute | solution.py:444

commit v3 on v2

--- a/solution.py
+++ b/solution.py
@@ -80,39 +80,54 @@
 
 
 def project_kernel(
-    hid_hbm, wbc_hbm, wdt_hbm, x_hbm, g_hbm, send_ref, hid_ref, wbc_ref, wdt_ref, sems
+    hid_hbm, wbc_hbm, wdt_hbm, x_hbm, g_hbm, send_hbm, tail_ref, x_ref, g_ref, hid_ref, wbc_ref, wdt_ref, sems
 ):
+    rows = D // STAGES
+    chunks = [slice(i * rows, (i + 1) * rows) for i in range(STAGES)]
     first = [
         pltpu.make_async_copy(hid_hbm, hid_ref, sems.at[0]),
         pltpu.make_async_copy(wdt_hbm, wdt_ref, sems.at[1]),
-        pltpu.make_async_copy(wbc_hbm, wbc_ref, sems.at[2]),
     ]
+    for i, at in enumerate(chunks):
+        first.append(pltpu.make_async_copy(wbc_hbm.at[at], wbc_ref.at[at], sems.at[2 + i]))
+    given = []
+    for i, (far, near) in enumerate(((x_hbm, x_ref), (g_hbm, g_ref))):
+        given.append(pltpu.make_async_copy(far, near, sems.at[2 + STAGES + i]))
+    for copy in first + given:
+        copy.start()
     rest = []
-    for k in range(HEAD):
-        for i, ref in enumerate((x_hbm, g_hbm)):
+    for i, near in enumerate((x_ref, g_ref)):
+        given[i].wait()
+        for k in range(HEAD):
             rest.append(
                 pltpu.make_async_copy(
-                    ref.at[:, k * CH : (k + 1) * CH],
-                    send_ref.at[k, :, i * CH : (i + 1) * CH],
-                    sems.at[3 + 2 * k + i],
+                    near.at[:, k * CH : (k + 1) * CH],
+                    send_hbm.at[k, :, i * CH : (i + 1) * CH],
+                    sems.at[4 + STAGES + 2 * k + i],
                 )
             )
-    for copy in first + rest:
-        copy.start()
+            rest[-1].start()
     first[0].wait()
-    hid = hid_ref[...]
     first[1].wait()
-    raw = dot(hid, wdt_ref[...], 1, 1).astype(BF16).astype(F32)
+    raw = dot(hid_ref[...], wdt_ref[...], 1, 1).astype(BF16).astype(F32)
     raw = jnp.concatenate([raw, jnp.zeros((TOKENS, LANES - H), F32)], axis=1)
-    first[2].wait()
-    bc = dot(hid, wbc_ref[...]).astype(BF16)
     lane = iota((TOKENS, LANES), 1)
     for k in range(HEAD):
-        send_ref[k, :, 2 * CH : STEP] = bc
         mine = pltpu.roll(raw, (LANES - HEADS * k) % LANES, 1)
-        send_ref[k, :, STEP:] = jnp.where(lane < HEADS, mine, 0.0).astype(BF16)
+        tail_ref[k, :, 2 * N :] = jnp.where(lane < HEADS, mine, 0.0).astype(BF16)
+    bc = jnp.zeros((TOKENS, 2 * N), F32)
+    for i, at in enumerate(chunks):
+        first[2 + i].wait()
+        bc += dot(hid_ref[:, at], wbc_ref[at])
+    for k in range(HEAD):
+        tail_ref[k, :, : 2 * N] = bc.astype(BF16)
+    last = pltpu.make_async_copy(
+        tail_ref, send_hbm.at[:, :, 2 * CH :], sems.at[4 + STAGES + 2 * HEAD]
+    )
+    last.start()
     for copy in rest:
         copy.wait()
+    last.wait()
 
 
 def slab_kernel(hid_ref, hs_ref):
@@ -323,9 +338,7 @@
     for i in range(2):
         rows = h[:, :, i * COLS : (i + 1) * COLS].reshape(SEQ * half, COLS).astype(BF16)
         grad += dot(rows, d[:, i * half : (i + 1) * half].reshape(SEQ * half, DPACK), 0, 0)
-    grad = grad.astype(BF16)
-    for k in range(HEAD):
-        send_ref[k] = grad
+    send_ref[...] = (grad / TOTAL).astype(BF16)
     tail = jnp.sum(d[:, :, 2 * N :].astype(F32), axis=0)
     low = iota((8, LANES), 1)
     out = jnp.zeros((8, LANES), F32)
@@ -337,10 +350,14 @@
     par_ref[...] = ((out[0:3] + out[3:6]) / TOTAL)[:, :H]
 
 
-def sum_kernel(r_ref, send_ref):
-    grad = (jnp.sum(r_ref[...].astype(F32), axis=0) / TOTAL).astype(BF16)
+def add_kernel(a_ref, b_ref, out_ref):
+    out_ref[...] = (a_ref[...].astype(F32) + b_ref[...].astype(F32)).astype(BF16)
+
+
+def spread_kernel(a_ref, b_ref, send_ref):
+    total = (a_ref[...].astype(F32) + b_ref[...].astype(F32)).astype(BF16)
     for s in range(SEQ):
-        send_ref[s] = grad
+        send_ref[s] = total
 
 
 def unpack_kernel(r_ref, bc_hbm, dt_hbm, bc_ref, dt_ref, sems):
@@ -359,12 +376,12 @@
         copy.wait()
 
 
-def call(kernel, outs, *args, scratch=(), far=False, limit=LIMIT):
+def call(kernel, outs, *args, scratch=(), far=False, far_out=False, limit=LIMIT):
     return pl.pallas_call(
         kernel,
         out_shape=[jax.ShapeDtypeStruct(shape, kind) for shape, kind in outs],
         in_specs=[pl.BlockSpec(memory_space=pltpu.HBM if far else pltpu.VMEM)] * len(args),
-        out_specs=[pl.BlockSpec(memory_space=pltpu.VMEM)] * len(outs),
+        out_specs=[pl.BlockSpec(memory_space=pltpu.HBM if far_out else pltpu.VMEM)] * len(outs),
         scratch_shapes=list(scratch),
         compiler_params=pltpu.CompilerParams(vmem_limit_bytes=limit),
     )(*args)
@@ -396,12 +413,16 @@
         [((HEAD, TOKENS, PACK), BF16)],
         hidden, bc_weight, dt_weight.T, x_input, grad_out,
         scratch=[
+            pltpu.VMEM((HEAD, TOKENS, DPACK), BF16),
+            pltpu.VMEM((TOKENS, H * WIDTH), BF16),
+            pltpu.VMEM((TOKENS, H * WIDTH), BF16),
             pltpu.VMEM((TOKENS, D), BF16),
             pltpu.VMEM((D, 2 * N), BF16),
             pltpu.VMEM((H, D), BF16),
-            pltpu.SemaphoreType.DMA((3 + 2 * HEAD,)),
+            pltpu.SemaphoreType.DMA((5 + STAGES + 2 * HEAD,)),
         ],
         far=True,
+        far_out=True,
         limit=FULL,
     )
     mine = exchange(packed, "head").reshape(SPAN, PACK)
@@ -425,17 +446,28 @@
         mine, prm, states, inner,
     )
     d_part = exchange(d_part, "head")
-    [d_send] = call(reduce_kernel, [((SEQ, TOKENS, DPACK), BF16)], d_part)
+    [d_send] = call(
+        reduce_kernel,
+        [((SEQ, TOKENS, DPACK), BF16)],
+        d_part,
+    )
     d_all = exchange(d_send, "seq")
     [grad_hidden] = call(
         hidden_kernel, [((TOKENS, D), BF16)], d_send, bc_weight, dt_weight.T
     )
     d_all, grad_hidden = lax.optimization_barrier((d_all, grad_hidden))
-    w_send, param_grads = call(
-        weight_kernel, [((HEAD, COLS, DPACK), BF16), ((3, H), F32)], d_all, totals
-    )
-    w_parts = exchange(w_send, "head")
-    [w_sum] = call(sum_kernel, [((SEQ, COLS, DPACK), BF16)], w_parts)
+    w_part, param_grads = call(
+        weight_kernel, [((COLS, DPACK), BF16), ((3, H), F32)], d_all, totals
+    )
+    for far in (1, 2):
+        other = lax.ppermute(w_part, "head", [(i, i ^ far) for i in range(HEAD)])
+        [w_part] = call(add_kernel, [((COLS, DPACK), BF16)], w_part, other)
+    other = lax.ppermute(w_part, "head", [(i, i ^ 4) for i in range(HEAD)])
+    [w_sum] = call(
+        spread_kernel,
+        [((SEQ, COLS, DPACK), BF16)],
+        w_part, other,
+    )
     w_sum, both = lax.optimization_barrier((w_sum, both))
     w_all = exchange(w_sum, "seq")
     blocks = list(call(rotate_kernel, [((TOKENS, 2 * CH), BF16)] * HEAD, both))

time: 157 us -> 151 us (0.962)
  blocking collectives: 51.7 us -> 25.9 us
  waiting for transfers between devices: 47.1 us -> 58.7 us
  starting transfers between devices: 35.7 us -> 43.5 us
    all_to_all x3 -> x2, blocking collectives: 51.7 us -> 25.9 us  [exchange(): return lax.all_to_all(v, axis, split_axis=0, concat_axis=0, tiled=True)]
    ppermute x0 -> x3, waiting for transfers between devices: none -> 15.9 us  [the longest x2 10 us: per_device(): other = lax.ppermute(w_part, 'head', [(i, i ^ far) for i in range(HEAD)])]
    ppermute x0 -> x3, starting transfers between devices: none -> 4.95 us  [the longest x1 3 us: per_device(): other = lax.ppermute(w_part, 'head', [(i, i ^ 4) for i in range(HEAD)])]
    all_to_all x4, waiting for transfers between devices: 41.2 us -> 38.4 us  [exchange(): return lax.all_to_all(v, axis, split_axis=0, concat_axis=0, tiled=True)]
    ppermute x7, starting transfers between devices: 12.7 us -> 15.3 us  [per_device(): blocks[k] = lax.ppermute(blocks[k], 'head', ring)]
    pallas_call x11 -> x13, Pallas kernels: 14.5 us -> 15 us  [call(): pl.pallas_call(kernel, out_shape=[jax.ShapeDtypeStruct(shape, kind) for s...]
  transfers between devices with their start and end apart: 11 -> 14, of which waited for: 7 -> 10; matrix products, arithmetic and copies ran while one was open for 0% -> 0% of each run, Pallas kernels for 4% -> 4%
where the time goes in v3:
time: 151 us; the launch traced here: 149 us
  waiting for transfers between devices  58.7 us (39%)
  starting transfers between devices  43.5 us (29%)
  blocking collectives  25.9 us (17%)
  Pallas kernels  17.9 us (12%)
  local copies, waits for them, and re-layouts  2.13 us (1%)
    all_to_all x4, waiting for transfers between devices, exchange(): return lax.all_to_all(v, axis, split_axis=0, concat_axis=0, tiled=True)  38.4 us
    all_to_all x2, blocking collectives, exchange(): return lax.all_to_all(v, axis, split_axis=0, concat_axis=0, tiled=True)  25.9 us
    all_to_all x4, starting transfers between devices, exchange(): return lax.all_to_all(v, axis, split_axis=0, concat_axis=0, tiled=True)  23.2 us
    ppermute x7, starting transfers between devices, per_device(): blocks[k] = lax.ppermute(blocks[k], 'head', ring)  15.3 us
    pallas_call x13, Pallas kernels, call(): pl.pallas_call(kernel, out_shape=[jax.ShapeDtypeStruct(shape, kind) for s...  15 us
    ppermute x2, waiting for transfers between devices, per_device(): other = lax.ppermute(w_part, 'head', [(i, i ^ far) for i in range(HEAD)])  10 us
    ppermute x1, waiting for transfers between devices, per_device(): other = lax.ppermute(w_part, 'head', [(i, i ^ 4) for i in range(HEAD)])  5.88 us
    ppermute x7, waiting for transfers between devices, per_device(): blocks[k] = lax.ppermute(blocks[k], 'head', ring)  4.44 us
  transfers between devices with their start and end apart: 14, of which 10 were waited for; matrix products, arithmetic and copies ran while one was open for 0% of the time, Pallas kernels for 4%

profile of v3, /device:TPU:32, one launch (start us, length us, event | category | flops | bytes accessed | tf_op | source)
XLA Modules:
  0.0 149.2 jit_solution(15381768435421759775)
XLA Ops:
  0.6 0.0 copy-start.3
  0.6 0.0 copy-start.6
  0.7 0.0 copy-start.7
  0.7 0.0 copy-start.8
  0.7 3.6 %shard_map.127 = bf16[8,32,1664]{2,1,0:T(8,128)(2,1)} custom-call(bf16[32,2560]{1,0:T(8,128)(2,1)} %hid_ref.1, bf16[2560,256]{1,0:T(8,128)(2,1)} %wbc_ref.1, bf16[80,2560]{1,0:T(8,128)(2,1)} %bitcast.9, bf16[32,5120]{1,0:T(8,128)(2,1)} %x_hbm.1, bf16[32,5120]{1,0:T(8,128)(2,1)} %g_hbm.1), custom_call_target="tpu_custom_call" | custom-call | tf_op jit(solution)/shard_map/pallas_call | solution.py:380
  4.3 8.6 %all-to-all-start = ((bf16[8,32,1664]{2,1,0:T(8,128)(2,1)}), bf16[8,32,1664]{2,1,0:T(8,128)(2,1)S(1)}, u32[]{:S(2)}, u32[]{:S(2)}) async-start(bf16[8,32,1664]{2,1,0:T(8,128)(2,1)} %shard_map.127), calls=%async_computation | async-start | bytes 1703936 | tf_op jit(solution)/shard_map/all_to_all | solution.py:406
  12.8 0.0 copy-done.3
  12.9 0.1 shard_map.128.hs_ref
  13.0 0.0 copy-done.6
  13.0 0.0 copy-done.7
  13.0 0.0 copy-done.8
  13.0 22.9 %all-to-all-done = bf16[8,32,1664]{2,1,0:T(8,128)(2,1)S(1)} async-done(((bf16[8,32,1664]{2,1,0:T(8,128)(2,1)}), bf16[8,32,1664]{2,1,0:T(8,128)(2,1)S(1)}, u32[]{:S(2)}, u32[]{:S(2)}) %all-to-all-start) | async-done | bytes 852000 | tf_op jit(solution)/shard_map/all_to_all | solution.py:406
  35.9 1.9 %shard_map.129 = bf16[16,16,1024]{2,1,0:T(8,128)(2,1)} custom-call(bf16[256,1664]{1,0:T(8,128)(2,1)S(1)} %bitcast.6, f32[8,128]{1,0:T(8,128)S(1)} %select_maximum_fusion.prm_ref, bf16[16,16,384]{2,1,0:T(8,128)(2,1)S(1)} %shard_map.128.hs_ref), custom_call_target="tpu_custom_call" | custom-call | tf_op jit(solution)/shard_map/pallas_call | solution.py:380
  37.8 7.0 %all-to-all-start.1 = ((bf16[16,16,1024]{2,1,0:T(8,128)(2,1)}), bf16[16,16,1024]{2,1,0:T(8,128)(2,1)S(1)}, u32[]{:S(2)}, u32[]{:S(2)}) async-start(bf16[16,16,1024]{2,1,0:T(8,128)(2,1)} %shard_map.129), calls=%async_computation.1 | async-start | bytes 1048576 | tf_op jit(solution)/shard_map/all_to_all | solution.py:406
  44.8 2.3 %shard_map.130.in_ref = f32[256,1664]{1,0:T(8,128)S(1)} custom-call(bf16[256,1664]{1,0:T(8,128)(2,1)S(1)} %bitcast.7, f32[8,128]{1,0:T(8,128)S(1)} %select_maximum_fusion.prm_ref), custom_call_target="tpu_custom_call" | custom-call | tf_op jit(solution)/shard_map/pallas_call | solution.py:380
  47.1 7.8 %all-to-all-done.1.r_ref.h_ref = bf16[16,16,1024]{2,1,0:T(8,128)(2,1)S(1)} async-done(((bf16[16,16,1024]{2,1,0:T(8,128)(2,1)}), bf16[16,16,1024]{2,1,0:T(8,128)(2,1)S(1)}, u32[]{:S(2)}, u32[]{:S(2)}) %all-to-all-start.1) | async-done | bytes 524320 | tf_op jit(solution)/shard_map/all_to_all | solution.py:406
  55.0 0.2 shard_map.131
  55.2 12.0 %all_to_all.30.st_ref = bf16[16,16,640]{2,1,0:T(8,128)(2,1)S(1)} all-to-all(bf16[16,16,640]{2,1,0:T(8,128)(2,1)S(1)} %shard_map.131), channel_id=1, replica_groups=mesh['seq'=16,'head'=8,'dp'=2] {'seq'}, dimensions={0} | all-to-all | bytes 655360 | tf_op jit(solution)/shard_map/all_to_all | solution.py:406
  67.2 0.0 copy-start.2
  67.2 2.6 %shard_map.132 = (bf16[8,32,384]{2,1,0:T(8,128)(2,1)S(1)}, bf16[256,1280]{1,0:T(8,128)(2,1)S(1)}) custom-call(bf16[256,1664]{1,0:T(8,128)(2,1)S(1)} %bitcast.8, f32[8,128]{1,0:T(8,128)S(1)} %select_maximum_fusion.prm_ref, bf16[16,16,640]{2,1,0:T(8,128)(2,1)S(1)} %all_to_all.30.st_ref, f32[256,1664]{1,0:T(8,128)S(1)} %shard_map.130.in_ref), custom_call_target="tpu_custom_call" | custom-call | tf_op jit(solution)/shard_map/pallas_call | solution.py:380
  69.9 0.0 copy-start.4
  69.9 0.8 copy-done.4
  70.7 0.0 copy-start.1
  70.7 13.9 %all_to_all.31.r_ref = bf16[8,32,384]{2,1,0:T(8,128)(2,1)S(1)} all-to-all(bf16[8,32,384]{2,1,0:T(8,128)(2,1)S(1)} %get-tuple-element.30), channel_id=1, replica_groups=mesh['seq'=16,'head'=8,'dp'=2] {'head'}, dimensions={0} | all-to-all | bytes 393216 | tf_op jit(solution)/shard_map/all_to_all | solution.py:406
  84.6 0.9 shard_map.133.d_ref
  85.4 3.6 %all-to-all-start.4 = ((bf16[16,32,384]{2,1,0:T(8,128)(2,1)}), bf16[16,32,384]{2,1,0:T(8,128)(2,1)S(1)}, u32[]{:S(2)}, u32[]{:S(2)}) async-start(bf16[16,32,384]{2,1,0:T(8,128)(2,1)} %shard_map.133.d_ref), calls=%async_computation.4 | async-start | bytes 786432 | tf_op jit(solution)/shard_map/all_to_all | solution.py:406
  89.0 0.0 copy-done.2
  89.0 0.0 copy-done.1
  89.0 2.3 %shard_map.134 = bf16[32,2560]{1,0:T(8,128)(2,1)} custom-call(bf16[16,32,384]{2,1,0:T(8,128)(2,1)} %shard_map.133.d_ref, bf16[2560,256]{1,0:T(8,128)(2,1)S(1)} %copy-done.1, bf16[80,2560]{1,0:T(8,128)(2,1)S(1)} %bitcast.10), custom_call_target="tpu_custom_call" | custom-call | tf_op jit(solution)/shard_map/pallas_call | solution.py:380
  91.3 7.1 %all-to-all-done.4.d_ref = bf16[16,32,384]{2,1,0:T(8,128)(2,1)S(1)} async-done(((bf16[16,32,384]{2,1,0:T(8,128)(2,1)}), bf16[16,32,384]{2,1,0:T(8,128)(2,1)S(1)}, u32[]{:S(2)}, u32[]{:S(2)}) %all-to-all-start.4) | async-done | bytes 393248 | tf_op jit(solution)/shard_map/all_to_all | solution.py:406
  98.4 0.9 shard_map.135
  99.2 1.5 collective-permute-start
  100.7 3.7 %collective-permute-done.b_ref = bf16[160,384]{1,0:T(8,128)(2,1)S(1)} collective-permute-done((bf16[160,384]{1,0:T(8,128)(2,1)S(1)}, bf16[160,384]{1,0:T(8,128)(2,1)S(1)}, u32[]{:S(2)}, u32[]{:S(2)}) %collective-permute-start) | collective-permute-done | bytes 122912 | tf_op jit(solution)/shard_map/ppermute | solution.py:463
  104.4 0.5 collective-permute-start.1
  104.9 6.3 %collective-permute-done.1.b_ref = bf16[160,384]{1,0:T(8,128)(2,1)S(1)} collective-permute-done((bf16[160,384]{1,0:T(8,128)(2,1)S(1)}, bf16[160,384]{1,0:T(8,128)(2,1)S(1)}, u32[]{:S(2)}, u32[]{:S(2)}) %collective-permute-start.1) | collective-permute-done | bytes 122912 | tf_op jit(solution)/shard_map/ppermute | solution.py:463
  111.3 3.0 %collective-permute-start.2 = (bf16[160,384]{1,0:T(8,128)(2,1)S(1)}, bf16[160,384]{1,0:T(8,128)(2,1)S(1)}, u32[]{:S(2)}, u32[]{:S(2)}) collective-permute-start(bf16[160,384]{1,0:T(8,128)(2,1)S(1)} %shard_map.137.a_ref), channel_id=1, source_target_pairs={{0,8},{2,10},{4,12},{6,14},{8,0},{10,2},{12,4},{14,6},{1,9},{3,11}... | collective-permute-start | bytes 368648 | tf_op jit(solution)/shard_map/ppermute | solution.py:465
  114.3 5.9 %collective-permute-done.2.b_ref = bf16[160,384]{1,0:T(8,128)(2,1)S(1)} collective-permute-done((bf16[160,384]{1,0:T(8,128)(2,1)S(1)}, bf16[160,384]{1,0:T(8,128)(2,1)S(1)}, u32[]{:S(2)}, u32[]{:S(2)}) %collective-permute-start.2) | collective-permute-done | bytes 122912 | tf_op jit(solution)/shard_map/ppermute | solution.py:465
  120.1 0.2 shard_map.138
  120.3 0.0 copy-start
  120.3 1.3 copy-done
  121.6 0.0 copy-start.5
  121.6 4.1 %all-to-all-start.5 = ((bf16[16,160,384]{2,1,0:T(8,128)(2,1)}), bf16[16,160,384]{2,1,0:T(8,128)(2,1)S(1)}, u32[]{:S(2)}, u32[]{:S(2)}) async-start(bf16[16,160,384]{2,1,0:T(8,128)(2,1)} %copy-done), calls=%async_computation.5 | async-start | bytes 3932160 | tf_op jit(solution)/shard_map/all_to_all | solution.py:406
  125.7 0.0 copy-done.5
  125.7 0.1 shard_map.139
  125.8 1.4 collective-permute-start.3
  127.2 3.7 %collective-permute-start.4 = (bf16[32,1280]{1,0:T(8,128)(2,1)S(1)}, bf16[32,1280]{1,0:T(8,128)(2,1)S(1)}, u32[]{:S(2)}, u32[]{:S(2)}) collective-permute-start(bf16[32,1280]{1,0:T(8,128)(2,1)S(1)} %get-tuple-element.37), channel_id=1, source_target_pairs={{0,4},{2,6},{4,8},{6,10},{8,12},{10,14},{12,0},{14,2},{1,5},{3,7},... | collective-permute-start | bytes 245768 | tf_op jit(solution)/shard_map/ppermute | solution.py:476
  130.9 1.0 collective-permute-start.5
  131.9 3.8 %collective-permute-start.6 = (bf16[32,1280]{1,0:T(8,128)(2,1)S(1)}, bf16[32,1280]{1,0:T(8,128)(2,1)S(1)}, u32[]{:S(2)}, u32[]{:S(2)}) collective-permute-start(bf16[32,1280]{1,0:T(8,128)(2,1)S(1)} %get-tuple-element.39), channel_id=1, source_target_pairs={{0,8},{2,10},{4,12},{6,14},{8,0},{10,2},{12,4},{14,6},{1,9},{3,11}... | collective-permute-start | bytes 245768 | tf_op jit(solution)/shard_map/ppermute | solution.py:476
  135.7 3.5 %collective-permute-start.7 = (bf16[32,1280]{1,0:T(8,128)(2,1)S(1)}, bf16[32,1280]{1,0:T(8,128)(2,1)S(1)}, u32[]{:S(2)}, u32[]{:S(2)}) collective-permute-start(bf16[32,1280]{1,0:T(8,128)(2,1)S(1)} %get-tuple-element.40), channel_id=1, source_target_pairs={{0,10},{2,12},{4,14},{6,0},{8,2},{10,4},{12,6},{14,8},{1,11},{3,13... | collective-permute-start | bytes 245768 | tf_op jit(solution)/shard_map/ppermute | solution.py:476
  139.2 0.0 collective-permute-done.3.refs_1_
  139.2 0.0 collective-permute-start.8
  139.2 0.0 collective-permute-done.4.refs_2_
  139.2 1.8 %collective-permute-start.9 = (bf16[32,1280]{1,0:T(8,128)(2,1)S(1)}, bf16[32,1280]{1,0:T(8,128)(2,1)S(1)}, u32[]{:S(2)}, u32[]{:S(2)}) collective-permute-start(bf16[32,1280]{1,0:T(8,128)(2,1)S(1)} %get-tuple-element.42), channel_id=1, source_target_pairs={{0,14},{2,0},{4,2},{6,4},{8,6},{10,8},{12,10},{14,12},{1,15},{3,1}... | collective-permute-start | bytes 245768 | tf_op jit(solution)/shard_map/ppermute | solution.py:476
  141.1 0.0 collective-permute-done.5.refs_3_
  141.1 0.0 collective-permute-done.6.refs_4_
  141.1 2.1 %collective-permute-done.7.refs_5_ = bf16[32,1280]{1,0:T(8,128)(2,1)S(1)} collective-permute-done((bf16[32,1280]{1,0:T(8,128)(2,1)S(1)}, bf16[32,1280]{1,0:T(8,128)(2,1)S(1)}, u32[]{:S(2)}, u32[]{:S(2)}) %collective-permute-start.7) | collective-permute-done | bytes 81952 | tf_op jit(solution)/shard_map/ppermute | solution.py:476
  143.2 2.2 %collective-permute-done.8.refs_6_ = bf16[32,1280]{1,0:T(8,128)(2,1)S(1)} collective-permute-done((bf16[32,1280]{1,0:T(8,128)(2,1)S(1)}, bf16[32,1280]{1,0:T(8,128)(2,1)S(1)}, u32[]{:S(2)}, u32[]{:S(2)}) %collective-permute-start.8) | collective-permute-done | bytes 81952 | tf_op jit(solution)/shard_map/ppermute | solution.py:476
  145.4 0.1 collective-permute-done.9.refs_7_
  145.5 1.0 shard_map.140
  146.5 0.6 all-to-all-done.5.r_ref
  147.1 1.9 %shard_map.141 = (f32[2560,256]{1,0:T(8,128)}, f32[80,2560]{1,0:T(8,128)}) custom-call(bf16[16,160,384]{2,1,0:T(8,128)(2,1)S(1)} %all-to-all-done.5.r_ref), custom_call_target="tpu_custom_call" | custom-call | tf_op jit(solution)/shard_map/pallas_call | solution.py:391
  (3 shorter events, 0.1 us)
Async XLA Ops:
  0.6 12.2 %copy-start.3 = (bf16[32,2560]{1,0:T(8,128)(2,1)S(1)}, bf16[32,2560]{1,0:T(8,128)(2,1)}, u32[]{:S(2)}) copy-start(bf16[32,2560]{1,0:T(8,128)(2,1)} %hid_ref.1) | copy-start | bytes 491524
  0.6 12.3 %copy-start.6 = (f32[80]{0:T(128)S(1)}, f32[80]{0:T(128)}, u32[]{:S(2)}) copy-start(f32[80]{0:T(128)} %param.15) | copy-start | bytes 964
  0.7 12.3 %copy-start.7 = (f32[80]{0:T(128)S(1)}, f32[80]{0:T(128)}, u32[]{:S(2)}) copy-start(f32[80]{0:T(128)} %param.14) | copy-start | bytes 964
  0.7 12.3 %copy-start.8 = (f32[80]{0:T(128)S(1)}, f32[80]{0:T(128)}, u32[]{:S(2)}) copy-start(f32[80]{0:T(128)} %param.13) | copy-start | bytes 964
  4.3 31.6 %all-to-all-start = ((bf16[8,32,1664]{2,1,0:T(8,128)(2,1)}), bf16[8,32,1664]{2,1,0:T(8,128)(2,1)S(1)}, u32[]{:S(2)}, u32[]{:S(2)}) async-start(bf16[8,32,1664]{2,1,0:T(8,128)(2,1)} %shard_map.127), calls=%async_computation | async-start | bytes 1703936 | tf_op jit(solution)/shard_map/all_to_all | solution.py:406
  37.8 17.2 %all-to-all-start.1 = ((bf16[16,16,1024]{2,1,0:T(8,128)(2,1)}), bf16[16,16,1024]{2,1,0:T(8,128)(2,1)S(1)}, u32[]{:S(2)}, u32[]{:S(2)}) async-start(bf16[16,16,1024]{2,1,0:T(8,128)(2,1)} %shard_map.129), calls=%async_computation.1 | async-start | bytes 1048576 | tf_op jit(solution)/shard_map/all_to_all | solution.py:406
  67.2 21.8 %copy-start.2 = (bf16[2560,80]{0,1:T(8,128)(2,1)S(1)}, bf16[2560,80]{0,1:T(8,128)(2,1)}, u32[]{:S(2)}) copy-start(bf16[2560,80]{0,1:T(8,128)(2,1)} %param.12) | copy-start | bytes 1228804
  69.9 0.8 copy-start.4
  70.7 18.3 %copy-start.1 = (bf16[2560,256]{1,0:T(8,128)(2,1)S(1)}, bf16[2560,256]{1,0:T(8,128)(2,1)}, u32[]{:S(2)}) copy-start(bf16[2560,256]{1,0:T(8,128)(2,1)} %wbc_ref.1) | copy-start | bytes 3932164
  85.4 12.9 %all-to-all-start.4 = ((bf16[16,32,384]{2,1,0:T(8,128)(2,1)}), bf16[16,32,384]{2,1,0:T(8,128)(2,1)S(1)}, u32[]{:S(2)}, u32[]{:S(2)}) async-start(bf16[16,32,384]{2,1,0:T(8,128)(2,1)} %shard_map.133.d_ref), calls=%async_computation.4 | async-start | bytes 786432 | tf_op jit(solution)/shard_map/all_to_all | solution.py:406
  99.2 5.1 %collective-permute-start = (bf16[160,384]{1,0:T(8,128)(2,1)S(1)}, bf16[160,384]{1,0:T(8,128)(2,1)S(1)}, u32[]{:S(2)}, u32[]{:S(2)}) collective-permute-start(bf16[160,384]{1,0:T(8,128)(2,1)S(1)} %get-tuple-element.32.a_ref), channel_id=1, source_target_pairs={{0,2},{2,0},{4,6},{6,4},{8,10},{10,8},{12,14},{14,12},{1,3},{3,1},... | collective-permute-start | bytes 368648 | tf_op jit(solution)/shard_map/ppermute | solution.py:463
  104.4 6.8 %collective-permute-start.1 = (bf16[160,384]{1,0:T(8,128)(2,1)S(1)}, bf16[160,384]{1,0:T(8,128)(2,1)S(1)}, u32[]{:S(2)}, u32[]{:S(2)}) collective-permute-start(bf16[160,384]{1,0:T(8,128)(2,1)S(1)} %shard_map.136.a_ref), channel_id=1, source_target_pairs={{0,4},{2,6},{4,0},{6,2},{8,12},{10,14},{12,8},{14,10},{1,5},{3,7},... | collective-permute-start | bytes 368648 | tf_op jit(solution)/shard_map/ppermute | solution.py:463
  111.3 8.9 %collective-permute-start.2 = (bf16[160,384]{1,0:T(8,128)(2,1)S(1)}, bf16[160,384]{1,0:T(8,128)(2,1)S(1)}, u32[]{:S(2)}, u32[]{:S(2)}) collective-permute-start(bf16[160,384]{1,0:T(8,128)(2,1)S(1)} %shard_map.137.a_ref), channel_id=1, source_target_pairs={{0,8},{2,10},{4,12},{6,14},{8,0},{10,2},{12,4},{14,6},{1,9},{3,11}... | collective-permute-start | bytes 368648 | tf_op jit(solution)/shard_map/ppermute | solution.py:465
  120.3 1.3 copy-start
  121.6 4.1 %copy-start.5 = (bf16[256,1280]{1,0:T(8,128)(2,1)S(1)}, bf16[256,1280]{1,0:T(8,128)(2,1)}, u32[]{:S(2)}) copy-start(bf16[256,1280]{1,0:T(8,128)(2,1)} %copy-done.4) | copy-start | bytes 1966084
  121.6 25.5 %all-to-all-start.5 = ((bf16[16,160,384]{2,1,0:T(8,128)(2,1)}), bf16[16,160,384]{2,1,0:T(8,128)(2,1)S(1)}, u32[]{:S(2)}, u32[]{:S(2)}) async-start(bf16[16,160,384]{2,1,0:T(8,128)(2,1)} %copy-done), calls=%async_computation.5 | async-start | bytes 3932160 | tf_op jit(solution)/shard_map/all_to_all | solution.py:406
  125.8 13.5 %collective-permute-start.3 = (bf16[32,1280]{1,0:T(8,128)(2,1)S(1)}, bf16[32,1280]{1,0:T(8,128)(2,1)S(1)}, u32[]{:S(2)}, u32[]{:S(2)}) collective-permute-start(bf16[32,1280]{1,0:T(8,128)(2,1)S(1)} %get-tuple-element.36), channel_id=1, source_target_pairs={{0,2},{2,4},{4,6},{6,8},{8,10},{10,12},{12,14},{14,0},{1,3},{3,5},... | collective-permute-start | bytes 245768 | tf_op jit(solution)/shard_map/ppermute | solution.py:476
  127.2 12.1 %collective-permute-start.4 = (bf16[32,1280]{1,0:T(8,128)(2,1)S(1)}, bf16[32,1280]{1,0:T(8,128)(2,1)S(1)}, u32[]{:S(2)}, u32[]{:S(2)}) collective-permute-start(bf16[32,1280]{1,0:T(8,128)(2,1)S(1)} %get-tuple-element.37), channel_id=1, source_target_pairs={{0,4},{2,6},{4,8},{6,10},{8,12},{10,14},{12,0},{14,2},{1,5},{3,7},... | collective-permute-start | bytes 245768 | tf_op jit(solution)/shard_map/ppermute | solution.py:476
  130.9 10.2 %collective-permute-start.5 = (bf16[32,1280]{1,0:T(8,128)(2,1)S(1)}, bf16[32,1280]{1,0:T(8,128)(2,1)S(1)}, u32[]{:S(2)}, u32[]{:S(2)}) collective-permute-start(bf16[32,1280]{1,0:T(8,128)(2,1)S(1)} %get-tuple-element.38), channel_id=1, source_target_pairs={{0,6},{2,8},{4,10},{6,12},{8,14},{10,0},{12,2},{14,4},{1,7},{3,9},... | collective-permute-start | bytes 245768 | tf_op jit(solution)/shard_map/ppermute | solution.py:476
  131.9 9.2 %collective-permute-start.6 = (bf16[32,1280]{1,0:T(8,128)(2,1)S(1)}, bf16[32,1280]{1,0:T(8,128)(2,1)S(1)}, u32[]{:S(2)}, u32[]{:S(2)}) collective-permute-start(bf16[32,1280]{1,0:T(8,128)(2,1)S(1)} %get-tuple-element.39), channel_id=1, source_target_pairs={{0,8},{2,10},{4,12},{6,14},{8,0},{10,2},{12,4},{14,6},{1,9},{3,11}... | collective-permute-start | bytes 245768 | tf_op jit(solution)/shard_map/ppermute | solution.py:476
  135.7 7.5 %collective-permute-start.7 = (bf16[32,1280]{1,0:T(8,128)(2,1)S(1)}, bf16[32,1280]{1,0:T(8,128)(2,1)S(1)}, u32[]{:S(2)}, u32[]{:S(2)}) collective-permute-start(bf16[32,1280]{1,0:T(8,128)(2,1)S(1)} %get-tuple-element.40), channel_id=1, source_target_pairs={{0,10},{2,12},{4,14},{6,0},{8,2},{10,4},{12,6},{14,8},{1,11},{3,13... | collective-permute-start | bytes 245768 | tf_op jit(solution)/shard_map/ppermute | solution.py:476
  139.2 6.2 %collective-permute-start.8 = (bf16[32,1280]{1,0:T(8,128)(2,1)S(1)}, bf16[32,1280]{1,0:T(8,128)(2,1)S(1)}, u32[]{:S(2)}, u32[]{:S(2)}) collective-permute-start(bf16[32,1280]{1,0:T(8,128)(2,1)S(1)} %get-tuple-element.41), channel_id=1, source_target_pairs={{0,12},{2,14},{4,0},{6,2},{8,4},{10,6},{12,8},{14,10},{1,13},{3,15... | collective-permute-start | bytes 245768 | tf_op jit(solution)/shard_map/ppermute | solution.py:476
  139.2 6.3 %collective-permute-start.9 = (bf16[32,1280]{1,0:T(8,128)(2,1)S(1)}, bf16[32,1280]{1,0:T(8,128)(2,1)S(1)}, u32[]{:S(2)}, u32[]{:S(2)}) collective-permute-start(bf16[32,1280]{1,0:T(8,128)(2,1)S(1)} %get-tuple-element.42), channel_id=1, source_target_pairs={{0,14},{2,0},{4,2},{6,4},{8,6},{10,8},{12,10},{14,12},{1,15},{3,1}... | collective-permute-start | bytes 245768 | tf_op jit(solution)/shard_map/ppermute | solution.py:476

commit v4 on v3

--- a/solution.py
+++ b/solution.py
@@ -11,6 +11,7 @@
 BF16 = jnp.bfloat16
 LANES = 128
 LIMIT = 24 * 2**20
+NEAR = 52 * 2**20
 FULL = 60 * 2**20
 
 SEQ, HEAD = 16, 8
@@ -71,63 +72,55 @@
     return prm[0:1], -jnp.exp(prm[1:2]), prm[2:3]
 
 
-def step_sizes(r_ref, prm_ref):
+def step_sizes(r_ref, prm_ref, cum=None):
     bias, rate, skip = head_params(prm_ref)
     pre = r_ref[:, STEP:].astype(F32) + bias
     step = jnp.maximum(pre, 0.0) + jnp.log1p(jnp.exp(-jnp.abs(pre)))
-    cum = running_sum(triangle(0), step * rate)
+    if cum is None:
+        cum = running_sum(triangle(0), step * rate)
     return pre, step, cum, rate, skip
 
 
 def project_kernel(
-    hid_hbm, wbc_hbm, wdt_hbm, x_hbm, g_hbm, send_hbm, tail_ref, x_ref, g_ref, hid_ref, wbc_ref, wdt_ref, sems
+    hid_hbm, wbc_hbm, wdt_hbm, x_hbm, g_hbm, send_hbm, pack_ref, x_ref, g_ref, hid_ref, wbc_ref, wdt_ref, sems
 ):
-    rows = D // STAGES
-    chunks = [slice(i * rows, (i + 1) * rows) for i in range(STAGES)]
-    first = [
-        pltpu.make_async_copy(hid_hbm, hid_ref, sems.at[0]),
-        pltpu.make_async_copy(wdt_hbm, wdt_ref, sems.at[1]),
+    half = D // 2
+    halves = [slice(0, half), slice(half, D)]
+    come = [
+        pltpu.make_async_copy(far, near, sems.at[i])
+        for i, (far, near) in enumerate(
+            [(x_hbm, x_ref), (g_hbm, g_ref), (hid_hbm, hid_ref), (wdt_hbm, wdt_ref)]
+            + [(wbc_hbm.at[at], wbc_ref.at[at]) for at in halves]
+        )
     ]
-    for i, at in enumerate(chunks):
-        first.append(pltpu.make_async_copy(wbc_hbm.at[at], wbc_ref.at[at], sems.at[2 + i]))
-    given = []
-    for i, (far, near) in enumerate(((x_hbm, x_ref), (g_hbm, g_ref))):
-        given.append(pltpu.make_async_copy(far, near, sems.at[2 + STAGES + i]))
-    for copy in first + given:
+    go = [
+        pltpu.make_async_copy(pack_ref.at[:, :, at], send_hbm.at[:, :, at], sems.at[len(come) + i])
+        for i, at in enumerate((slice(0, 2 * CH), slice(2 * CH, PACK)))
+    ]
+    for copy in come:
         copy.start()
-    rest = []
-    for i, near in enumerate((x_ref, g_ref)):
-        given[i].wait()
+    for i, ref in enumerate((x_ref, g_ref)):
+        come[i].wait()
         for k in range(HEAD):
-            rest.append(
-                pltpu.make_async_copy(
-                    near.at[:, k * CH : (k + 1) * CH],
-                    send_hbm.at[k, :, i * CH : (i + 1) * CH],
-                    sems.at[4 + STAGES + 2 * k + i],
-                )
-            )
-            rest[-1].start()
-    first[0].wait()
-    first[1].wait()
+            pack_ref[k, :, i * CH : (i + 1) * CH] = ref[:, k * CH : (k + 1) * CH]
+    go[0].start()
+    come[2].wait()
+    come[3].wait()
     raw = dot(hid_ref[...], wdt_ref[...], 1, 1).astype(BF16).astype(F32)
     raw = jnp.concatenate([raw, jnp.zeros((TOKENS, LANES - H), F32)], axis=1)
     lane = iota((TOKENS, LANES), 1)
     for k in range(HEAD):
         mine = pltpu.roll(raw, (LANES - HEADS * k) % LANES, 1)
-        tail_ref[k, :, 2 * N :] = jnp.where(lane < HEADS, mine, 0.0).astype(BF16)
+        pack_ref[k, :, STEP:] = jnp.where(lane < HEADS, mine, 0.0).astype(BF16)
     bc = jnp.zeros((TOKENS, 2 * N), F32)
-    for i, at in enumerate(chunks):
-        first[2 + i].wait()
+    for i, at in enumerate(halves):
+        come[4 + i].wait()
         bc += dot(hid_ref[:, at], wbc_ref[at])
     for k in range(HEAD):
-        tail_ref[k, :, : 2 * N] = bc.astype(BF16)
-    last = pltpu.make_async_copy(
-        tail_ref, send_hbm.at[:, :, 2 * CH :], sems.at[4 + STAGES + 2 * HEAD]
-    )
-    last.start()
-    for copy in rest:
+        pack_ref[k, :, 2 * CH : STEP] = bc.astype(BF16)
+    go[1].start()
+    for copy in go:
         copy.wait()
-    last.wait()
 
 
 def slab_kernel(hid_ref, hs_ref):
@@ -218,14 +211,15 @@
         out_ref[:, at] = y
         out_ref[:, CH + j * LANES : CH + (j + 1) * LANES] = du
         products.append(g.astype(F32) * y - u.astype(F32) * du)
-    out_ref[:, STEP:] = gather_heads(jnp.concatenate(products, axis=1), hot, 3)
+    out_ref[:, PACK:] = cum
+    out_ref[:, STEP:PACK] = gather_heads(jnp.concatenate(products, axis=1), hot, 3)
     ds = ds_ref[...]
     out_ref[:, 2 * CH : 2 * CH + N] = dot(ds.T.astype(BF16), c)
     out_ref[:, 2 * CH + N : STEP] = dot(ds.astype(BF16), b)
 
 
 def carry_kernel(r_ref, prm_ref, st_ref, in_ref, send_ref, both_ref):
-    pre, step, cum, rate, skip = step_sizes(r_ref, prm_ref)
+    pre, step, cum, rate, skip = step_sizes(r_ref, prm_ref, in_ref[:, PACK:])
     hot = one_hot()
     total = cum[SPAN - 1 :]
     step_x = spread(step, hot)
@@ -249,7 +243,7 @@
     gx = step_x * du + skip_x * g
     d_c = in_ref[:, 2 * CH + N : STEP] + dot((g * from_start).astype(BF16), s_b, 1, 1)
     d_b = in_ref[:, 2 * CH : 2 * CH + N] + dot((u * to_end).astype(BF16), q_b, 1, 1)
-    e = in_ref[:, STEP:] + gather_heads(g * carried, hot)
+    e = in_ref[:, STEP:PACK] + gather_heads(g * carried, hot)
     f = gather_heads(u * late, hot)
     xdu = gather_heads(x * du, hot)
     sums = jnp.concatenate(
@@ -313,21 +307,12 @@
 
 
 def finish_kernel(*refs):
-    blocks, (y_hbm, gx_hbm), sems = refs[:HEAD], refs[HEAD : HEAD + 2], refs[HEAD + 2]
-    copies = []
+    blocks, outs = refs[:HEAD], refs[HEAD:]
     for k in range(HEAD):
         of = lax.rem(lax.axis_index("head") + HEAD - k, HEAD)
         cols = pl.ds(pl.multiple_of(of * CH, LANES), CH)
-        for i, out in enumerate((y_hbm, gx_hbm)):
-            copies.append(
-                pltpu.make_async_copy(
-                    blocks[k].at[:, i * CH : (i + 1) * CH], out.at[:, cols], sems.at[k, i]
-                )
-            )
-    for copy in copies:
-        copy.start()
-    for copy in copies:
-        copy.wait()
+        for i, out_ref in enumerate(outs):
+            out_ref[:, cols] = blocks[k][:, i * CH : (i + 1) * CH]
 
 
 def weight_kernel(d_ref, h_ref, send_ref, par_ref):
@@ -413,13 +398,13 @@
         [((HEAD, TOKENS, PACK), BF16)],
         hidden, bc_weight, dt_weight.T, x_input, grad_out,
         scratch=[
-            pltpu.VMEM((HEAD, TOKENS, DPACK), BF16),
+            pltpu.VMEM((HEAD, TOKENS, PACK), BF16),
             pltpu.VMEM((TOKENS, H * WIDTH), BF16),
             pltpu.VMEM((TOKENS, H * WIDTH), BF16),
             pltpu.VMEM((TOKENS, D), BF16),
             pltpu.VMEM((D, 2 * N), BF16),
             pltpu.VMEM((H, D), BF16),
-            pltpu.SemaphoreType.DMA((5 + STAGES + 2 * HEAD,)),
+            pltpu.SemaphoreType.DMA((8,)),
         ],
         far=True,
         far_out=True,
@@ -433,7 +418,7 @@
     totals = exchange(sent, "seq")
     [inner] = call(
         inner_kernel,
-        [((SPAN, PACK), F32)],
+        [((SPAN, PACK + LANES), F32)],
         mine, prm,
         scratch=[pltpu.VMEM((SPAN, SPAN), F32)],
     )
@@ -467,6 +452,7 @@
         spread_kernel,
         [((SEQ, COLS, DPACK), BF16)],
         w_part, other,
+        limit=NEAR,
     )
     w_sum, both = lax.optimization_barrier((w_sum, both))
     w_all = exchange(w_sum, "seq")
@@ -474,14 +460,9 @@
     for k in range(1, HEAD):
         ring = [(i, (i + k) % HEAD) for i in range(HEAD)]
         blocks[k] = lax.ppermute(blocks[k], "head", ring)
-    mixer_out, grad_x = pl.pallas_call(
-        finish_kernel,
-        out_shape=[jax.ShapeDtypeStruct((TOKENS, H * WIDTH), BF16)] * 2,
-        in_specs=[pl.BlockSpec(memory_space=pl.ANY)] * HEAD,
-        out_specs=[pl.BlockSpec(memory_space=pltpu.HBM)] * 2,
-        scratch_shapes=[pltpu.SemaphoreType.DMA((HEAD, 2))],
-        compiler_params=pltpu.CompilerParams(vmem_limit_bytes=LIMIT),
-    )(*blocks)
+    mixer_out, grad_x = call(
+        finish_kernel, [((TOKENS, H * WIDTH), BF16)] * 2, *blocks
+    )
     grad_bc_weight, grad_dt_weight = unpack(w_all)
     return (mixer_out, grad_x, grad_hidden, grad_bc_weight, grad_dt_weight.T, param_grads)
 

time: 151 us -> 150 us (level)
    pallas_call x13 -> x14, Pallas kernels: 15 us -> 16.5 us  [call(): pl.pallas_call(kernel, out_shape=[jax.ShapeDtypeStruct(shape, kind) for s...]
where the time goes in v4:
time: 150 us; the launch traced here: 148 us
  waiting for transfers between devices  58.9 us (39%)
  starting transfers between devices  43.4 us (29%)
  blocking collectives  25.9 us (17%)
  Pallas kernels  18.4 us (12%)
    all_to_all x4, waiting for transfers between devices, exchange(): return lax.all_to_all(v, axis, split_axis=0, concat_axis=0, tiled=True)  38.5 us
    all_to_all x2, blocking collectives, exchange(): return lax.all_to_all(v, axis, split_axis=0, concat_axis=0, tiled=True)  25.9 us
    all_to_all x4, starting transfers between devices, exchange(): return lax.all_to_all(v, axis, split_axis=0, concat_axis=0, tiled=True)  23.2 us
    pallas_call x14, Pallas kernels, call(): pl.pallas_call(kernel, out_shape=[jax.ShapeDtypeStruct(shape, kind) for s...  16.5 us
    ppermute x7, starting transfers between devices, per_device(): blocks[k] = lax.ppermute(blocks[k], 'head', ring)  15.3 us
    ppermute x2, waiting for transfers between devices, per_device(): other = lax.ppermute(w_part, 'head', [(i, i ^ far) for i in range(HEAD)])  10.1 us
    ppermute x1, waiting for transfers between devices, per_device(): other = lax.ppermute(w_part, 'head', [(i, i ^ 4) for i in range(HEAD)])  5.96 us
    ppermute x7, waiting for transfers between devices, per_device(): blocks[k] = lax.ppermute(blocks[k], 'head', ring)  4.42 us
  transfers between devices with their start and end apart: 14, of which 10 were waited for; matrix products, arithmetic and copies ran while one was open for 0% of the time, Pallas kernels for 4%

profile of v4, /device:TPU:32, one launch (start us, length us, event | category | flops | bytes accessed | tf_op | source)
XLA Modules:
  0.0 148.4 jit_solution(3651765866956248259)
XLA Ops:
  0.6 0.0 copy-start.2
  0.6 0.0 copy-start.5
  0.7 0.0 copy-start.6
  0.7 0.0 copy-start.7
  0.7 2.9 %shard_map.127 = bf16[8,32,1664]{2,1,0:T(8,128)(2,1)} custom-call(bf16[32,2560]{1,0:T(8,128)(2,1)} %hid_ref.1, bf16[2560,256]{1,0:T(8,128)(2,1)} %wbc_ref.1, bf16[80,2560]{1,0:T(8,128)(2,1)} %bitcast.9, bf16[32,5120]{1,0:T(8,128)(2,1)} %x_hbm.1, bf16[32,5120]{1,0:T(8,128)(2,1)} %g_hbm.1), custom_call_target="tpu_custom_call" | custom-call | tf_op jit(solution)/shard_map/pallas_call | solution.py:365
  3.6 8.6 %all-to-all-start = ((bf16[8,32,1664]{2,1,0:T(8,128)(2,1)}), bf16[8,32,1664]{2,1,0:T(8,128)(2,1)S(1)}, u32[]{:S(2)}, u32[]{:S(2)}) async-start(bf16[8,32,1664]{2,1,0:T(8,128)(2,1)} %shard_map.127), calls=%async_computation | async-start | bytes 1703936 | tf_op jit(solution)/shard_map/all_to_all | solution.py:391
  12.2 0.0 copy-done.2
  12.2 0.1 shard_map.128.hs_ref
  12.3 0.0 copy-done.5
  12.3 0.0 copy-done.6
  12.3 0.0 copy-done.7
  12.4 22.9 %all-to-all-done = bf16[8,32,1664]{2,1,0:T(8,128)(2,1)S(1)} async-done(((bf16[8,32,1664]{2,1,0:T(8,128)(2,1)}), bf16[8,32,1664]{2,1,0:T(8,128)(2,1)S(1)}, u32[]{:S(2)}, u32[]{:S(2)}) %all-to-all-start) | async-done | bytes 852000 | tf_op jit(solution)/shard_map/all_to_all | solution.py:391
  35.3 1.9 %shard_map.129 = bf16[16,16,1024]{2,1,0:T(8,128)(2,1)} custom-call(bf16[256,1664]{1,0:T(8,128)(2,1)S(1)} %bitcast.6, f32[8,128]{1,0:T(8,128)S(1)} %select_maximum_fusion.prm_ref, bf16[16,16,384]{2,1,0:T(8,128)(2,1)S(1)} %shard_map.128.hs_ref), custom_call_target="tpu_custom_call" | custom-call | tf_op jit(solution)/shard_map/pallas_call | solution.py:365
  37.1 7.0 %all-to-all-start.1 = ((bf16[16,16,1024]{2,1,0:T(8,128)(2,1)}), bf16[16,16,1024]{2,1,0:T(8,128)(2,1)S(1)}, u32[]{:S(2)}, u32[]{:S(2)}) async-start(bf16[16,16,1024]{2,1,0:T(8,128)(2,1)} %shard_map.129), calls=%async_computation.1 | async-start | bytes 1048576 | tf_op jit(solution)/shard_map/all_to_all | solution.py:391
  44.2 2.3 %shard_map.130.in_ref = f32[256,1792]{1,0:T(8,128)S(1)} custom-call(bf16[256,1664]{1,0:T(8,128)(2,1)S(1)} %bitcast.7, f32[8,128]{1,0:T(8,128)S(1)} %select_maximum_fusion.prm_ref), custom_call_target="tpu_custom_call" | custom-call | tf_op jit(solution)/shard_map/pallas_call | solution.py:365
  46.5 7.8 %all-to-all-done.1.r_ref.h_ref = bf16[16,16,1024]{2,1,0:T(8,128)(2,1)S(1)} async-done(((bf16[16,16,1024]{2,1,0:T(8,128)(2,1)}), bf16[16,16,1024]{2,1,0:T(8,128)(2,1)S(1)}, u32[]{:S(2)}, u32[]{:S(2)}) %all-to-all-start.1) | async-done | bytes 524320 | tf_op jit(solution)/shard_map/all_to_all | solution.py:391
  54.3 0.2 shard_map.131
  54.6 12.0 %all_to_all.30.st_ref = bf16[16,16,640]{2,1,0:T(8,128)(2,1)S(1)} all-to-all(bf16[16,16,640]{2,1,0:T(8,128)(2,1)S(1)} %shard_map.131), channel_id=1, replica_groups=mesh['seq'=16,'head'=8,'dp'=2] {'seq'}, dimensions={0} | all-to-all | bytes 655360 | tf_op jit(solution)/shard_map/all_to_all | solution.py:391
  66.6 2.5 %shard_map.132 = (bf16[8,32,384]{2,1,0:T(8,128)(2,1)S(1)}, bf16[256,1280]{1,0:T(8,128)(2,1)S(1)}) custom-call(bf16[256,1664]{1,0:T(8,128)(2,1)S(1)} %bitcast.8, f32[8,128]{1,0:T(8,128)S(1)} %select_maximum_fusion.prm_ref, bf16[16,16,640]{2,1,0:T(8,128)(2,1)S(1)} %all_to_all.30.st_ref, f32[256,1792]{1,0:T(8,128)S(1)} %shard_map.130.in_ref), custom_call_target="tpu_custom_call" | custom-call | tf_op jit(solution)/shard_map/pallas_call | solution.py:365
  69.1 0.0 copy-start.3
  69.1 0.8 copy-done.3
  69.9 0.0 copy-start
  69.9 0.0 copy-start.1
  69.9 13.9 %all_to_all.31.r_ref = bf16[8,32,384]{2,1,0:T(8,128)(2,1)S(1)} all-to-all(bf16[8,32,384]{2,1,0:T(8,128)(2,1)S(1)} %get-tuple-element.30), channel_id=1, replica_groups=mesh['seq'=16,'head'=8,'dp'=2] {'head'}, dimensions={0} | all-to-all | bytes 393216 | tf_op jit(solution)/shard_map/all_to_all | solution.py:391
  83.8 0.9 shard_map.133.d_ref
  84.7 3.6 %all-to-all-start.4 = ((bf16[16,32,384]{2,1,0:T(8,128)(2,1)}), bf16[16,32,384]{2,1,0:T(8,128)(2,1)S(1)}, u32[]{:S(2)}, u32[]{:S(2)}) async-start(bf16[16,32,384]{2,1,0:T(8,128)(2,1)} %shard_map.133.d_ref), calls=%async_computation.4 | async-start | bytes 786432 | tf_op jit(solution)/shard_map/all_to_all | solution.py:391
  88.2 0.0 copy-done
  88.2 0.0 copy-done.1
  88.2 2.3 %shard_map.134 = bf16[32,2560]{1,0:T(8,128)(2,1)} custom-call(bf16[16,32,384]{2,1,0:T(8,128)(2,1)} %shard_map.133.d_ref, bf16[2560,256]{1,0:T(8,128)(2,1)S(1)} %copy-done, bf16[80,2560]{1,0:T(8,128)(2,1)S(1)} %bitcast.10), custom_call_target="tpu_custom_call" | custom-call | tf_op jit(solution)/shard_map/pallas_call | solution.py:365
  90.5 7.1 %all-to-all-done.4.d_ref = bf16[16,32,384]{2,1,0:T(8,128)(2,1)S(1)} async-done(((bf16[16,32,384]{2,1,0:T(8,128)(2,1)}), bf16[16,32,384]{2,1,0:T(8,128)(2,1)S(1)}, u32[]{:S(2)}, u32[]{:S(2)}) %all-to-all-start.4) | async-done | bytes 393248 | tf_op jit(solution)/shard_map/all_to_all | solution.py:391
  97.6 0.9 shard_map.135
  98.4 1.5 collective-permute-start
  99.9 3.7 %collective-permute-done.b_ref = bf16[160,384]{1,0:T(8,128)(2,1)S(1)} collective-permute-done((bf16[160,384]{1,0:T(8,128)(2,1)S(1)}, bf16[160,384]{1,0:T(8,128)(2,1)S(1)}, u32[]{:S(2)}, u32[]{:S(2)}) %collective-permute-start) | collective-permute-done | bytes 122912 | tf_op jit(solution)/shard_map/ppermute | solution.py:448
  103.6 0.5 collective-permute-start.1
  104.1 6.4 %collective-permute-done.1.b_ref = bf16[160,384]{1,0:T(8,128)(2,1)S(1)} collective-permute-done((bf16[160,384]{1,0:T(8,128)(2,1)S(1)}, bf16[160,384]{1,0:T(8,128)(2,1)S(1)}, u32[]{:S(2)}, u32[]{:S(2)}) %collective-permute-start.1) | collective-permute-done | bytes 122912 | tf_op jit(solution)/shard_map/ppermute | solution.py:448
  110.6 2.9 %collective-permute-start.2 = (bf16[160,384]{1,0:T(8,128)(2,1)S(1)}, bf16[160,384]{1,0:T(8,128)(2,1)S(1)}, u32[]{:S(2)}, u32[]{:S(2)}) collective-permute-start(bf16[160,384]{1,0:T(8,128)(2,1)S(1)} %shard_map.137.a_ref), channel_id=1, source_target_pairs={{0,8},{2,10},{4,12},{6,14},{8,0},{10,2},{12,4},{14,6},{1,9},{3,11}... | collective-permute-start | bytes 368648 | tf_op jit(solution)/shard_map/ppermute | solution.py:450
  113.5 6.0 %collective-permute-done.2.b_ref = bf16[160,384]{1,0:T(8,128)(2,1)S(1)} collective-permute-done((bf16[160,384]{1,0:T(8,128)(2,1)S(1)}, bf16[160,384]{1,0:T(8,128)(2,1)S(1)}, u32[]{:S(2)}, u32[]{:S(2)}) %collective-permute-start.2) | collective-permute-done | bytes 122912 | tf_op jit(solution)/shard_map/ppermute | solution.py:450
  119.4 1.4 shard_map.138
  120.9 0.0 copy-start.4
  120.9 4.0 %all-to-all-start.5 = ((bf16[16,160,384]{2,1,0:T(8,128)(2,1)}), bf16[16,160,384]{2,1,0:T(8,128)(2,1)S(1)}, u32[]{:S(2)}, u32[]{:S(2)}) async-start(bf16[16,160,384]{2,1,0:T(8,128)(2,1)} %shard_map.138), calls=%async_computation.5 | async-start | bytes 3932160 | tf_op jit(solution)/shard_map/all_to_all | solution.py:391
  124.9 0.0 copy-done.4
  124.9 0.1 shard_map.139
  125.0 1.5 %collective-permute-start.3 = (bf16[32,1280]{1,0:T(8,128)(2,1)S(1)}, bf16[32,1280]{1,0:T(8,128)(2,1)S(1)}, u32[]{:S(2)}, u32[]{:S(2)}) collective-permute-start(bf16[32,1280]{1,0:T(8,128)(2,1)S(1)} %get-tuple-element.36), channel_id=1, source_target_pairs={{0,2},{2,4},{4,6},{6,8},{8,10},{10,12},{12,14},{14,0},{1,3},{3,5},... | collective-permute-start | bytes 245768 | tf_op jit(solution)/shard_map/ppermute | solution.py:462
  126.5 3.6 %collective-permute-start.4 = (bf16[32,1280]{1,0:T(8,128)(2,1)S(1)}, bf16[32,1280]{1,0:T(8,128)(2,1)S(1)}, u32[]{:S(2)}, u32[]{:S(2)}) collective-permute-start(bf16[32,1280]{1,0:T(8,128)(2,1)S(1)} %get-tuple-element.37), channel_id=1, source_target_pairs={{0,4},{2,6},{4,8},{6,10},{8,12},{10,14},{12,0},{14,2},{1,5},{3,7},... | collective-permute-start | bytes 245768 | tf_op jit(solution)/shard_map/ppermute | solution.py:462
  130.1 1.0 collective-permute-start.5
  131.1 3.8 %collective-permute-start.6 = (bf16[32,1280]{1,0:T(8,128)(2,1)S(1)}, bf16[32,1280]{1,0:T(8,128)(2,1)S(1)}, u32[]{:S(2)}, u32[]{:S(2)}) collective-permute-start(bf16[32,1280]{1,0:T(8,128)(2,1)S(1)} %get-tuple-element.39), channel_id=1, source_target_pairs={{0,8},{2,10},{4,12},{6,14},{8,0},{10,2},{12,4},{14,6},{1,9},{3,11}... | collective-permute-start | bytes 245768 | tf_op jit(solution)/shard_map/ppermute | solution.py:462
  134.9 3.5 %collective-permute-start.7 = (bf16[32,1280]{1,0:T(8,128)(2,1)S(1)}, bf16[32,1280]{1,0:T(8,128)(2,1)S(1)}, u32[]{:S(2)}, u32[]{:S(2)}) collective-permute-start(bf16[32,1280]{1,0:T(8,128)(2,1)S(1)} %get-tuple-element.40), channel_id=1, source_target_pairs={{0,10},{2,12},{4,14},{6,0},{8,2},{10,4},{12,6},{14,8},{1,11},{3,13... | collective-permute-start | bytes 245768 | tf_op jit(solution)/shard_map/ppermute | solution.py:462
  138.5 0.0 collective-permute-done.3.refs_1_
  138.5 0.0 collective-permute-start.8
  138.5 0.0 collective-permute-done.4.refs_2_
  138.5 1.9 %collective-permute-start.9 = (bf16[32,1280]{1,0:T(8,128)(2,1)S(1)}, bf16[32,1280]{1,0:T(8,128)(2,1)S(1)}, u32[]{:S(2)}, u32[]{:S(2)}) collective-permute-start(bf16[32,1280]{1,0:T(8,128)(2,1)S(1)} %get-tuple-element.42), channel_id=1, source_target_pairs={{0,14},{2,0},{4,2},{6,4},{8,6},{10,8},{12,10},{14,12},{1,15},{3,1}... | collective-permute-start | bytes 245768 | tf_op jit(solution)/shard_map/ppermute | solution.py:462
  140.3 0.0 collective-permute-done.5.refs_3_
  140.3 0.0 collective-permute-done.6.refs_4_
  140.3 2.1 %collective-permute-done.7.refs_5_ = bf16[32,1280]{1,0:T(8,128)(2,1)S(1)} collective-permute-done((bf16[32,1280]{1,0:T(8,128)(2,1)S(1)}, bf16[32,1280]{1,0:T(8,128)(2,1)S(1)}, u32[]{:S(2)}, u32[]{:S(2)}) %collective-permute-start.7) | collective-permute-done | bytes 81952 | tf_op jit(solution)/shard_map/ppermute | solution.py:462
  142.5 2.2 %collective-permute-done.8.refs_6_ = bf16[32,1280]{1,0:T(8,128)(2,1)S(1)} collective-permute-done((bf16[32,1280]{1,0:T(8,128)(2,1)S(1)}, bf16[32,1280]{1,0:T(8,128)(2,1)S(1)}, u32[]{:S(2)}, u32[]{:S(2)}) %collective-permute-start.8) | collective-permute-done | bytes 81952 | tf_op jit(solution)/shard_map/ppermute | solution.py:462
  144.7 0.1 collective-permute-done.9.refs_7_
  144.7 0.9 shard_map.140
  145.7 0.7 all-to-all-done.5.r_ref
  146.3 1.9 %shard_map.141 = (f32[2560,256]{1,0:T(8,128)}, f32[80,2560]{1,0:T(8,128)}) custom-call(bf16[16,160,384]{2,1,0:T(8,128)(2,1)S(1)} %all-to-all-done.5.r_ref), custom_call_target="tpu_custom_call" | custom-call | tf_op jit(solution)/shard_map/pallas_call | solution.py:376
  (3 shorter events, 0.1 us)
Async XLA Ops:
  0.6 11.6 %copy-start.2 = (bf16[32,2560]{1,0:T(8,128)(2,1)S(1)}, bf16[32,2560]{1,0:T(8,128)(2,1)}, u32[]{:S(2)}) copy-start(bf16[32,2560]{1,0:T(8,128)(2,1)} %hid_ref.1) | copy-start | bytes 491524
  0.6 11.7 %copy-start.5 = (f32[80]{0:T(128)S(1)}, f32[80]{0:T(128)}, u32[]{:S(2)}) copy-start(f32[80]{0:T(128)} %param.15) | copy-start | bytes 964
  0.7 11.7 %copy-start.6 = (f32[80]{0:T(128)S(1)}, f32[80]{0:T(128)}, u32[]{:S(2)}) copy-start(f32[80]{0:T(128)} %param.14) | copy-start | bytes 964
  0.7 11.7 %copy-start.7 = (f32[80]{0:T(128)S(1)}, f32[80]{0:T(128)}, u32[]{:S(2)}) copy-start(f32[80]{0:T(128)} %param.13) | copy-start | bytes 964
  3.6 31.6 %all-to-all-start = ((bf16[8,32,1664]{2,1,0:T(8,128)(2,1)}), bf16[8,32,1664]{2,1,0:T(8,128)(2,1)S(1)}, u32[]{:S(2)}, u32[]{:S(2)}) async-start(bf16[8,32,1664]{2,1,0:T(8,128)(2,1)} %shard_map.127), calls=%async_computation | async-start | bytes 1703936 | tf_op jit(solution)/shard_map/all_to_all | solution.py:391
  37.1 17.2 %all-to-all-start.1 = ((bf16[16,16,1024]{2,1,0:T(8,128)(2,1)}), bf16[16,16,1024]{2,1,0:T(8,128)(2,1)S(1)}, u32[]{:S(2)}, u32[]{:S(2)}) async-start(bf16[16,16,1024]{2,1,0:T(8,128)(2,1)} %shard_map.129), calls=%async_computation.1 | async-start | bytes 1048576 | tf_op jit(solution)/shard_map/all_to_all | solution.py:391
  69.1 0.8 copy-start.3
  69.9 18.3 %copy-start = (bf16[2560,256]{1,0:T(8,128)(2,1)S(1)}, bf16[2560,256]{1,0:T(8,128)(2,1)}, u32[]{:S(2)}) copy-start(bf16[2560,256]{1,0:T(8,128)(2,1)} %wbc_ref.1) | copy-start | bytes 3932164
  69.9 18.3 %copy-start.1 = (bf16[2560,80]{0,1:T(8,128)(2,1)S(1)}, bf16[2560,80]{0,1:T(8,128)(2,1)}, u32[]{:S(2)}) copy-start(bf16[2560,80]{0,1:T(8,128)(2,1)} %param.12) | copy-start | bytes 1228804
  84.7 12.9 %all-to-all-start.4 = ((bf16[16,32,384]{2,1,0:T(8,128)(2,1)}), bf16[16,32,384]{2,1,0:T(8,128)(2,1)S(1)}, u32[]{:S(2)}, u32[]{:S(2)}) async-start(bf16[16,32,384]{2,1,0:T(8,128)(2,1)} %shard_map.133.d_ref), calls=%async_computation.4 | async-start | bytes 786432 | tf_op jit(solution)/shard_map/all_to_all | solution.py:391
  98.4 5.1 %collective-permute-start = (bf16[160,384]{1,0:T(8,128)(2,1)S(1)}, bf16[160,384]{1,0:T(8,128)(2,1)S(1)}, u32[]{:S(2)}, u32[]{:S(2)}) collective-permute-start(bf16[160,384]{1,0:T(8,128)(2,1)S(1)} %get-tuple-element.32.a_ref), channel_id=1, source_target_pairs={{0,2},{2,0},{4,6},{6,4},{8,10},{10,8},{12,14},{14,12},{1,3},{3,1},... | collective-permute-start | bytes 368648 | tf_op jit(solution)/shard_map/ppermute | solution.py:448
  103.6 6.9 %collective-permute-start.1 = (bf16[160,384]{1,0:T(8,128)(2,1)S(1)}, bf16[160,384]{1,0:T(8,128)(2,1)S(1)}, u32[]{:S(2)}, u32[]{:S(2)}) collective-permute-start(bf16[160,384]{1,0:T(8,128)(2,1)S(1)} %shard_map.136.a_ref), channel_id=1, source_target_pairs={{0,4},{2,6},{4,0},{6,2},{8,12},{10,14},{12,8},{14,10},{1,5},{3,7},... | collective-permute-start | bytes 368648 | tf_op jit(solution)/shard_map/ppermute | solution.py:448
  110.6 8.9 %collective-permute-start.2 = (bf16[160,384]{1,0:T(8,128)(2,1)S(1)}, bf16[160,384]{1,0:T(8,128)(2,1)S(1)}, u32[]{:S(2)}, u32[]{:S(2)}) collective-permute-start(bf16[160,384]{1,0:T(8,128)(2,1)S(1)} %shard_map.137.a_ref), channel_id=1, source_target_pairs={{0,8},{2,10},{4,12},{6,14},{8,0},{10,2},{12,4},{14,6},{1,9},{3,11}... | collective-permute-start | bytes 368648 | tf_op jit(solution)/shard_map/ppermute | solution.py:450
  120.9 4.0 %copy-start.4 = (bf16[256,1280]{1,0:T(8,128)(2,1)S(1)}, bf16[256,1280]{1,0:T(8,128)(2,1)}, u32[]{:S(2)}) copy-start(bf16[256,1280]{1,0:T(8,128)(2,1)} %copy-done.3) | copy-start | bytes 1966084
  120.9 25.4 %all-to-all-start.5 = ((bf16[16,160,384]{2,1,0:T(8,128)(2,1)}), bf16[16,160,384]{2,1,0:T(8,128)(2,1)S(1)}, u32[]{:S(2)}, u32[]{:S(2)}) async-start(bf16[16,160,384]{2,1,0:T(8,128)(2,1)} %shard_map.138), calls=%async_computation.5 | async-start | bytes 3932160 | tf_op jit(solution)/shard_map/all_to_all | solution.py:391
  125.0 13.5 %collective-permute-start.3 = (bf16[32,1280]{1,0:T(8,128)(2,1)S(1)}, bf16[32,1280]{1,0:T(8,128)(2,1)S(1)}, u32[]{:S(2)}, u32[]{:S(2)}) collective-permute-start(bf16[32,1280]{1,0:T(8,128)(2,1)S(1)} %get-tuple-element.36), channel_id=1, source_target_pairs={{0,2},{2,4},{4,6},{6,8},{8,10},{10,12},{12,14},{14,0},{1,3},{3,5},... | collective-permute-start | bytes 245768 | tf_op jit(solution)/shard_map/ppermute | solution.py:462
  126.5 12.0 %collective-permute-start.4 = (bf16[32,1280]{1,0:T(8,128)(2,1)S(1)}, bf16[32,1280]{1,0:T(8,128)(2,1)S(1)}, u32[]{:S(2)}, u32[]{:S(2)}) collective-permute-start(bf16[32,1280]{1,0:T(8,128)(2,1)S(1)} %get-tuple-element.37), channel_id=1, source_target_pairs={{0,4},{2,6},{4,8},{6,10},{8,12},{10,14},{12,0},{14,2},{1,5},{3,7},... | collective-permute-start | bytes 245768 | tf_op jit(solution)/shard_map/ppermute | solution.py:462
  130.1 10.2 %collective-permute-start.5 = (bf16[32,1280]{1,0:T(8,128)(2,1)S(1)}, bf16[32,1280]{1,0:T(8,128)(2,1)S(1)}, u32[]{:S(2)}, u32[]{:S(2)}) collective-permute-start(bf16[32,1280]{1,0:T(8,128)(2,1)S(1)} %get-tuple-element.38), channel_id=1, source_target_pairs={{0,6},{2,8},{4,10},{6,12},{8,14},{10,0},{12,2},{14,4},{1,7},{3,9},... | collective-permute-start | bytes 245768 | tf_op jit(solution)/shard_map/ppermute | solution.py:462
  131.1 9.2 %collective-permute-start.6 = (bf16[32,1280]{1,0:T(8,128)(2,1)S(1)}, bf16[32,1280]{1,0:T(8,128)(2,1)S(1)}, u32[]{:S(2)}, u32[]{:S(2)}) collective-permute-start(bf16[32,1280]{1,0:T(8,128)(2,1)S(1)} %get-tuple-element.39), channel_id=1, source_target_pairs={{0,8},{2,10},{4,12},{6,14},{8,0},{10,2},{12,4},{14,6},{1,9},{3,11}... | collective-permute-start | bytes 245768 | tf_op jit(solution)/shard_map/ppermute | solution.py:462
  134.9 7.6 %collective-permute-start.7 = (bf16[32,1280]{1,0:T(8,128)(2,1)S(1)}, bf16[32,1280]{1,0:T(8,128)(2,1)S(1)}, u32[]{:S(2)}, u32[]{:S(2)}) collective-permute-start(bf16[32,1280]{1,0:T(8,128)(2,1)S(1)} %get-tuple-element.40), channel_id=1, source_target_pairs={{0,10},{2,12},{4,14},{6,0},{8,2},{10,4},{12,6},{14,8},{1,11},{3,13... | collective-permute-start | bytes 245768 | tf_op jit(solution)/shard_map/ppermute | solution.py:462
  138.5 6.2 %collective-permute-start.8 = (bf16[32,1280]{1,0:T(8,128)(2,1)S(1)}, bf16[32,1280]{1,0:T(8,128)(2,1)S(1)}, u32[]{:S(2)}, u32[]{:S(2)}) collective-permute-start(bf16[32,1280]{1,0:T(8,128)(2,1)S(1)} %get-tuple-element.41), channel_id=1, source_target_pairs={{0,12},{2,14},{4,0},{6,2},{8,4},{10,6},{12,8},{14,10},{1,13},{3,15... | collective-permute-start | bytes 245768 | tf_op jit(solution)/shard_map/ppermute | solution.py:462
  138.5 6.3 %collective-permute-start.9 = (bf16[32,1280]{1,0:T(8,128)(2,1)S(1)}, bf16[32,1280]{1,0:T(8,128)(2,1)S(1)}, u32[]{:S(2)}, u32[]{:S(2)}) collective-permute-start(bf16[32,1280]{1,0:T(8,128)(2,1)S(1)} %get-tuple-element.42), channel_id=1, source_target_pairs={{0,14},{2,0},{4,2},{6,4},{8,6},{10,8},{12,10},{14,12},{1,15},{3,1}... | collective-permute-start | bytes 245768 | tf_op jit(solution)/shard_map/ppermute | solution.py:462

commit v5 on v4

--- a/solution.py
+++ b/solution.py
@@ -24,6 +24,7 @@
 COLS = D // SEQ
 PACK = 2 * CH + 2 * N + LANES
 DPACK = 2 * N + LANES
+STEPS = (0, 4, 3, 5, 2, 6, 1, 7)
 STAGES = 4
 SLAB = N // SEQ
 STEP = 2 * CH + 2 * N
@@ -276,9 +277,9 @@
 
 
 def rotate_kernel(both_ref, *blocks):
-    for k in range(HEAD):
+    for k, block in zip(STEPS, blocks):
         to = lax.rem(lax.axis_index("head") + k, HEAD)
-        blocks[k][...] = both_ref[pl.ds(pl.multiple_of(to * TOKENS, TOKENS), TOKENS), :]
+        block[...] = both_ref[pl.ds(pl.multiple_of(to * TOKENS, TOKENS), TOKENS), :]
 
 
 def reduce_kernel(r_ref, send_ref):
@@ -308,11 +309,11 @@
 
 def finish_kernel(*refs):
     blocks, outs = refs[:HEAD], refs[HEAD:]
-    for k in range(HEAD):
+    for k, block in zip(STEPS, blocks):
         of = lax.rem(lax.axis_index("head") + HEAD - k, HEAD)
         cols = pl.ds(pl.multiple_of(of * CH, LANES), CH)
         for i, out_ref in enumerate(outs):
-            out_ref[:, cols] = blocks[k][:, i * CH : (i + 1) * CH]
+            out_ref[:, cols] = block[:, i * CH : (i + 1) * CH]
 
 
 def weight_kernel(d_ref, h_ref, send_ref, par_ref):
@@ -447,7 +448,7 @@
     for far in (1, 2):
         other = lax.ppermute(w_part, "head", [(i, i ^ far) for i in range(HEAD)])
         [w_part] = call(add_kernel, [((COLS, DPACK), BF16)], w_part, other)
-    other = lax.ppermute(w_part, "head", [(i, i ^ 4) for i in range(HEAD)])
+    other = lax.ppermute(w_part, "head", [(i, i ^ 7) for i in range(HEAD)])
     [w_sum] = call(
         spread_kernel,
         [((SEQ, COLS, DPACK), BF16)],
@@ -457,9 +458,10 @@
     w_sum, both = lax.optimization_barrier((w_sum, both))
     w_all = exchange(w_sum, "seq")
     blocks = list(call(rotate_kernel, [((TOKENS, 2 * CH), BF16)] * HEAD, both))
-    for k in range(1, HEAD):
-        ring = [(i, (i + k) % HEAD) for i in range(HEAD)]
-        blocks[k] = lax.ppermute(blocks[k], "head", ring)
+    for j, k in enumerate(STEPS):
+        if k > 0:
+            ring = [(i, (i + k) % HEAD) for i in range(HEAD)]
+            blocks[j] = lax.ppermute(blocks[j], "head", ring)
     mixer_out, grad_x = call(
         finish_kernel, [((TOKENS, H * WIDTH), BF16)] * 2, *blocks
     )

time: 150 us -> 149 us (level)
  waiting for transfers between devices: 58.9 us -> 63.5 us
  starting transfers between devices: 43.4 us -> 38.9 us
    ppermute x8, starting transfers between devices: 18.2 us -> 13.9 us  [the longest x7 12.8 us: per_device(): blocks[j] = lax.ppermute(blocks[j], 'head', ring)]
    all_to_all x4, waiting for transfers between devices: 38.5 us -> 42.8 us  [exchange(): return lax.all_to_all(v, axis, split_axis=0, concat_axis=0, tiled=True)]
where the time goes in v5:
time: 149 us; the launch traced here: 148 us
  waiting for transfers between devices  63.5 us (43%)
  starting transfers between devices  38.9 us (26%)
  blocking collectives  25.9 us (17%)
  Pallas kernels  18.4 us (12%)
    all_to_all x4, waiting for transfers between devices, exchange(): return lax.all_to_all(v, axis, split_axis=0, concat_axis=0, tiled=True)  42.8 us
    all_to_all x2, blocking collectives, exchange(): return lax.all_to_all(v, axis, split_axis=0, concat_axis=0, tiled=True)  25.9 us
    all_to_all x4, starting transfers between devices, exchange(): return lax.all_to_all(v, axis, split_axis=0, concat_axis=0, tiled=True)  23 us
    pallas_call x14, Pallas kernels, call(): pl.pallas_call(kernel, out_shape=[jax.ShapeDtypeStruct(shape, kind) for s...  16.5 us
    ppermute x7, starting transfers between devices, per_device(): blocks[j] = lax.ppermute(blocks[j], 'head', ring)  12.8 us
    ppermute x2, waiting for transfers between devices, per_device(): other = lax.ppermute(w_part, 'head', [(i, i ^ far) for i in range(HEAD)])  10.4 us
    ppermute x1, waiting for transfers between devices, per_device(): other = lax.ppermute(w_part, 'head', [(i, i ^ 7) for i in range(HEAD)])  7.07 us
    ppermute x7, waiting for transfers between devices, per_device(): blocks[j] = lax.ppermute(blocks[j], 'head', ring)  3.24 us
  transfers between devices with their start and end apart: 14, of which 10 were waited for; matrix products, arithmetic and copies ran while one was open for 0% of the time, Pallas kernels for 4%

profile of v5, /device:TPU:32, one launch (start us, length us, event | category | flops | bytes accessed | tf_op | source)
XLA Modules:
  0.0 148.5 jit_solution(37541583436722931)
XLA Ops:
  0.6 0.0 copy-start.2
  0.6 0.0 copy-start.5
  0.7 0.0 copy-start.6
  0.7 0.0 copy-start.7
  0.7 2.9 %shard_map.127 = bf16[8,32,1664]{2,1,0:T(8,128)(2,1)} custom-call(bf16[32,2560]{1,0:T(8,128)(2,1)} %hid_ref.1, bf16[2560,256]{1,0:T(8,128)(2,1)} %wbc_ref.1, bf16[80,2560]{1,0:T(8,128)(2,1)} %bitcast.9, bf16[32,5120]{1,0:T(8,128)(2,1)} %x_hbm.1, bf16[32,5120]{1,0:T(8,128)(2,1)} %g_hbm.1), custom_call_target="tpu_custom_call" | custom-call | tf_op jit(solution)/shard_map/pallas_call | solution.py:366
  3.6 8.6 %all-to-all-start = ((bf16[8,32,1664]{2,1,0:T(8,128)(2,1)}), bf16[8,32,1664]{2,1,0:T(8,128)(2,1)S(1)}, u32[]{:S(2)}, u32[]{:S(2)}) async-start(bf16[8,32,1664]{2,1,0:T(8,128)(2,1)} %shard_map.127), calls=%async_computation | async-start | bytes 1703936 | tf_op jit(solution)/shard_map/all_to_all | solution.py:392
  12.2 0.0 copy-done.2
  12.2 0.1 shard_map.128.hs_ref
  12.3 0.0 copy-done.5
  12.3 0.0 copy-done.6
  12.3 0.0 copy-done.7
  12.4 22.9 %all-to-all-done = bf16[8,32,1664]{2,1,0:T(8,128)(2,1)S(1)} async-done(((bf16[8,32,1664]{2,1,0:T(8,128)(2,1)}), bf16[8,32,1664]{2,1,0:T(8,128)(2,1)S(1)}, u32[]{:S(2)}, u32[]{:S(2)}) %all-to-all-start) | async-done | bytes 852000 | tf_op jit(solution)/shard_map/all_to_all | solution.py:392
  35.3 1.9 %shard_map.129 = bf16[16,16,1024]{2,1,0:T(8,128)(2,1)} custom-call(bf16[256,1664]{1,0:T(8,128)(2,1)S(1)} %bitcast.6, f32[8,128]{1,0:T(8,128)S(1)} %select_maximum_fusion.prm_ref, bf16[16,16,384]{2,1,0:T(8,128)(2,1)S(1)} %shard_map.128.hs_ref), custom_call_target="tpu_custom_call" | custom-call | tf_op jit(solution)/shard_map/pallas_call | solution.py:366
  37.1 7.0 %all-to-all-start.1 = ((bf16[16,16,1024]{2,1,0:T(8,128)(2,1)}), bf16[16,16,1024]{2,1,0:T(8,128)(2,1)S(1)}, u32[]{:S(2)}, u32[]{:S(2)}) async-start(bf16[16,16,1024]{2,1,0:T(8,128)(2,1)} %shard_map.129), calls=%async_computation.1 | async-start | bytes 1048576 | tf_op jit(solution)/shard_map/all_to_all | solution.py:392
  44.2 2.3 %shard_map.130.in_ref = f32[256,1792]{1,0:T(8,128)S(1)} custom-call(bf16[256,1664]{1,0:T(8,128)(2,1)S(1)} %bitcast.7, f32[8,128]{1,0:T(8,128)S(1)} %select_maximum_fusion.prm_ref), custom_call_target="tpu_custom_call" | custom-call | tf_op jit(solution)/shard_map/pallas_call | solution.py:366
  46.5 7.8 %all-to-all-done.1.r_ref.h_ref = bf16[16,16,1024]{2,1,0:T(8,128)(2,1)S(1)} async-done(((bf16[16,16,1024]{2,1,0:T(8,128)(2,1)}), bf16[16,16,1024]{2,1,0:T(8,128)(2,1)S(1)}, u32[]{:S(2)}, u32[]{:S(2)}) %all-to-all-start.1) | async-done | bytes 524320 | tf_op jit(solution)/shard_map/all_to_all | solution.py:392
  54.3 0.2 shard_map.131
  54.6 12.0 %all_to_all.30.st_ref = bf16[16,16,640]{2,1,0:T(8,128)(2,1)S(1)} all-to-all(bf16[16,16,640]{2,1,0:T(8,128)(2,1)S(1)} %shard_map.131), channel_id=1, replica_groups=mesh['seq'=16,'head'=8,'dp'=2] {'seq'}, dimensions={0} | all-to-all | bytes 655360 | tf_op jit(solution)/shard_map/all_to_all | solution.py:392
  66.6 2.5 %shard_map.132 = (bf16[8,32,384]{2,1,0:T(8,128)(2,1)S(1)}, bf16[256,1280]{1,0:T(8,128)(2,1)S(1)}) custom-call(bf16[256,1664]{1,0:T(8,128)(2,1)S(1)} %bitcast.8, f32[8,128]{1,0:T(8,128)S(1)} %select_maximum_fusion.prm_ref, bf16[16,16,640]{2,1,0:T(8,128)(2,1)S(1)} %all_to_all.30.st_ref, f32[256,1792]{1,0:T(8,128)S(1)} %shard_map.130.in_ref), custom_call_target="tpu_custom_call" | custom-call | tf_op jit(solution)/shard_map/pallas_call | solution.py:366
  69.1 0.0 copy-start.3
  69.1 0.8 copy-done.3
  69.9 0.0 copy-start
  69.9 0.0 copy-start.1
  69.9 13.9 %all_to_all.31.r_ref = bf16[8,32,384]{2,1,0:T(8,128)(2,1)S(1)} all-to-all(bf16[8,32,384]{2,1,0:T(8,128)(2,1)S(1)} %get-tuple-element.30), channel_id=1, replica_groups=mesh['seq'=16,'head'=8,'dp'=2] {'head'}, dimensions={0} | all-to-all | bytes 393216 | tf_op jit(solution)/shard_map/all_to_all | solution.py:392
  83.8 0.9 shard_map.133.d_ref
  84.7 3.6 %all-to-all-start.4 = ((bf16[16,32,384]{2,1,0:T(8,128)(2,1)}), bf16[16,32,384]{2,1,0:T(8,128)(2,1)S(1)}, u32[]{:S(2)}, u32[]{:S(2)}) async-start(bf16[16,32,384]{2,1,0:T(8,128)(2,1)} %shard_map.133.d_ref), calls=%async_computation.4 | async-start | bytes 786432 | tf_op jit(solution)/shard_map/all_to_all | solution.py:392
  88.2 0.0 copy-done
  88.2 0.0 copy-done.1
  88.2 2.3 %shard_map.134 = bf16[32,2560]{1,0:T(8,128)(2,1)} custom-call(bf16[16,32,384]{2,1,0:T(8,128)(2,1)} %shard_map.133.d_ref, bf16[2560,256]{1,0:T(8,128)(2,1)S(1)} %copy-done, bf16[80,2560]{1,0:T(8,128)(2,1)S(1)} %bitcast.10), custom_call_target="tpu_custom_call" | custom-call | tf_op jit(solution)/shard_map/pallas_call | solution.py:366
  90.5 7.1 %all-to-all-done.4.d_ref = bf16[16,32,384]{2,1,0:T(8,128)(2,1)S(1)} async-done(((bf16[16,32,384]{2,1,0:T(8,128)(2,1)}), bf16[16,32,384]{2,1,0:T(8,128)(2,1)S(1)}, u32[]{:S(2)}, u32[]{:S(2)}) %all-to-all-start.4) | async-done | bytes 393248 | tf_op jit(solution)/shard_map/all_to_all | solution.py:392
  97.6 0.9 shard_map.135
  98.4 1.5 collective-permute-start
  99.9 3.7 %collective-permute-done.b_ref = bf16[160,384]{1,0:T(8,128)(2,1)S(1)} collective-permute-done((bf16[160,384]{1,0:T(8,128)(2,1)S(1)}, bf16[160,384]{1,0:T(8,128)(2,1)S(1)}, u32[]{:S(2)}, u32[]{:S(2)}) %collective-permute-start) | collective-permute-done | bytes 122912 | tf_op jit(solution)/shard_map/ppermute | solution.py:449
  103.6 0.5 collective-permute-start.1
  104.1 6.7 %collective-permute-done.1.b_ref = bf16[160,384]{1,0:T(8,128)(2,1)S(1)} collective-permute-done((bf16[160,384]{1,0:T(8,128)(2,1)S(1)}, bf16[160,384]{1,0:T(8,128)(2,1)S(1)}, u32[]{:S(2)}, u32[]{:S(2)}) %collective-permute-start.1) | collective-permute-done | bytes 122912 | tf_op jit(solution)/shard_map/ppermute | solution.py:449
  110.9 1.1 collective-permute-start.2
  111.9 7.1 %collective-permute-done.2.b_ref = bf16[160,384]{1,0:T(8,128)(2,1)S(1)} collective-permute-done((bf16[160,384]{1,0:T(8,128)(2,1)S(1)}, bf16[160,384]{1,0:T(8,128)(2,1)S(1)}, u32[]{:S(2)}, u32[]{:S(2)}) %collective-permute-start.2) | collective-permute-done | bytes 122912 | tf_op jit(solution)/shard_map/ppermute | solution.py:451
  119.0 1.4 shard_map.138
  120.5 0.0 copy-start.4
  120.5 3.8 %all-to-all-start.5 = ((bf16[16,160,384]{2,1,0:T(8,128)(2,1)}), bf16[16,160,384]{2,1,0:T(8,128)(2,1)S(1)}, u32[]{:S(2)}, u32[]{:S(2)}) async-start(bf16[16,160,384]{2,1,0:T(8,128)(2,1)} %shard_map.138), calls=%async_computation.5 | async-start | bytes 3932160 | tf_op jit(solution)/shard_map/all_to_all | solution.py:392
  124.3 0.0 copy-done.4
  124.3 0.1 shard_map.139
  124.4 0.3 collective-permute-start.3
  124.7 4.9 %collective-permute-start.4 = (bf16[32,1280]{1,0:T(8,128)(2,1)S(1)}, bf16[32,1280]{1,0:T(8,128)(2,1)S(1)}, u32[]{:S(2)}, u32[]{:S(2)}) collective-permute-start(bf16[32,1280]{1,0:T(8,128)(2,1)S(1)} %get-tuple-element.37), channel_id=1, source_target_pairs={{0,6},{2,8},{4,10},{6,12},{8,14},{10,0},{12,2},{14,4},{1,7},{3,9},... | collective-permute-start | bytes 245768 | tf_op jit(solution)/shard_map/ppermute | solution.py:464
  129.6 0.1 collective-permute-start.5
  129.8 1.0 collective-permute-start.6
  130.8 3.1 %collective-permute-start.7 = (bf16[32,1280]{1,0:T(8,128)(2,1)S(1)}, bf16[32,1280]{1,0:T(8,128)(2,1)S(1)}, u32[]{:S(2)}, u32[]{:S(2)}) collective-permute-start(bf16[32,1280]{1,0:T(8,128)(2,1)S(1)} %get-tuple-element.40), channel_id=1, source_target_pairs={{0,12},{2,14},{4,0},{6,2},{8,4},{10,6},{12,8},{14,10},{1,13},{3,15... | collective-permute-start | bytes 245768 | tf_op jit(solution)/shard_map/ppermute | solution.py:464
  133.9 0.0 collective-permute-done.3.refs_1_
  133.9 1.3 collective-permute-start.8
  135.2 0.0 collective-permute-done.4.refs_2_
  135.2 2.0 %collective-permute-start.9 = (bf16[32,1280]{1,0:T(8,128)(2,1)S(1)}, bf16[32,1280]{1,0:T(8,128)(2,1)S(1)}, u32[]{:S(2)}, u32[]{:S(2)}) collective-permute-start(bf16[32,1280]{1,0:T(8,128)(2,1)S(1)} %get-tuple-element.42), channel_id=1, source_target_pairs={{0,14},{2,0},{4,2},{6,4},{8,6},{10,8},{12,10},{14,12},{1,15},{3,1}... | collective-permute-start | bytes 245768 | tf_op jit(solution)/shard_map/ppermute | solution.py:464
  137.2 1.6 %collective-permute-done.5.refs_3_ = bf16[32,1280]{1,0:T(8,128)(2,1)S(1)} collective-permute-done((bf16[32,1280]{1,0:T(8,128)(2,1)S(1)}, bf16[32,1280]{1,0:T(8,128)(2,1)S(1)}, u32[]{:S(2)}, u32[]{:S(2)}) %collective-permute-start.5) | collective-permute-done | bytes 81952 | tf_op jit(solution)/shard_map/ppermute | solution.py:464
  138.8 0.0 collective-permute-done.6.refs_4_
  138.8 0.9 collective-permute-done.7.refs_5_
  139.7 0.0 collective-permute-done.8.refs_6_
  139.7 0.8 collective-permute-done.9.refs_7_
  140.5 0.9 shard_map.140
  141.4 5.0 %all-to-all-done.5.r_ref = bf16[16,160,384]{2,1,0:T(8,128)(2,1)S(1)} async-done(((bf16[16,160,384]{2,1,0:T(8,128)(2,1)}), bf16[16,160,384]{2,1,0:T(8,128)(2,1)S(1)}, u32[]{:S(2)}, u32[]{:S(2)}) %all-to-all-start.5) | async-done | bytes 1966112 | tf_op jit(solution)/shard_map/all_to_all | solution.py:392
  146.4 1.9 %shard_map.141 = (f32[2560,256]{1,0:T(8,128)}, f32[80,2560]{1,0:T(8,128)}) custom-call(bf16[16,160,384]{2,1,0:T(8,128)(2,1)S(1)} %all-to-all-done.5.r_ref), custom_call_target="tpu_custom_call" | custom-call | tf_op jit(solution)/shard_map/pallas_call | solution.py:377
  (3 shorter events, 0.1 us)
Async XLA Ops:
  0.6 11.6 %copy-start.2 = (bf16[32,2560]{1,0:T(8,128)(2,1)S(1)}, bf16[32,2560]{1,0:T(8,128)(2,1)}, u32[]{:S(2)}) copy-start(bf16[32,2560]{1,0:T(8,128)(2,1)} %hid_ref.1) | copy-start | bytes 491524
  0.6 11.7 %copy-start.5 = (f32[80]{0:T(128)S(1)}, f32[80]{0:T(128)}, u32[]{:S(2)}) copy-start(f32[80]{0:T(128)} %param.15) | copy-start | bytes 964
  0.7 11.7 %copy-start.6 = (f32[80]{0:T(128)S(1)}, f32[80]{0:T(128)}, u32[]{:S(2)}) copy-start(f32[80]{0:T(128)} %param.14) | copy-start | bytes 964
  0.7 11.7 %copy-start.7 = (f32[80]{0:T(128)S(1)}, f32[80]{0:T(128)}, u32[]{:S(2)}) copy-start(f32[80]{0:T(128)} %param.13) | copy-start | bytes 964
  3.6 31.6 %all-to-all-start = ((bf16[8,32,1664]{2,1,0:T(8,128)(2,1)}), bf16[8,32,1664]{2,1,0:T(8,128)(2,1)S(1)}, u32[]{:S(2)}, u32[]{:S(2)}) async-start(bf16[8,32,1664]{2,1,0:T(8,128)(2,1)} %shard_map.127), calls=%async_computation | async-start | bytes 1703936 | tf_op jit(solution)/shard_map/all_to_all | solution.py:392
  37.1 17.2 %all-to-all-start.1 = ((bf16[16,16,1024]{2,1,0:T(8,128)(2,1)}), bf16[16,16,1024]{2,1,0:T(8,128)(2,1)S(1)}, u32[]{:S(2)}, u32[]{:S(2)}) async-start(bf16[16,16,1024]{2,1,0:T(8,128)(2,1)} %shard_map.129), calls=%async_computation.1 | async-start | bytes 1048576 | tf_op jit(solution)/shard_map/all_to_all | solution.py:392
  69.1 0.8 copy-start.3
  69.9 18.3 %copy-start = (bf16[2560,256]{1,0:T(8,128)(2,1)S(1)}, bf16[2560,256]{1,0:T(8,128)(2,1)}, u32[]{:S(2)}) copy-start(bf16[2560,256]{1,0:T(8,128)(2,1)} %wbc_ref.1) | copy-start | bytes 3932164
  69.9 18.3 %copy-start.1 = (bf16[2560,80]{0,1:T(8,128)(2,1)S(1)}, bf16[2560,80]{0,1:T(8,128)(2,1)}, u32[]{:S(2)}) copy-start(bf16[2560,80]{0,1:T(8,128)(2,1)} %param.12) | copy-start | bytes 1228804
  84.7 12.9 %all-to-all-start.4 = ((bf16[16,32,384]{2,1,0:T(8,128)(2,1)}), bf16[16,32,384]{2,1,0:T(8,128)(2,1)S(1)}, u32[]{:S(2)}, u32[]{:S(2)}) async-start(bf16[16,32,384]{2,1,0:T(8,128)(2,1)} %shard_map.133.d_ref), calls=%async_computation.4 | async-start | bytes 786432 | tf_op jit(solution)/shard_map/all_to_all | solution.py:392
  98.4 5.1 %collective-permute-start = (bf16[160,384]{1,0:T(8,128)(2,1)S(1)}, bf16[160,384]{1,0:T(8,128)(2,1)S(1)}, u32[]{:S(2)}, u32[]{:S(2)}) collective-permute-start(bf16[160,384]{1,0:T(8,128)(2,1)S(1)} %get-tuple-element.32.a_ref), channel_id=1, source_target_pairs={{0,2},{2,0},{4,6},{6,4},{8,10},{10,8},{12,14},{14,12},{1,3},{3,1},... | collective-permute-start | bytes 368648 | tf_op jit(solution)/shard_map/ppermute | solution.py:449
  103.6 7.2 %collective-permute-start.1 = (bf16[160,384]{1,0:T(8,128)(2,1)S(1)}, bf16[160,384]{1,0:T(8,128)(2,1)S(1)}, u32[]{:S(2)}, u32[]{:S(2)}) collective-permute-start(bf16[160,384]{1,0:T(8,128)(2,1)S(1)} %shard_map.136.a_ref), channel_id=1, source_target_pairs={{0,4},{2,6},{4,0},{6,2},{8,12},{10,14},{12,8},{14,10},{1,5},{3,7},... | collective-permute-start | bytes 368648 | tf_op jit(solution)/shard_map/ppermute | solution.py:449
  110.9 8.1 %collective-permute-start.2 = (bf16[160,384]{1,0:T(8,128)(2,1)S(1)}, bf16[160,384]{1,0:T(8,128)(2,1)S(1)}, u32[]{:S(2)}, u32[]{:S(2)}) collective-permute-start(bf16[160,384]{1,0:T(8,128)(2,1)S(1)} %shard_map.137.a_ref), channel_id=1, source_target_pairs={{0,14},{2,12},{4,10},{6,8},{8,6},{10,4},{12,2},{14,0},{1,15},{3,13... | collective-permute-start | bytes 368648 | tf_op jit(solution)/shard_map/ppermute | solution.py:451
  120.5 3.9 %copy-start.4 = (bf16[256,1280]{1,0:T(8,128)(2,1)S(1)}, bf16[256,1280]{1,0:T(8,128)(2,1)}, u32[]{:S(2)}) copy-start(bf16[256,1280]{1,0:T(8,128)(2,1)} %copy-done.3) | copy-start | bytes 1966084
  120.5 25.9 %all-to-all-start.5 = ((bf16[16,160,384]{2,1,0:T(8,128)(2,1)}), bf16[16,160,384]{2,1,0:T(8,128)(2,1)S(1)}, u32[]{:S(2)}, u32[]{:S(2)}) async-start(bf16[16,160,384]{2,1,0:T(8,128)(2,1)} %shard_map.138), calls=%async_computation.5 | async-start | bytes 3932160 | tf_op jit(solution)/shard_map/all_to_all | solution.py:392
  124.4 9.5 %collective-permute-start.3 = (bf16[32,1280]{1,0:T(8,128)(2,1)S(1)}, bf16[32,1280]{1,0:T(8,128)(2,1)S(1)}, u32[]{:S(2)}, u32[]{:S(2)}) collective-permute-start(bf16[32,1280]{1,0:T(8,128)(2,1)S(1)} %get-tuple-element.36), channel_id=1, source_target_pairs={{0,8},{2,10},{4,12},{6,14},{8,0},{10,2},{12,4},{14,6},{1,9},{3,11}... | collective-permute-start | bytes 245768 | tf_op jit(solution)/shard_map/ppermute | solution.py:464
  124.7 10.5 %collective-permute-start.4 = (bf16[32,1280]{1,0:T(8,128)(2,1)S(1)}, bf16[32,1280]{1,0:T(8,128)(2,1)S(1)}, u32[]{:S(2)}, u32[]{:S(2)}) collective-permute-start(bf16[32,1280]{1,0:T(8,128)(2,1)S(1)} %get-tuple-element.37), channel_id=1, source_target_pairs={{0,6},{2,8},{4,10},{6,12},{8,14},{10,0},{12,2},{14,4},{1,7},{3,9},... | collective-permute-start | bytes 245768 | tf_op jit(solution)/shard_map/ppermute | solution.py:464
  129.6 9.2 %collective-permute-start.5 = (bf16[32,1280]{1,0:T(8,128)(2,1)S(1)}, bf16[32,1280]{1,0:T(8,128)(2,1)S(1)}, u32[]{:S(2)}, u32[]{:S(2)}) collective-permute-start(bf16[32,1280]{1,0:T(8,128)(2,1)S(1)} %get-tuple-element.38), channel_id=1, source_target_pairs={{0,10},{2,12},{4,14},{6,0},{8,2},{10,4},{12,6},{14,8},{1,11},{3,13... | collective-permute-start | bytes 245768 | tf_op jit(solution)/shard_map/ppermute | solution.py:464
  129.8 9.1 %collective-permute-start.6 = (bf16[32,1280]{1,0:T(8,128)(2,1)S(1)}, bf16[32,1280]{1,0:T(8,128)(2,1)S(1)}, u32[]{:S(2)}, u32[]{:S(2)}) collective-permute-start(bf16[32,1280]{1,0:T(8,128)(2,1)S(1)} %get-tuple-element.39), channel_id=1, source_target_pairs={{0,4},{2,6},{4,8},{6,10},{8,12},{10,14},{12,0},{14,2},{1,5},{3,7},... | collective-permute-start | bytes 245768 | tf_op jit(solution)/shard_map/ppermute | solution.py:464
  130.8 8.9 %collective-permute-start.7 = (bf16[32,1280]{1,0:T(8,128)(2,1)S(1)}, bf16[32,1280]{1,0:T(8,128)(2,1)S(1)}, u32[]{:S(2)}, u32[]{:S(2)}) collective-permute-start(bf16[32,1280]{1,0:T(8,128)(2,1)S(1)} %get-tuple-element.40), channel_id=1, source_target_pairs={{0,12},{2,14},{4,0},{6,2},{8,4},{10,6},{12,8},{14,10},{1,13},{3,15... | collective-permute-start | bytes 245768 | tf_op jit(solution)/shard_map/ppermute | solution.py:464
  133.9 5.8 %collective-permute-start.8 = (bf16[32,1280]{1,0:T(8,128)(2,1)S(1)}, bf16[32,1280]{1,0:T(8,128)(2,1)S(1)}, u32[]{:S(2)}, u32[]{:S(2)}) collective-permute-start(bf16[32,1280]{1,0:T(8,128)(2,1)S(1)} %get-tuple-element.41), channel_id=1, source_target_pairs={{0,2},{2,4},{4,6},{6,8},{8,10},{10,12},{12,14},{14,0},{1,3},{3,5},... | collective-permute-start | bytes 245768 | tf_op jit(solution)/shard_map/ppermute | solution.py:464
  135.2 5.2 %collective-permute-start.9 = (bf16[32,1280]{1,0:T(8,128)(2,1)S(1)}, bf16[32,1280]{1,0:T(8,128)(2,1)S(1)}, u32[]{:S(2)}, u32[]{:S(2)}) collective-permute-start(bf16[32,1280]{1,0:T(8,128)(2,1)S(1)} %get-tuple-element.42), channel_id=1, source_target_pairs={{0,14},{2,0},{4,2},{6,4},{8,6},{10,8},{12,10},{14,12},{1,15},{3,1}... | collective-permute-start | bytes 245768 | tf_op jit(solution)/shard_map/ppermute | solution.py:464

commit v6 on v5

--- a/solution.py
+++ b/solution.py
@@ -24,6 +24,8 @@
 COLS = D // SEQ
 PACK = 2 * CH + 2 * N + LANES
 DPACK = 2 * N + LANES
+FOLD = 24
+ROWS = 2 * COLS + COLS // 2 + FOLD + 8
 STEPS = (0, 4, 3, 5, 2, 6, 1, 7)
 STAGES = 4
 SLAB = N // SEQ
@@ -316,6 +318,36 @@
             out_ref[:, cols] = block[:, i * CH : (i + 1) * CH]
 
 
+def fold(grad):
+    half, cut = COLS // 2, LANES // 2
+    steps = grad[:, 2 * N :]
+    lane = iota((half, LANES), 1)
+    wide = jnp.where(lane < cut, steps[:half], pltpu.roll(steps[half:], cut, 1))
+    padded = jnp.concatenate([steps, jnp.zeros((-COLS % FOLD, LANES), F32)], axis=0)
+    rest = jnp.zeros((FOLD, LANES), F32)
+    lane = iota((FOLD, LANES), 1)
+    for j in range(padded.shape[0] // FOLD):
+        piece = padded[j * FOLD : (j + 1) * FOLD]
+        piece = jnp.where(jnp.logical_and(lane >= cut, lane < H), piece, 0.0)
+        rest += pltpu.roll(piece, (cut + (H - cut) * j) % LANES, 1)
+    return jnp.concatenate(
+        [grad[:, :N], grad[:, N : 2 * N], wide, rest, jnp.zeros((8, LANES), F32)], axis=0
+    )
+
+
+def unfold_steps(packed):
+    half, cut = COLS // 2, LANES // 2
+    tail = packed[2 * COLS :].astype(F32)
+    wide, rest = tail[:half], tail[half : half + FOLD]
+    low = jnp.concatenate([wide, pltpu.roll(wide, cut, 1)], axis=0)
+    high = [
+        pltpu.roll(rest, (2 * LANES - cut - (H - cut) * j) % LANES, 1)
+        for j in range(-(-COLS // FOLD))
+    ]
+    high = jnp.concatenate(high, axis=0)[:COLS]
+    return jnp.where(iota((COLS, LANES), 1) < cut, low, high)
+
+
 def weight_kernel(d_ref, h_ref, send_ref, par_ref):
     half = TOKENS // 2
     d = d_ref[...]
@@ -324,7 +356,7 @@
     for i in range(2):
         rows = h[:, :, i * COLS : (i + 1) * COLS].reshape(SEQ * half, COLS).astype(BF16)
         grad += dot(rows, d[:, i * half : (i + 1) * half].reshape(SEQ * half, DPACK), 0, 0)
-    send_ref[...] = (grad / TOTAL).astype(BF16)
+    send_ref[...] = fold(grad / TOTAL).astype(BF16)
     tail = jnp.sum(d[:, :, 2 * N :].astype(F32), axis=0)
     low = iota((8, LANES), 1)
     out = jnp.zeros((8, LANES), F32)
@@ -350,12 +382,16 @@
     parts = SEQ // STAGES
     copies = []
     for i in range(STAGES):
-        part = r_ref[i * parts : (i + 1) * parts]
+        part = range(i * parts, (i + 1) * parts)
         at = slice(i * parts * COLS, (i + 1) * parts * COLS)
-        bc_ref[at] = part[:, :, : 2 * N].astype(F32).reshape(parts * COLS, 2 * N)
+        for s in part:
+            rows = slice(s * COLS, (s + 1) * COLS)
+            bc_ref[rows, :N] = r_ref[s, :COLS].astype(F32)
+            bc_ref[rows, N:] = r_ref[s, COLS : 2 * COLS].astype(F32)
         copies.append(pltpu.make_async_copy(bc_ref.at[at], bc_hbm.at[at], sems.at[i, 0]))
         copies[-1].start()
-        dt_ref[:, at] = part[:, :, 2 * N :].astype(F32).reshape(parts * COLS, LANES).T[:H]
+        steps = jnp.concatenate([unfold_steps(r_ref[s]) for s in part], axis=0)
+        dt_ref[:, at] = steps.T[:H]
         copies.append(pltpu.make_async_copy(dt_ref.at[:, at], dt_hbm.at[:, at], sems.at[i, 1]))
         copies[-1].start()
     for copy in copies:
@@ -443,15 +479,15 @@
     )
     d_all, grad_hidden = lax.optimization_barrier((d_all, grad_hidden))
     w_part, param_grads = call(
-        weight_kernel, [((COLS, DPACK), BF16), ((3, H), F32)], d_all, totals
+        weight_kernel, [((ROWS, LANES), BF16), ((3, H), F32)], d_all, totals
     )
     for far in (1, 2):
         other = lax.ppermute(w_part, "head", [(i, i ^ far) for i in range(HEAD)])
-        [w_part] = call(add_kernel, [((COLS, DPACK), BF16)], w_part, other)
+        [w_part] = call(add_kernel, [((ROWS, LANES), BF16)], w_part, other)
     other = lax.ppermute(w_part, "head", [(i, i ^ 7) for i in range(HEAD)])
     [w_sum] = call(
         spread_kernel,
-        [((SEQ, COLS, DPACK), BF16)],
+        [((SEQ, ROWS, LANES), BF16)],
         w_part, other,
         limit=NEAR,
     )

time: 149 us -> 146 us (0.980)
  waiting for transfers between devices: 63.5 us -> 58.4 us
  starting transfers between devices: 38.9 us -> 41 us
    all_to_all x4, waiting for transfers between devices: 42.8 us -> 41 us  [exchange(): return lax.all_to_all(v, axis, split_axis=0, concat_axis=0, tiled=True)]
    ppermute x2, waiting for transfers between devices: 10.4 us -> 8.62 us  [per_device(): other = lax.ppermute(w_part, 'head', [(i, i ^ far) for i in range(HEAD)])]
    ppermute x1, waiting for transfers between devices: 7.07 us -> 5.55 us  [per_device(): other = lax.ppermute(w_part, 'head', [(i, i ^ 7) for i in range(HEAD)])]
where the time goes in v6:
time: 146 us
  waiting for transfers between devices  58.4 us (40%)
  starting transfers between devices  41 us (28%)
  blocking collectives  25.9 us (18%)
  Pallas kernels  18.6 us (13%)
    all_to_all x4, waiting for transfers between devices, exchange(): return lax.all_to_all(v, axis, split_axis=0, concat_axis=0, tiled=True)  41 us
    all_to_all x2, blocking collectives, exchange(): return lax.all_to_all(v, axis, split_axis=0, concat_axis=0, tiled=True)  25.9 us
    all_to_all x4, starting transfers between devices, exchange(): return lax.all_to_all(v, axis, split_axis=0, concat_axis=0, tiled=True)  23.7 us
    pallas_call x14, Pallas kernels, call(): pl.pallas_call(kernel, out_shape=[jax.ShapeDtypeStruct(shape, kind) for s...  16.4 us
    ppermute x7, starting transfers between devices, per_device(): blocks[j] = lax.ppermute(blocks[j], 'head', ring)  12.8 us
    ppermute x2, waiting for transfers between devices, per_device(): other = lax.ppermute(w_part, 'head', [(i, i ^ far) for i in range(HEAD)])  8.62 us
    ppermute x1, waiting for transfers between devices, per_device(): other = lax.ppermute(w_part, 'head', [(i, i ^ 7) for i in range(HEAD)])  5.55 us
    ppermute x7, waiting for transfers between devices, per_device(): blocks[j] = lax.ppermute(blocks[j], 'head', ring)  3.33 us
  transfers between devices with their start and end apart: 14, of which 10 were waited for; matrix products, arithmetic and copies ran while one was open for 0% of the time, Pallas kernels for 4%

profile of v6, /device:TPU:32, one launch (start us, length us, event | category | flops | bytes accessed | tf_op | source)
XLA Modules:
  0.0 145.7 jit_solution(5664547763887130197)
XLA Ops:
  0.6 0.0 copy-start.2
  0.6 3.0 %shard_map.127 = bf16[8,32,1664]{2,1,0:T(8,128)(2,1)} custom-call(bf16[32,2560]{1,0:T(8,128)(2,1)} %hid_ref.1, bf16[2560,256]{1,0:T(8,128)(2,1)} %wbc_ref.1, bf16[80,2560]{1,0:T(8,128)(2,1)} %bitcast.9, bf16[32,5120]{1,0:T(8,128)(2,1)} %x_hbm.1, bf16[32,5120]{1,0:T(8,128)(2,1)} %g_hbm.1), custom_call_target="tpu_custom_call" | custom-call | tf_op jit(solution)/shard_map/pallas_call | solution.py:402
  3.6 0.0 copy-start.5
  3.6 0.0 copy-start.6
  3.6 0.0 copy-start.7
  3.7 8.7 %all-to-all-start = ((bf16[8,32,1664]{2,1,0:T(8,128)(2,1)}), bf16[8,32,1664]{2,1,0:T(8,128)(2,1)S(1)}, u32[]{:S(2)}, u32[]{:S(2)}) async-start(bf16[8,32,1664]{2,1,0:T(8,128)(2,1)} %shard_map.127), calls=%async_computation | async-start | bytes 1703936 | tf_op jit(solution)/shard_map/all_to_all | solution.py:428
  12.4 0.0 copy-done.2
  12.4 0.1 shard_map.128.hs_ref
  12.5 0.0 copy-done.5
  12.5 0.0 copy-done.6
  12.5 0.0 copy-done.7
  12.5 22.9 %all-to-all-done = bf16[8,32,1664]{2,1,0:T(8,128)(2,1)S(1)} async-done(((bf16[8,32,1664]{2,1,0:T(8,128)(2,1)}), bf16[8,32,1664]{2,1,0:T(8,128)(2,1)S(1)}, u32[]{:S(2)}, u32[]{:S(2)}) %all-to-all-start) | async-done | bytes 852000 | tf_op jit(solution)/shard_map/all_to_all | solution.py:428
  35.4 1.9 %shard_map.129 = bf16[16,16,1024]{2,1,0:T(8,128)(2,1)} custom-call(bf16[256,1664]{1,0:T(8,128)(2,1)S(1)} %bitcast.6, f32[8,128]{1,0:T(8,128)S(1)} %select_maximum_fusion.prm_ref, bf16[16,16,384]{2,1,0:T(8,128)(2,1)S(1)} %shard_map.128.hs_ref), custom_call_target="tpu_custom_call" | custom-call | tf_op jit(solution)/shard_map/pallas_call | solution.py:402
  37.3 7.0 %all-to-all-start.1 = ((bf16[16,16,1024]{2,1,0:T(8,128)(2,1)}), bf16[16,16,1024]{2,1,0:T(8,128)(2,1)S(1)}, u32[]{:S(2)}, u32[]{:S(2)}) async-start(bf16[16,16,1024]{2,1,0:T(8,128)(2,1)} %shard_map.129), calls=%async_computation.1 | async-start | bytes 1048576 | tf_op jit(solution)/shard_map/all_to_all | solution.py:428
  44.4 2.3 %shard_map.130.in_ref = f32[256,1792]{1,0:T(8,128)S(1)} custom-call(bf16[256,1664]{1,0:T(8,128)(2,1)S(1)} %bitcast.7, f32[8,128]{1,0:T(8,128)S(1)} %select_maximum_fusion.prm_ref), custom_call_target="tpu_custom_call" | custom-call | tf_op jit(solution)/shard_map/pallas_call | solution.py:402
  46.7 7.8 %all-to-all-done.1.r_ref.h_ref = bf16[16,16,1024]{2,1,0:T(8,128)(2,1)S(1)} async-done(((bf16[16,16,1024]{2,1,0:T(8,128)(2,1)}), bf16[16,16,1024]{2,1,0:T(8,128)(2,1)S(1)}, u32[]{:S(2)}, u32[]{:S(2)}) %all-to-all-start.1) | async-done | bytes 524320 | tf_op jit(solution)/shard_map/all_to_all | solution.py:428
  54.5 0.2 shard_map.131
  54.7 12.0 %all_to_all.30.st_ref = bf16[16,16,640]{2,1,0:T(8,128)(2,1)S(1)} all-to-all(bf16[16,16,640]{2,1,0:T(8,128)(2,1)S(1)} %shard_map.131), channel_id=1, replica_groups=mesh['seq'=16,'head'=8,'dp'=2] {'seq'}, dimensions={0} | all-to-all | bytes 655360 | tf_op jit(solution)/shard_map/all_to_all | solution.py:428
  66.7 2.5 %shard_map.132 = (bf16[8,32,384]{2,1,0:T(8,128)(2,1)S(1)}, bf16[256,1280]{1,0:T(8,128)(2,1)S(1)}) custom-call(bf16[256,1664]{1,0:T(8,128)(2,1)S(1)} %bitcast.8, f32[8,128]{1,0:T(8,128)S(1)} %select_maximum_fusion.prm_ref, bf16[16,16,640]{2,1,0:T(8,128)(2,1)S(1)} %all_to_all.30.st_ref, f32[256,1792]{1,0:T(8,128)S(1)} %shard_map.130.in_ref), custom_call_target="tpu_custom_call" | custom-call | tf_op jit(solution)/shard_map/pallas_call | solution.py:402
  69.3 0.0 copy-start.3
  69.3 0.8 copy-done.3
  70.1 0.0 copy-start
  70.1 0.0 copy-start.1
  70.1 13.9 %all_to_all.31.r_ref = bf16[8,32,384]{2,1,0:T(8,128)(2,1)S(1)} all-to-all(bf16[8,32,384]{2,1,0:T(8,128)(2,1)S(1)} %get-tuple-element.30), channel_id=1, replica_groups=mesh['seq'=16,'head'=8,'dp'=2] {'head'}, dimensions={0} | all-to-all | bytes 393216 | tf_op jit(solution)/shard_map/all_to_all | solution.py:428
  84.0 0.9 shard_map.133.d_ref
  84.8 3.6 %all-to-all-start.4 = ((bf16[16,32,384]{2,1,0:T(8,128)(2,1)}), bf16[16,32,384]{2,1,0:T(8,128)(2,1)S(1)}, u32[]{:S(2)}, u32[]{:S(2)}) async-start(bf16[16,32,384]{2,1,0:T(8,128)(2,1)} %shard_map.133.d_ref), calls=%async_computation.4 | async-start | bytes 786432 | tf_op jit(solution)/shard_map/all_to_all | solution.py:428
  88.4 0.0 copy-done
  88.4 0.0 copy-done.1
  88.4 2.3 %shard_map.134 = bf16[32,2560]{1,0:T(8,128)(2,1)} custom-call(bf16[16,32,384]{2,1,0:T(8,128)(2,1)} %shard_map.133.d_ref, bf16[2560,256]{1,0:T(8,128)(2,1)S(1)} %copy-done, bf16[80,2560]{1,0:T(8,128)(2,1)S(1)} %bitcast.10), custom_call_target="tpu_custom_call" | custom-call | tf_op jit(solution)/shard_map/pallas_call | solution.py:402
  90.7 7.1 %all-to-all-done.4.d_ref = bf16[16,32,384]{2,1,0:T(8,128)(2,1)S(1)} async-done(((bf16[16,32,384]{2,1,0:T(8,128)(2,1)}), bf16[16,32,384]{2,1,0:T(8,128)(2,1)S(1)}, u32[]{:S(2)}, u32[]{:S(2)}) %all-to-all-start.4) | async-done | bytes 393248 | tf_op jit(solution)/shard_map/all_to_all | solution.py:428
  97.8 0.9 shard_map.135
  98.7 1.5 %collective-permute-start = (bf16[432,128]{1,0:T(8,128)(2,1)S(1)}, bf16[432,128]{1,0:T(8,128)(2,1)S(1)}, u32[]{:S(2)}, u32[]{:S(2)}) collective-permute-start(bf16[432,128]{1,0:T(8,128)(2,1)S(1)} %get-tuple-element.32.a_ref), channel_id=1, source_target_pairs={{0,2},{2,0},{4,6},{6,4},{8,10},{10,8},{12,14},{14,12},{1,3},{3,1},... | collective-permute-start | bytes 331784 | tf_op jit(solution)/shard_map/ppermute | solution.py:485
  100.1 3.4 %collective-permute-done.b_ref = bf16[432,128]{1,0:T(8,128)(2,1)S(1)} collective-permute-done((bf16[432,128]{1,0:T(8,128)(2,1)S(1)}, bf16[432,128]{1,0:T(8,128)(2,1)S(1)}, u32[]{:S(2)}, u32[]{:S(2)}) %collective-permute-start) | collective-permute-done | bytes 110624 | tf_op jit(solution)/shard_map/ppermute | solution.py:485
  103.5 0.6 collective-permute-start.1
  104.1 5.2 %collective-permute-done.1.b_ref = bf16[432,128]{1,0:T(8,128)(2,1)S(1)} collective-permute-done((bf16[432,128]{1,0:T(8,128)(2,1)S(1)}, bf16[432,128]{1,0:T(8,128)(2,1)S(1)}, u32[]{:S(2)}, u32[]{:S(2)}) %collective-permute-start.1) | collective-permute-done | bytes 110624 | tf_op jit(solution)/shard_map/ppermute | solution.py:485
  109.4 2.4 %collective-permute-start.2 = (bf16[432,128]{1,0:T(8,128)(2,1)S(1)}, bf16[432,128]{1,0:T(8,128)(2,1)S(1)}, u32[]{:S(2)}, u32[]{:S(2)}) collective-permute-start(bf16[432,128]{1,0:T(8,128)(2,1)S(1)} %shard_map.137.a_ref), channel_id=1, source_target_pairs={{0,14},{2,12},{4,10},{6,8},{8,6},{10,4},{12,2},{14,0},{1,15},{3,13... | collective-permute-start | bytes 331784 | tf_op jit(solution)/shard_map/ppermute | solution.py:487
  111.8 5.5 %collective-permute-done.2.b_ref = bf16[432,128]{1,0:T(8,128)(2,1)S(1)} collective-permute-done((bf16[432,128]{1,0:T(8,128)(2,1)S(1)}, bf16[432,128]{1,0:T(8,128)(2,1)S(1)}, u32[]{:S(2)}, u32[]{:S(2)}) %collective-permute-start.2) | collective-permute-done | bytes 110624 | tf_op jit(solution)/shard_map/ppermute | solution.py:487
  117.3 1.3 shard_map.138
  118.6 0.0 copy-start.4
  118.6 4.4 %all-to-all-start.5 = ((bf16[16,432,128]{2,1,0:T(8,128)(2,1)}), bf16[16,432,128]{2,1,0:T(8,128)(2,1)S(1)}, u32[]{:S(2)}, u32[]{:S(2)}) async-start(bf16[16,432,128]{2,1,0:T(8,128)(2,1)} %shard_map.138), calls=%async_computation.5 | async-start | bytes 3538944 | tf_op jit(solution)/shard_map/all_to_all | solution.py:428
  123.1 0.0 copy-done.4
  123.1 0.1 shard_map.139
  123.2 1.2 collective-permute-start.3
  124.4 4.4 %collective-permute-start.4 = (bf16[32,1280]{1,0:T(8,128)(2,1)S(1)}, bf16[32,1280]{1,0:T(8,128)(2,1)S(1)}, u32[]{:S(2)}, u32[]{:S(2)}) collective-permute-start(bf16[32,1280]{1,0:T(8,128)(2,1)S(1)} %get-tuple-element.37), channel_id=1, source_target_pairs={{0,6},{2,8},{4,10},{6,12},{8,14},{10,0},{12,2},{14,4},{1,7},{3,9},... | collective-permute-start | bytes 245768 | tf_op jit(solution)/shard_map/ppermute | solution.py:500
  128.8 0.6 collective-permute-start.5
  129.4 0.6 collective-permute-start.6
  130.0 3.6 %collective-permute-start.7 = (bf16[32,1280]{1,0:T(8,128)(2,1)S(1)}, bf16[32,1280]{1,0:T(8,128)(2,1)S(1)}, u32[]{:S(2)}, u32[]{:S(2)}) collective-permute-start(bf16[32,1280]{1,0:T(8,128)(2,1)S(1)} %get-tuple-element.40), channel_id=1, source_target_pairs={{0,12},{2,14},{4,0},{6,2},{8,4},{10,6},{12,8},{14,10},{1,13},{3,15... | collective-permute-start | bytes 245768 | tf_op jit(solution)/shard_map/ppermute | solution.py:500
  133.5 0.0 collective-permute-done.3.refs_1_
  133.5 0.9 collective-permute-start.8
  134.4 0.0 collective-permute-done.4.refs_2_
  134.4 1.6 %collective-permute-start.9 = (bf16[32,1280]{1,0:T(8,128)(2,1)S(1)}, bf16[32,1280]{1,0:T(8,128)(2,1)S(1)}, u32[]{:S(2)}, u32[]{:S(2)}) collective-permute-start(bf16[32,1280]{1,0:T(8,128)(2,1)S(1)} %get-tuple-element.42), channel_id=1, source_target_pairs={{0,14},{2,0},{4,2},{6,4},{8,6},{10,8},{12,10},{14,12},{1,15},{3,1}... | collective-permute-start | bytes 245768 | tf_op jit(solution)/shard_map/ppermute | solution.py:500
  136.0 2.0 %collective-permute-done.5.refs_3_ = bf16[32,1280]{1,0:T(8,128)(2,1)S(1)} collective-permute-done((bf16[32,1280]{1,0:T(8,128)(2,1)S(1)}, bf16[32,1280]{1,0:T(8,128)(2,1)S(1)}, u32[]{:S(2)}, u32[]{:S(2)}) %collective-permute-start.5) | collective-permute-done | bytes 81952 | tf_op jit(solution)/shard_map/ppermute | solution.py:500
  138.0 0.0 collective-permute-done.6.refs_4_
  138.0 0.5 collective-permute-done.7.refs_5_
  138.5 0.0 collective-permute-done.8.refs_6_
  138.5 0.8 collective-permute-done.9.refs_7_
  139.3 0.9 shard_map.140
  140.2 3.2 %all-to-all-done.5.r_ref = bf16[16,432,128]{2,1,0:T(8,128)(2,1)S(1)} async-done(((bf16[16,432,128]{2,1,0:T(8,128)(2,1)}), bf16[16,432,128]{2,1,0:T(8,128)(2,1)S(1)}, u32[]{:S(2)}, u32[]{:S(2)}) %all-to-all-start.5) | async-done | bytes 1769504 | tf_op jit(solution)/shard_map/all_to_all | solution.py:428
  143.4 2.2 %shard_map.141 = (f32[2560,256]{1,0:T(8,128)}, f32[80,2560]{1,0:T(8,128)}) custom-call(bf16[16,432,128]{2,1,0:T(8,128)(2,1)S(1)} %all-to-all-done.5.r_ref), custom_call_target="tpu_custom_call" | custom-call | tf_op jit(solution)/shard_map/pallas_call | solution.py:413
  (3 shorter events, 0.1 us)
Async XLA Ops:
  0.6 11.7 %copy-start.2 = (bf16[32,2560]{1,0:T(8,128)(2,1)S(1)}, bf16[32,2560]{1,0:T(8,128)(2,1)}, u32[]{:S(2)}) copy-start(bf16[32,2560]{1,0:T(8,128)(2,1)} %hid_ref.1) | copy-start | bytes 491524
  3.6 8.9 %copy-start.5 = (f32[80]{0:T(128)S(1)}, f32[80]{0:T(128)}, u32[]{:S(2)}) copy-start(f32[80]{0:T(128)} %param.15) | copy-start | bytes 964
  3.6 8.9 %copy-start.6 = (f32[80]{0:T(128)S(1)}, f32[80]{0:T(128)}, u32[]{:S(2)}) copy-start(f32[80]{0:T(128)} %param.14) | copy-start | bytes 964
  3.6 8.9 %copy-start.7 = (f32[80]{0:T(128)S(1)}, f32[80]{0:T(128)}, u32[]{:S(2)}) copy-start(f32[80]{0:T(128)} %param.13) | copy-start | bytes 964
  3.7 31.8 %all-to-all-start = ((bf16[8,32,1664]{2,1,0:T(8,128)(2,1)}), bf16[8,32,1664]{2,1,0:T(8,128)(2,1)S(1)}, u32[]{:S(2)}, u32[]{:S(2)}) async-start(bf16[8,32,1664]{2,1,0:T(8,128)(2,1)} %shard_map.127), calls=%async_computation | async-start | bytes 1703936 | tf_op jit(solution)/shard_map/all_to_all | solution.py:428
  37.3 17.2 %all-to-all-start.1 = ((bf16[16,16,1024]{2,1,0:T(8,128)(2,1)}), bf16[16,16,1024]{2,1,0:T(8,128)(2,1)S(1)}, u32[]{:S(2)}, u32[]{:S(2)}) async-start(bf16[16,16,1024]{2,1,0:T(8,128)(2,1)} %shard_map.129), calls=%async_computation.1 | async-start | bytes 1048576 | tf_op jit(solution)/shard_map/all_to_all | solution.py:428
  69.3 0.8 copy-start.3
  70.1 18.3 %copy-start = (bf16[2560,256]{1,0:T(8,128)(2,1)S(1)}, bf16[2560,256]{1,0:T(8,128)(2,1)}, u32[]{:S(2)}) copy-start(bf16[2560,256]{1,0:T(8,128)(2,1)} %wbc_ref.1) | copy-start | bytes 3932164
  70.1 18.3 %copy-start.1 = (bf16[2560,80]{0,1:T(8,128)(2,1)S(1)}, bf16[2560,80]{0,1:T(8,128)(2,1)}, u32[]{:S(2)}) copy-start(bf16[2560,80]{0,1:T(8,128)(2,1)} %param.12) | copy-start | bytes 1228804
  84.8 12.9 %all-to-all-start.4 = ((bf16[16,32,384]{2,1,0:T(8,128)(2,1)}), bf16[16,32,384]{2,1,0:T(8,128)(2,1)S(1)}, u32[]{:S(2)}, u32[]{:S(2)}) async-start(bf16[16,32,384]{2,1,0:T(8,128)(2,1)} %shard_map.133.d_ref), calls=%async_computation.4 | async-start | bytes 786432 | tf_op jit(solution)/shard_map/all_to_all | solution.py:428
  98.7 4.8 %collective-permute-start = (bf16[432,128]{1,0:T(8,128)(2,1)S(1)}, bf16[432,128]{1,0:T(8,128)(2,1)S(1)}, u32[]{:S(2)}, u32[]{:S(2)}) collective-permute-start(bf16[432,128]{1,0:T(8,128)(2,1)S(1)} %get-tuple-element.32.a_ref), channel_id=1, source_target_pairs={{0,2},{2,0},{4,6},{6,4},{8,10},{10,8},{12,14},{14,12},{1,3},{3,1},... | collective-permute-start | bytes 331784 | tf_op jit(solution)/shard_map/ppermute | solution.py:485
  103.5 5.8 %collective-permute-start.1 = (bf16[432,128]{1,0:T(8,128)(2,1)S(1)}, bf16[432,128]{1,0:T(8,128)(2,1)S(1)}, u32[]{:S(2)}, u32[]{:S(2)}) collective-permute-start(bf16[432,128]{1,0:T(8,128)(2,1)S(1)} %shard_map.136.a_ref), channel_id=1, source_target_pairs={{0,4},{2,6},{4,0},{6,2},{8,12},{10,14},{12,8},{14,10},{1,5},{3,7},... | collective-permute-start | bytes 331784 | tf_op jit(solution)/shard_map/ppermute | solution.py:485
  109.4 7.9 %collective-permute-start.2 = (bf16[432,128]{1,0:T(8,128)(2,1)S(1)}, bf16[432,128]{1,0:T(8,128)(2,1)S(1)}, u32[]{:S(2)}, u32[]{:S(2)}) collective-permute-start(bf16[432,128]{1,0:T(8,128)(2,1)S(1)} %shard_map.137.a_ref), channel_id=1, source_target_pairs={{0,14},{2,12},{4,10},{6,8},{8,6},{10,4},{12,2},{14,0},{1,15},{3,13... | collective-permute-start | bytes 331784 | tf_op jit(solution)/shard_map/ppermute | solution.py:487
  118.6 4.5 %copy-start.4 = (bf16[256,1280]{1,0:T(8,128)(2,1)S(1)}, bf16[256,1280]{1,0:T(8,128)(2,1)}, u32[]{:S(2)}) copy-start(bf16[256,1280]{1,0:T(8,128)(2,1)} %copy-done.3) | copy-start | bytes 1966084
  118.6 24.7 %all-to-all-start.5 = ((bf16[16,432,128]{2,1,0:T(8,128)(2,1)}), bf16[16,432,128]{2,1,0:T(8,128)(2,1)S(1)}, u32[]{:S(2)}, u32[]{:S(2)}) async-start(bf16[16,432,128]{2,1,0:T(8,128)(2,1)} %shard_map.138), calls=%async_computation.5 | async-start | bytes 3538944 | tf_op jit(solution)/shard_map/all_to_all | solution.py:428
  123.2 10.4 %collective-permute-start.3 = (bf16[32,1280]{1,0:T(8,128)(2,1)S(1)}, bf16[32,1280]{1,0:T(8,128)(2,1)S(1)}, u32[]{:S(2)}, u32[]{:S(2)}) collective-permute-start(bf16[32,1280]{1,0:T(8,128)(2,1)S(1)} %get-tuple-element.36), channel_id=1, source_target_pairs={{0,8},{2,10},{4,12},{6,14},{8,0},{10,2},{12,4},{14,6},{1,9},{3,11}... | collective-permute-start | bytes 245768 | tf_op jit(solution)/shard_map/ppermute | solution.py:500
  124.4 10.0 %collective-permute-start.4 = (bf16[32,1280]{1,0:T(8,128)(2,1)S(1)}, bf16[32,1280]{1,0:T(8,128)(2,1)S(1)}, u32[]{:S(2)}, u32[]{:S(2)}) collective-permute-start(bf16[32,1280]{1,0:T(8,128)(2,1)S(1)} %get-tuple-element.37), channel_id=1, source_target_pairs={{0,6},{2,8},{4,10},{6,12},{8,14},{10,0},{12,2},{14,4},{1,7},{3,9},... | collective-permute-start | bytes 245768 | tf_op jit(solution)/shard_map/ppermute | solution.py:500
  128.8 9.2 %collective-permute-start.5 = (bf16[32,1280]{1,0:T(8,128)(2,1)S(1)}, bf16[32,1280]{1,0:T(8,128)(2,1)S(1)}, u32[]{:S(2)}, u32[]{:S(2)}) collective-permute-start(bf16[32,1280]{1,0:T(8,128)(2,1)S(1)} %get-tuple-element.38), channel_id=1, source_target_pairs={{0,10},{2,12},{4,14},{6,0},{8,2},{10,4},{12,6},{14,8},{1,11},{3,13... | collective-permute-start | bytes 245768 | tf_op jit(solution)/shard_map/ppermute | solution.py:500
  129.4 8.6 %collective-permute-start.6 = (bf16[32,1280]{1,0:T(8,128)(2,1)S(1)}, bf16[32,1280]{1,0:T(8,128)(2,1)S(1)}, u32[]{:S(2)}, u32[]{:S(2)}) collective-permute-start(bf16[32,1280]{1,0:T(8,128)(2,1)S(1)} %get-tuple-element.39), channel_id=1, source_target_pairs={{0,4},{2,6},{4,8},{6,10},{8,12},{10,14},{12,0},{14,2},{1,5},{3,7},... | collective-permute-start | bytes 245768 | tf_op jit(solution)/shard_map/ppermute | solution.py:500
  130.0 8.5 %collective-permute-start.7 = (bf16[32,1280]{1,0:T(8,128)(2,1)S(1)}, bf16[32,1280]{1,0:T(8,128)(2,1)S(1)}, u32[]{:S(2)}, u32[]{:S(2)}) collective-permute-start(bf16[32,1280]{1,0:T(8,128)(2,1)S(1)} %get-tuple-element.40), channel_id=1, source_target_pairs={{0,12},{2,14},{4,0},{6,2},{8,4},{10,6},{12,8},{14,10},{1,13},{3,15... | collective-permute-start | bytes 245768 | tf_op jit(solution)/shard_map/ppermute | solution.py:500
  133.5 5.0 %collective-permute-start.8 = (bf16[32,1280]{1,0:T(8,128)(2,1)S(1)}, bf16[32,1280]{1,0:T(8,128)(2,1)S(1)}, u32[]{:S(2)}, u32[]{:S(2)}) collective-permute-start(bf16[32,1280]{1,0:T(8,128)(2,1)S(1)} %get-tuple-element.41), channel_id=1, source_target_pairs={{0,2},{2,4},{4,6},{6,8},{8,10},{10,12},{12,14},{14,0},{1,3},{3,5},... | collective-permute-start | bytes 245768 | tf_op jit(solution)/shard_map/ppermute | solution.py:500
  134.4 4.9 %collective-permute-start.9 = (bf16[32,1280]{1,0:T(8,128)(2,1)S(1)}, bf16[32,1280]{1,0:T(8,128)(2,1)S(1)}, u32[]{:S(2)}, u32[]{:S(2)}) collective-permute-start(bf16[32,1280]{1,0:T(8,128)(2,1)S(1)} %get-tuple-element.42), channel_id=1, source_target_pairs={{0,14},{2,0},{4,2},{6,4},{8,6},{10,8},{12,10},{14,12},{1,15},{3,1}... | collective-permute-start | bytes 245768 | tf_op jit(solution)/shard_map/ppermute | solution.py:500

commit v7 on v6

--- a/solution.py
+++ b/solution.py
@@ -381,15 +381,16 @@
 def unpack_kernel(r_ref, bc_hbm, dt_hbm, bc_ref, dt_ref, sems):
     parts = SEQ // STAGES
     copies = []
-    for i in range(STAGES):
-        part = range(i * parts, (i + 1) * parts)
-        at = slice(i * parts * COLS, (i + 1) * parts * COLS)
-        for s in part:
+    spans = [slice(i * parts * COLS, (i + 1) * parts * COLS) for i in range(STAGES)]
+    for i, at in enumerate(spans):
+        for s in range(i * parts, (i + 1) * parts):
             rows = slice(s * COLS, (s + 1) * COLS)
             bc_ref[rows, :N] = r_ref[s, :COLS].astype(F32)
             bc_ref[rows, N:] = r_ref[s, COLS : 2 * COLS].astype(F32)
         copies.append(pltpu.make_async_copy(bc_ref.at[at], bc_hbm.at[at], sems.at[i, 0]))
         copies[-1].start()
+    for i, at in enumerate(spans):
+        part = range(i * parts, (i + 1) * parts)
         steps = jnp.concatenate([unfold_steps(r_ref[s]) for s in part], axis=0)
         dt_ref[:, at] = steps.T[:H]
         copies.append(pltpu.make_async_copy(dt_ref.at[:, at], dt_hbm.at[:, at], sems.at[i, 1]))

time: 146 us -> 146 us (level)
  no operation moved by 1% of the time
where the time goes in v7:
time: 146 us
  waiting for transfers between devices  58.4 us (40%)
  starting transfers between devices  41 us (28%)
  blocking collectives  25.9 us (18%)
  Pallas kernels  18.6 us (13%)
    all_to_all x4, waiting for transfers between devices, exchange(): return lax.all_to_all(v, axis, split_axis=0, concat_axis=0, tiled=True)  41 us
    all_to_all x2, blocking collectives, exchange(): return lax.all_to_all(v, axis, split_axis=0, concat_axis=0, tiled=True)  25.9 us
    all_to_all x4, starting transfers between devices, exchange(): return lax.all_to_all(v, axis, split_axis=0, concat_axis=0, tiled=True)  23.7 us
    pallas_call x14, Pallas kernels, call(): pl.pallas_call(kernel, out_shape=[jax.ShapeDtypeStruct(shape, kind) for s...  16.4 us
    ppermute x7, starting transfers between devices, per_device(): blocks[j] = lax.ppermute(blocks[j], 'head', ring)  12.8 us
    ppermute x2, waiting for transfers between devices, per_device(): other = lax.ppermute(w_part, 'head', [(i, i ^ far) for i in range(HEAD)])  8.62 us
    ppermute x1, waiting for transfers between devices, per_device(): other = lax.ppermute(w_part, 'head', [(i, i ^ 7) for i in range(HEAD)])  5.55 us
    ppermute x7, waiting for transfers between devices, per_device(): blocks[j] = lax.ppermute(blocks[j], 'head', ring)  3.33 us
  transfers between devices with their start and end apart: 14, of which 10 were waited for; matrix products, arithmetic and copies ran while one was open for 0% of the time, Pallas kernels for 4%

profile of v7, /device:TPU:32, one launch (start us, length us, event | category | flops | bytes accessed | tf_op | source)
XLA Modules:
  0.0 145.7 jit_solution(15497688266606199168)
XLA Ops:
  0.6 0.0 copy-start.2
  0.6 3.0 %shard_map.127 = bf16[8,32,1664]{2,1,0:T(8,128)(2,1)} custom-call(bf16[32,2560]{1,0:T(8,128)(2,1)} %hid_ref.1, bf16[2560,256]{1,0:T(8,128)(2,1)} %wbc_ref.1, bf16[80,2560]{1,0:T(8,128)(2,1)} %bitcast.9, bf16[32,5120]{1,0:T(8,128)(2,1)} %x_hbm.1, bf16[32,5120]{1,0:T(8,128)(2,1)} %g_hbm.1), custom_call_target="tpu_custom_call" | custom-call | tf_op jit(solution)/shard_map/pallas_call | solution.py:403
  3.6 0.0 copy-start.5
  3.6 0.0 copy-start.6
  3.6 0.0 copy-start.7
  3.7 8.7 %all-to-all-start = ((bf16[8,32,1664]{2,1,0:T(8,128)(2,1)}), bf16[8,32,1664]{2,1,0:T(8,128)(2,1)S(1)}, u32[]{:S(2)}, u32[]{:S(2)}) async-start(bf16[8,32,1664]{2,1,0:T(8,128)(2,1)} %shard_map.127), calls=%async_computation | async-start | bytes 1703936 | tf_op jit(solution)/shard_map/all_to_all | solution.py:429
  12.4 0.0 copy-done.2
  12.4 0.1 shard_map.128.hs_ref
  12.5 0.0 copy-done.5
  12.5 0.0 copy-done.6
  12.5 0.0 copy-done.7
  12.5 22.9 %all-to-all-done = bf16[8,32,1664]{2,1,0:T(8,128)(2,1)S(1)} async-done(((bf16[8,32,1664]{2,1,0:T(8,128)(2,1)}), bf16[8,32,1664]{2,1,0:T(8,128)(2,1)S(1)}, u32[]{:S(2)}, u32[]{:S(2)}) %all-to-all-start) | async-done | bytes 852000 | tf_op jit(solution)/shard_map/all_to_all | solution.py:429
  35.4 1.9 %shard_map.129 = bf16[16,16,1024]{2,1,0:T(8,128)(2,1)} custom-call(bf16[256,1664]{1,0:T(8,128)(2,1)S(1)} %bitcast.6, f32[8,128]{1,0:T(8,128)S(1)} %select_maximum_fusion.prm_ref, bf16[16,16,384]{2,1,0:T(8,128)(2,1)S(1)} %shard_map.128.hs_ref), custom_call_target="tpu_custom_call" | custom-call | tf_op jit(solution)/shard_map/pallas_call | solution.py:403
  37.3 7.0 %all-to-all-start.1 = ((bf16[16,16,1024]{2,1,0:T(8,128)(2,1)}), bf16[16,16,1024]{2,1,0:T(8,128)(2,1)S(1)}, u32[]{:S(2)}, u32[]{:S(2)}) async-start(bf16[16,16,1024]{2,1,0:T(8,128)(2,1)} %shard_map.129), calls=%async_computation.1 | async-start | bytes 1048576 | tf_op jit(solution)/shard_map/all_to_all | solution.py:429
  44.4 2.3 %shard_map.130.in_ref = f32[256,1792]{1,0:T(8,128)S(1)} custom-call(bf16[256,1664]{1,0:T(8,128)(2,1)S(1)} %bitcast.7, f32[8,128]{1,0:T(8,128)S(1)} %select_maximum_fusion.prm_ref), custom_call_target="tpu_custom_call" | custom-call | tf_op jit(solution)/shard_map/pallas_call | solution.py:403
  46.7 7.8 %all-to-all-done.1.r_ref.h_ref = bf16[16,16,1024]{2,1,0:T(8,128)(2,1)S(1)} async-done(((bf16[16,16,1024]{2,1,0:T(8,128)(2,1)}), bf16[16,16,1024]{2,1,0:T(8,128)(2,1)S(1)}, u32[]{:S(2)}, u32[]{:S(2)}) %all-to-all-start.1) | async-done | bytes 524320 | tf_op jit(solution)/shard_map/all_to_all | solution.py:429
  54.5 0.2 shard_map.131
  54.7 12.0 %all_to_all.30.st_ref = bf16[16,16,640]{2,1,0:T(8,128)(2,1)S(1)} all-to-all(bf16[16,16,640]{2,1,0:T(8,128)(2,1)S(1)} %shard_map.131), channel_id=1, replica_groups=mesh['seq'=16,'head'=8,'dp'=2] {'seq'}, dimensions={0} | all-to-all | bytes 655360 | tf_op jit(solution)/shard_map/all_to_all | solution.py:429
  66.7 2.5 %shard_map.132 = (bf16[8,32,384]{2,1,0:T(8,128)(2,1)S(1)}, bf16[256,1280]{1,0:T(8,128)(2,1)S(1)}) custom-call(bf16[256,1664]{1,0:T(8,128)(2,1)S(1)} %bitcast.8, f32[8,128]{1,0:T(8,128)S(1)} %select_maximum_fusion.prm_ref, bf16[16,16,640]{2,1,0:T(8,128)(2,1)S(1)} %all_to_all.30.st_ref, f32[256,1792]{1,0:T(8,128)S(1)} %shard_map.130.in_ref), custom_call_target="tpu_custom_call" | custom-call | tf_op jit(solution)/shard_map/pallas_call | solution.py:403
  69.3 0.0 copy-start.3
  69.3 0.8 copy-done.3
  70.1 0.0 copy-start
  70.1 0.0 copy-start.1
  70.1 13.9 %all_to_all.31.r_ref = bf16[8,32,384]{2,1,0:T(8,128)(2,1)S(1)} all-to-all(bf16[8,32,384]{2,1,0:T(8,128)(2,1)S(1)} %get-tuple-element.30), channel_id=1, replica_groups=mesh['seq'=16,'head'=8,'dp'=2] {'head'}, dimensions={0} | all-to-all | bytes 393216 | tf_op jit(solution)/shard_map/all_to_all | solution.py:429
  84.0 0.9 shard_map.133.d_ref
  84.8 3.6 %all-to-all-start.4 = ((bf16[16,32,384]{2,1,0:T(8,128)(2,1)}), bf16[16,32,384]{2,1,0:T(8,128)(2,1)S(1)}, u32[]{:S(2)}, u32[]{:S(2)}) async-start(bf16[16,32,384]{2,1,0:T(8,128)(2,1)} %shard_map.133.d_ref), calls=%async_computation.4 | async-start | bytes 786432 | tf_op jit(solution)/shard_map/all_to_all | solution.py:429
  88.4 0.0 copy-done
  88.4 0.0 copy-done.1
  88.4 2.3 %shard_map.134 = bf16[32,2560]{1,0:T(8,128)(2,1)} custom-call(bf16[16,32,384]{2,1,0:T(8,128)(2,1)} %shard_map.133.d_ref, bf16[2560,256]{1,0:T(8,128)(2,1)S(1)} %copy-done, bf16[80,2560]{1,0:T(8,128)(2,1)S(1)} %bitcast.10), custom_call_target="tpu_custom_call" | custom-call | tf_op jit(solution)/shard_map/pallas_call | solution.py:403
  90.7 7.1 %all-to-all-done.4.d_ref = bf16[16,32,384]{2,1,0:T(8,128)(2,1)S(1)} async-done(((bf16[16,32,384]{2,1,0:T(8,128)(2,1)}), bf16[16,32,384]{2,1,0:T(8,128)(2,1)S(1)}, u32[]{:S(2)}, u32[]{:S(2)}) %all-to-all-start.4) | async-done | bytes 393248 | tf_op jit(solution)/shard_map/all_to_all | solution.py:429
  97.8 0.9 shard_map.135
  98.7 1.5 %collective-permute-start = (bf16[432,128]{1,0:T(8,128)(2,1)S(1)}, bf16[432,128]{1,0:T(8,128)(2,1)S(1)}, u32[]{:S(2)}, u32[]{:S(2)}) collective-permute-start(bf16[432,128]{1,0:T(8,128)(2,1)S(1)} %get-tuple-element.32.a_ref), channel_id=1, source_target_pairs={{0,2},{2,0},{4,6},{6,4},{8,10},{10,8},{12,14},{14,12},{1,3},{3,1},... | collective-permute-start | bytes 331784 | tf_op jit(solution)/shard_map/ppermute | solution.py:486
  100.1 3.4 %collective-permute-done.b_ref = bf16[432,128]{1,0:T(8,128)(2,1)S(1)} collective-permute-done((bf16[432,128]{1,0:T(8,128)(2,1)S(1)}, bf16[432,128]{1,0:T(8,128)(2,1)S(1)}, u32[]{:S(2)}, u32[]{:S(2)}) %collective-permute-start) | collective-permute-done | bytes 110624 | tf_op jit(solution)/shard_map/ppermute | solution.py:486
  103.5 0.6 collective-permute-start.1
  104.1 5.2 %collective-permute-done.1.b_ref = bf16[432,128]{1,0:T(8,128)(2,1)S(1)} collective-permute-done((bf16[432,128]{1,0:T(8,128)(2,1)S(1)}, bf16[432,128]{1,0:T(8,128)(2,1)S(1)}, u32[]{:S(2)}, u32[]{:S(2)}) %collective-permute-start.1) | collective-permute-done | bytes 110624 | tf_op jit(solution)/shard_map/ppermute | solution.py:486
  109.4 2.4 %collective-permute-start.2 = (bf16[432,128]{1,0:T(8,128)(2,1)S(1)}, bf16[432,128]{1,0:T(8,128)(2,1)S(1)}, u32[]{:S(2)}, u32[]{:S(2)}) collective-permute-start(bf16[432,128]{1,0:T(8,128)(2,1)S(1)} %shard_map.137.a_ref), channel_id=1, source_target_pairs={{0,14},{2,12},{4,10},{6,8},{8,6},{10,4},{12,2},{14,0},{1,15},{3,13... | collective-permute-start | bytes 331784 | tf_op jit(solution)/shard_map/ppermute | solution.py:488
  111.8 5.5 %collective-permute-done.2.b_ref = bf16[432,128]{1,0:T(8,128)(2,1)S(1)} collective-permute-done((bf16[432,128]{1,0:T(8,128)(2,1)S(1)}, bf16[432,128]{1,0:T(8,128)(2,1)S(1)}, u32[]{:S(2)}, u32[]{:S(2)}) %collective-permute-start.2) | collective-permute-done | bytes 110624 | tf_op jit(solution)/shard_map/ppermute | solution.py:488
  117.3 1.3 shard_map.138
  118.6 0.0 copy-start.4
  118.6 4.4 %all-to-all-start.5 = ((bf16[16,432,128]{2,1,0:T(8,128)(2,1)}), bf16[16,432,128]{2,1,0:T(8,128)(2,1)S(1)}, u32[]{:S(2)}, u32[]{:S(2)}) async-start(bf16[16,432,128]{2,1,0:T(8,128)(2,1)} %shard_map.138), calls=%async_computation.5 | async-start | bytes 3538944 | tf_op jit(solution)/shard_map/all_to_all | solution.py:429
  123.1 0.0 copy-done.4
  123.1 0.1 shard_map.139
  123.2 1.2 collective-permute-start.3
  124.4 4.4 %collective-permute-start.4 = (bf16[32,1280]{1,0:T(8,128)(2,1)S(1)}, bf16[32,1280]{1,0:T(8,128)(2,1)S(1)}, u32[]{:S(2)}, u32[]{:S(2)}) collective-permute-start(bf16[32,1280]{1,0:T(8,128)(2,1)S(1)} %get-tuple-element.37), channel_id=1, source_target_pairs={{0,6},{2,8},{4,10},{6,12},{8,14},{10,0},{12,2},{14,4},{1,7},{3,9},... | collective-permute-start | bytes 245768 | tf_op jit(solution)/shard_map/ppermute | solution.py:501
  128.8 0.6 collective-permute-start.5
  129.4 0.6 collective-permute-start.6
  130.0 3.6 %collective-permute-start.7 = (bf16[32,1280]{1,0:T(8,128)(2,1)S(1)}, bf16[32,1280]{1,0:T(8,128)(2,1)S(1)}, u32[]{:S(2)}, u32[]{:S(2)}) collective-permute-start(bf16[32,1280]{1,0:T(8,128)(2,1)S(1)} %get-tuple-element.40), channel_id=1, source_target_pairs={{0,12},{2,14},{4,0},{6,2},{8,4},{10,6},{12,8},{14,10},{1,13},{3,15... | collective-permute-start | bytes 245768 | tf_op jit(solution)/shard_map/ppermute | solution.py:501
  133.5 0.0 collective-permute-done.3.refs_1_
  133.5 0.9 collective-permute-start.8
  134.4 0.0 collective-permute-done.4.refs_2_
  134.4 1.6 %collective-permute-start.9 = (bf16[32,1280]{1,0:T(8,128)(2,1)S(1)}, bf16[32,1280]{1,0:T(8,128)(2,1)S(1)}, u32[]{:S(2)}, u32[]{:S(2)}) collective-permute-start(bf16[32,1280]{1,0:T(8,128)(2,1)S(1)} %get-tuple-element.42), channel_id=1, source_target_pairs={{0,14},{2,0},{4,2},{6,4},{8,6},{10,8},{12,10},{14,12},{1,15},{3,1}... | collective-permute-start | bytes 245768 | tf_op jit(solution)/shard_map/ppermute | solution.py:501
  136.0 2.0 %collective-permute-done.5.refs_3_ = bf16[32,1280]{1,0:T(8,128)(2,1)S(1)} collective-permute-done((bf16[32,1280]{1,0:T(8,128)(2,1)S(1)}, bf16[32,1280]{1,0:T(8,128)(2,1)S(1)}, u32[]{:S(2)}, u32[]{:S(2)}) %collective-permute-start.5) | collective-permute-done | bytes 81952 | tf_op jit(solution)/shard_map/ppermute | solution.py:501
  138.0 0.0 collective-permute-done.6.refs_4_
  138.0 0.5 collective-permute-done.7.refs_5_
  138.5 0.0 collective-permute-done.8.refs_6_
  138.5 0.8 collective-permute-done.9.refs_7_
  139.3 0.9 shard_map.140
  140.2 3.2 %all-to-all-done.5.r_ref = bf16[16,432,128]{2,1,0:T(8,128)(2,1)S(1)} async-done(((bf16[16,432,128]{2,1,0:T(8,128)(2,1)}), bf16[16,432,128]{2,1,0:T(8,128)(2,1)S(1)}, u32[]{:S(2)}, u32[]{:S(2)}) %all-to-all-start.5) | async-done | bytes 1769504 | tf_op jit(solution)/shard_map/all_to_all | solution.py:429
  143.4 2.2 %shard_map.141 = (f32[2560,256]{1,0:T(8,128)}, f32[80,2560]{1,0:T(8,128)}) custom-call(bf16[16,432,128]{2,1,0:T(8,128)(2,1)S(1)} %all-to-all-done.5.r_ref), custom_call_target="tpu_custom_call" | custom-call | tf_op jit(solution)/shard_map/pallas_call | solution.py:414
  (3 shorter events, 0.1 us)
Async XLA Ops:
  0.6 11.7 %copy-start.2 = (bf16[32,2560]{1,0:T(8,128)(2,1)S(1)}, bf16[32,2560]{1,0:T(8,128)(2,1)}, u32[]{:S(2)}) copy-start(bf16[32,2560]{1,0:T(8,128)(2,1)} %hid_ref.1) | copy-start | bytes 491524
  3.6 8.9 %copy-start.5 = (f32[80]{0:T(128)S(1)}, f32[80]{0:T(128)}, u32[]{:S(2)}) copy-start(f32[80]{0:T(128)} %param.15) | copy-start | bytes 964
  3.6 8.9 %copy-start.6 = (f32[80]{0:T(128)S(1)}, f32[80]{0:T(128)}, u32[]{:S(2)}) copy-start(f32[80]{0:T(128)} %param.14) | copy-start | bytes 964
  3.6 8.9 %copy-start.7 = (f32[80]{0:T(128)S(1)}, f32[80]{0:T(128)}, u32[]{:S(2)}) copy-start(f32[80]{0:T(128)} %param.13) | copy-start | bytes 964
  3.7 31.8 %all-to-all-start = ((bf16[8,32,1664]{2,1,0:T(8,128)(2,1)}), bf16[8,32,1664]{2,1,0:T(8,128)(2,1)S(1)}, u32[]{:S(2)}, u32[]{:S(2)}) async-start(bf16[8,32,1664]{2,1,0:T(8,128)(2,1)} %shard_map.127), calls=%async_computation | async-start | bytes 1703936 | tf_op jit(solution)/shard_map/all_to_all | solution.py:429
  37.3 17.2 %all-to-all-start.1 = ((bf16[16,16,1024]{2,1,0:T(8,128)(2,1)}), bf16[16,16,1024]{2,1,0:T(8,128)(2,1)S(1)}, u32[]{:S(2)}, u32[]{:S(2)}) async-start(bf16[16,16,1024]{2,1,0:T(8,128)(2,1)} %shard_map.129), calls=%async_computation.1 | async-start | bytes 1048576 | tf_op jit(solution)/shard_map/all_to_all | solution.py:429
  69.3 0.8 copy-start.3
  70.1 18.3 %copy-start = (bf16[2560,256]{1,0:T(8,128)(2,1)S(1)}, bf16[2560,256]{1,0:T(8,128)(2,1)}, u32[]{:S(2)}) copy-start(bf16[2560,256]{1,0:T(8,128)(2,1)} %wbc_ref.1) | copy-start | bytes 3932164
  70.1 18.3 %copy-start.1 = (bf16[2560,80]{0,1:T(8,128)(2,1)S(1)}, bf16[2560,80]{0,1:T(8,128)(2,1)}, u32[]{:S(2)}) copy-start(bf16[2560,80]{0,1:T(8,128)(2,1)} %param.12) | copy-start | bytes 1228804
  84.8 12.9 %all-to-all-start.4 = ((bf16[16,32,384]{2,1,0:T(8,128)(2,1)}), bf16[16,32,384]{2,1,0:T(8,128)(2,1)S(1)}, u32[]{:S(2)}, u32[]{:S(2)}) async-start(bf16[16,32,384]{2,1,0:T(8,128)(2,1)} %shard_map.133.d_ref), calls=%async_computation.4 | async-start | bytes 786432 | tf_op jit(solution)/shard_map/all_to_all | solution.py:429
  98.7 4.8 %collective-permute-start = (bf16[432,128]{1,0:T(8,128)(2,1)S(1)}, bf16[432,128]{1,0:T(8,128)(2,1)S(1)}, u32[]{:S(2)}, u32[]{:S(2)}) collective-permute-start(bf16[432,128]{1,0:T(8,128)(2,1)S(1)} %get-tuple-element.32.a_ref), channel_id=1, source_target_pairs={{0,2},{2,0},{4,6},{6,4},{8,10},{10,8},{12,14},{14,12},{1,3},{3,1},... | collective-permute-start | bytes 331784 | tf_op jit(solution)/shard_map/ppermute | solution.py:486
  103.5 5.8 %collective-permute-start.1 = (bf16[432,128]{1,0:T(8,128)(2,1)S(1)}, bf16[432,128]{1,0:T(8,128)(2,1)S(1)}, u32[]{:S(2)}, u32[]{:S(2)}) collective-permute-start(bf16[432,128]{1,0:T(8,128)(2,1)S(1)} %shard_map.136.a_ref), channel_id=1, source_target_pairs={{0,4},{2,6},{4,0},{6,2},{8,12},{10,14},{12,8},{14,10},{1,5},{3,7},... | collective-permute-start | bytes 331784 | tf_op jit(solution)/shard_map/ppermute | solution.py:486
  109.4 7.9 %collective-permute-start.2 = (bf16[432,128]{1,0:T(8,128)(2,1)S(1)}, bf16[432,128]{1,0:T(8,128)(2,1)S(1)}, u32[]{:S(2)}, u32[]{:S(2)}) collective-permute-start(bf16[432,128]{1,0:T(8,128)(2,1)S(1)} %shard_map.137.a_ref), channel_id=1, source_target_pairs={{0,14},{2,12},{4,10},{6,8},{8,6},{10,4},{12,2},{14,0},{1,15},{3,13... | collective-permute-start | bytes 331784 | tf_op jit(solution)/shard_map/ppermute | solution.py:488
  118.6 4.5 %copy-start.4 = (bf16[256,1280]{1,0:T(8,128)(2,1)S(1)}, bf16[256,1280]{1,0:T(8,128)(2,1)}, u32[]{:S(2)}) copy-start(bf16[256,1280]{1,0:T(8,128)(2,1)} %copy-done.3) | copy-start | bytes 1966084
  118.6 24.7 %all-to-all-start.5 = ((bf16[16,432,128]{2,1,0:T(8,128)(2,1)}), bf16[16,432,128]{2,1,0:T(8,128)(2,1)S(1)}, u32[]{:S(2)}, u32[]{:S(2)}) async-start(bf16[16,432,128]{2,1,0:T(8,128)(2,1)} %shard_map.138), calls=%async_computation.5 | async-start | bytes 3538944 | tf_op jit(solution)/shard_map/all_to_all | solution.py:429
  123.2 10.4 %collective-permute-start.3 = (bf16[32,1280]{1,0:T(8,128)(2,1)S(1)}, bf16[32,1280]{1,0:T(8,128)(2,1)S(1)}, u32[]{:S(2)}, u32[]{:S(2)}) collective-permute-start(bf16[32,1280]{1,0:T(8,128)(2,1)S(1)} %get-tuple-element.36), channel_id=1, source_target_pairs={{0,8},{2,10},{4,12},{6,14},{8,0},{10,2},{12,4},{14,6},{1,9},{3,11}... | collective-permute-start | bytes 245768 | tf_op jit(solution)/shard_map/ppermute | solution.py:501
  124.4 10.0 %collective-permute-start.4 = (bf16[32,1280]{1,0:T(8,128)(2,1)S(1)}, bf16[32,1280]{1,0:T(8,128)(2,1)S(1)}, u32[]{:S(2)}, u32[]{:S(2)}) collective-permute-start(bf16[32,1280]{1,0:T(8,128)(2,1)S(1)} %get-tuple-element.37), channel_id=1, source_target_pairs={{0,6},{2,8},{4,10},{6,12},{8,14},{10,0},{12,2},{14,4},{1,7},{3,9},... | collective-permute-start | bytes 245768 | tf_op jit(solution)/shard_map/ppermute | solution.py:501
  128.8 9.2 %collective-permute-start.5 = (bf16[32,1280]{1,0:T(8,128)(2,1)S(1)}, bf16[32,1280]{1,0:T(8,128)(2,1)S(1)}, u32[]{:S(2)}, u32[]{:S(2)}) collective-permute-start(bf16[32,1280]{1,0:T(8,128)(2,1)S(1)} %get-tuple-element.38), channel_id=1, source_target_pairs={{0,10},{2,12},{4,14},{6,0},{8,2},{10,4},{12,6},{14,8},{1,11},{3,13... | collective-permute-start | bytes 245768 | tf_op jit(solution)/shard_map/ppermute | solution.py:501
  129.4 8.6 %collective-permute-start.6 = (bf16[32,1280]{1,0:T(8,128)(2,1)S(1)}, bf16[32,1280]{1,0:T(8,128)(2,1)S(1)}, u32[]{:S(2)}, u32[]{:S(2)}) collective-permute-start(bf16[32,1280]{1,0:T(8,128)(2,1)S(1)} %get-tuple-element.39), channel_id=1, source_target_pairs={{0,4},{2,6},{4,8},{6,10},{8,12},{10,14},{12,0},{14,2},{1,5},{3,7},... | collective-permute-start | bytes 245768 | tf_op jit(solution)/shard_map/ppermute | solution.py:501
  130.0 8.5 %collective-permute-start.7 = (bf16[32,1280]{1,0:T(8,128)(2,1)S(1)}, bf16[32,1280]{1,0:T(8,128)(2,1)S(1)}, u32[]{:S(2)}, u32[]{:S(2)}) collective-permute-start(bf16[32,1280]{1,0:T(8,128)(2,1)S(1)} %get-tuple-element.40), channel_id=1, source_target_pairs={{0,12},{2,14},{4,0},{6,2},{8,4},{10,6},{12,8},{14,10},{1,13},{3,15... | collective-permute-start | bytes 245768 | tf_op jit(solution)/shard_map/ppermute | solution.py:501
  133.5 5.0 %collective-permute-start.8 = (bf16[32,1280]{1,0:T(8,128)(2,1)S(1)}, bf16[32,1280]{1,0:T(8,128)(2,1)S(1)}, u32[]{:S(2)}, u32[]{:S(2)}) collective-permute-start(bf16[32,1280]{1,0:T(8,128)(2,1)S(1)} %get-tuple-element.41), channel_id=1, source_target_pairs={{0,2},{2,4},{4,6},{6,8},{8,10},{10,12},{12,14},{14,0},{1,3},{3,5},... | collective-permute-start | bytes 245768 | tf_op jit(solution)/shard_map/ppermute | solution.py:501
  134.4 4.9 %collective-permute-start.9 = (bf16[32,1280]{1,0:T(8,128)(2,1)S(1)}, bf16[32,1280]{1,0:T(8,128)(2,1)S(1)}, u32[]{:S(2)}, u32[]{:S(2)}) collective-permute-start(bf16[32,1280]{1,0:T(8,128)(2,1)S(1)} %get-tuple-element.42), channel_id=1, source_target_pairs={{0,14},{2,0},{4,2},{6,4},{8,6},{10,8},{12,10},{14,12},{1,15},{3,1}... | collective-permute-start | bytes 245768 | tf_op jit(solution)/shard_map/ppermute | solution.py:501

commit v8 on v6

--- a/solution.py
+++ b/solution.py
@@ -225,9 +225,8 @@
     pre, step, cum, rate, skip = step_sizes(r_ref, prm_ref, in_ref[:, PACK:])
     hot = one_hot()
     total = cum[SPAN - 1 :]
-    step_x = spread(step, hot)
-    to_end = spread(jnp.exp(total - cum), hot)
-    from_start = spread(jnp.exp(cum), hot)
+    wide = spread(jnp.concatenate([step, jnp.exp(total - cum), jnp.exp(cum)], axis=0), hot)
+    step_x, to_end, from_start = (wide[i * SPAN : (i + 1) * SPAN] for i in range(3))
     skip_x = spread(jnp.broadcast_to(skip, (8, LANES)), hot)[:1]
     states = st_ref[...].astype(F32)
     state_in = states[:, :SLAB].reshape(N, CH)
@@ -246,9 +245,9 @@
     gx = step_x * du + skip_x * g
     d_c = in_ref[:, 2 * CH + N : STEP] + dot((g * from_start).astype(BF16), s_b, 1, 1)
     d_b = in_ref[:, 2 * CH : 2 * CH + N] + dot((u * to_end).astype(BF16), q_b, 1, 1)
-    e = in_ref[:, STEP:PACK] + gather_heads(g * carried, hot)
-    f = gather_heads(u * late, hot)
-    xdu = gather_heads(x * du, hot)
+    narrow = gather_heads(jnp.concatenate([g * carried, u * late, x * du], axis=0), hot)
+    e, f, xdu = (narrow[i * SPAN : (i + 1) * SPAN] for i in range(3))
+    e += in_ref[:, STEP:PACK]
     sums = jnp.concatenate(
         [
             jnp.sum(state_in * state_gr, axis=0, keepdims=True),

time: 146 us -> 146 us (level)
  no operation moved by 1% of the time
where the time goes in v8:
time: 146 us
  waiting for transfers between devices  58.7 us (40%)
  starting transfers between devices  40.9 us (28%)
  blocking collectives  25.7 us (18%)
  Pallas kernels  18.7 us (13%)
    all_to_all x4, waiting for transfers between devices, exchange(): return lax.all_to_all(v, axis, split_axis=0, concat_axis=0, tiled=True)  40.9 us
    all_to_all x2, blocking collectives, exchange(): return lax.all_to_all(v, axis, split_axis=0, concat_axis=0, tiled=True)  25.7 us
    all_to_all x4, starting transfers between devices, exchange(): return lax.all_to_all(v, axis, split_axis=0, concat_axis=0, tiled=True)  23.6 us
    pallas_call x14, Pallas kernels, call(): pl.pallas_call(kernel, out_shape=[jax.ShapeDtypeStruct(shape, kind) for s...  16.5 us
    ppermute x7, starting transfers between devices, per_device(): blocks[j] = lax.ppermute(blocks[j], 'head', ring)  12.8 us
    ppermute x2, waiting for transfers between devices, per_device(): other = lax.ppermute(w_part, 'head', [(i, i ^ far) for i in range(HEAD)])  8.71 us
    ppermute x1, waiting for transfers between devices, per_device(): other = lax.ppermute(w_part, 'head', [(i, i ^ 7) for i in range(HEAD)])  5.68 us
    ppermute x7, waiting for transfers between devices, per_device(): blocks[j] = lax.ppermute(blocks[j], 'head', ring)  3.35 us
  transfers between devices with their start and end apart: 14, of which 10 were waited for; matrix products, arithmetic and copies ran while one was open for 0% of the time, Pallas kernels for 4%

profile of v8, /device:TPU:32, one launch (start us, length us, event | category | flops | bytes accessed | tf_op | source)
XLA Modules:
  0.0 145.8 jit_solution(6613132698005353985)
XLA Ops:
  0.6 0.0 copy-start.2
  0.6 3.0 %shard_map.127 = bf16[8,32,1664]{2,1,0:T(8,128)(2,1)} custom-call(bf16[32,2560]{1,0:T(8,128)(2,1)} %hid_ref.1, bf16[2560,256]{1,0:T(8,128)(2,1)} %wbc_ref.1, bf16[80,2560]{1,0:T(8,128)(2,1)} %bitcast.9, bf16[32,5120]{1,0:T(8,128)(2,1)} %x_hbm.1, bf16[32,5120]{1,0:T(8,128)(2,1)} %g_hbm.1), custom_call_target="tpu_custom_call" | custom-call | tf_op jit(solution)/shard_map/pallas_call | solution.py:401
  3.6 0.0 copy-start.5
  3.6 0.0 copy-start.6
  3.6 0.0 copy-start.7
  3.7 8.7 %all-to-all-start = ((bf16[8,32,1664]{2,1,0:T(8,128)(2,1)}), bf16[8,32,1664]{2,1,0:T(8,128)(2,1)S(1)}, u32[]{:S(2)}, u32[]{:S(2)}) async-start(bf16[8,32,1664]{2,1,0:T(8,128)(2,1)} %shard_map.127), calls=%async_computation | async-start | bytes 1703936 | tf_op jit(solution)/shard_map/all_to_all | solution.py:427
  12.4 0.0 copy-done.2
  12.4 0.1 shard_map.128.hs_ref
  12.5 0.0 copy-done.5
  12.5 0.0 copy-done.6
  12.5 0.0 copy-done.7
  12.5 22.9 %all-to-all-done = bf16[8,32,1664]{2,1,0:T(8,128)(2,1)S(1)} async-done(((bf16[8,32,1664]{2,1,0:T(8,128)(2,1)}), bf16[8,32,1664]{2,1,0:T(8,128)(2,1)S(1)}, u32[]{:S(2)}, u32[]{:S(2)}) %all-to-all-start) | async-done | bytes 852000 | tf_op jit(solution)/shard_map/all_to_all | solution.py:427
  35.4 1.9 %shard_map.129 = bf16[16,16,1024]{2,1,0:T(8,128)(2,1)} custom-call(bf16[256,1664]{1,0:T(8,128)(2,1)S(1)} %bitcast.6, f32[8,128]{1,0:T(8,128)S(1)} %select_maximum_fusion.prm_ref, bf16[16,16,384]{2,1,0:T(8,128)(2,1)S(1)} %shard_map.128.hs_ref), custom_call_target="tpu_custom_call" | custom-call | tf_op jit(solution)/shard_map/pallas_call | solution.py:401
  37.3 7.0 %all-to-all-start.1 = ((bf16[16,16,1024]{2,1,0:T(8,128)(2,1)}), bf16[16,16,1024]{2,1,0:T(8,128)(2,1)S(1)}, u32[]{:S(2)}, u32[]{:S(2)}) async-start(bf16[16,16,1024]{2,1,0:T(8,128)(2,1)} %shard_map.129), calls=%async_computation.1 | async-start | bytes 1048576 | tf_op jit(solution)/shard_map/all_to_all | solution.py:427
  44.4 2.3 %shard_map.130.in_ref = f32[256,1792]{1,0:T(8,128)S(1)} custom-call(bf16[256,1664]{1,0:T(8,128)(2,1)S(1)} %bitcast.7, f32[8,128]{1,0:T(8,128)S(1)} %select_maximum_fusion.prm_ref), custom_call_target="tpu_custom_call" | custom-call | tf_op jit(solution)/shard_map/pallas_call | solution.py:401
  46.7 7.8 %all-to-all-done.1.r_ref.h_ref = bf16[16,16,1024]{2,1,0:T(8,128)(2,1)S(1)} async-done(((bf16[16,16,1024]{2,1,0:T(8,128)(2,1)}), bf16[16,16,1024]{2,1,0:T(8,128)(2,1)S(1)}, u32[]{:S(2)}, u32[]{:S(2)}) %all-to-all-start.1) | async-done | bytes 524320 | tf_op jit(solution)/shard_map/all_to_all | solution.py:427
  54.5 0.2 shard_map.131
  54.7 12.0 %all_to_all.30.st_ref = bf16[16,16,640]{2,1,0:T(8,128)(2,1)S(1)} all-to-all(bf16[16,16,640]{2,1,0:T(8,128)(2,1)S(1)} %shard_map.131), channel_id=1, replica_groups=mesh['seq'=16,'head'=8,'dp'=2] {'seq'}, dimensions={0} | all-to-all | bytes 655360 | tf_op jit(solution)/shard_map/all_to_all | solution.py:427
  66.7 2.6 %shard_map.132 = (bf16[8,32,384]{2,1,0:T(8,128)(2,1)S(1)}, bf16[256,1280]{1,0:T(8,128)(2,1)S(1)}) custom-call(bf16[256,1664]{1,0:T(8,128)(2,1)S(1)} %bitcast.8, f32[8,128]{1,0:T(8,128)S(1)} %select_maximum_fusion.prm_ref, bf16[16,16,640]{2,1,0:T(8,128)(2,1)S(1)} %all_to_all.30.st_ref, f32[256,1792]{1,0:T(8,128)S(1)} %shard_map.130.in_ref), custom_call_target="tpu_custom_call" | custom-call | tf_op jit(solution)/shard_map/pallas_call | solution.py:401
  69.3 0.0 copy-start.3
  69.3 0.8 copy-done.3
  70.1 0.0 copy-start
  70.1 0.0 copy-start.1
  70.1 13.7 %all_to_all.31.r_ref = bf16[8,32,384]{2,1,0:T(8,128)(2,1)S(1)} all-to-all(bf16[8,32,384]{2,1,0:T(8,128)(2,1)S(1)} %get-tuple-element.30), channel_id=1, replica_groups=mesh['seq'=16,'head'=8,'dp'=2] {'head'}, dimensions={0} | all-to-all | bytes 393216 | tf_op jit(solution)/shard_map/all_to_all | solution.py:427
  83.9 0.9 shard_map.133.d_ref
  84.7 3.6 %all-to-all-start.4 = ((bf16[16,32,384]{2,1,0:T(8,128)(2,1)}), bf16[16,32,384]{2,1,0:T(8,128)(2,1)S(1)}, u32[]{:S(2)}, u32[]{:S(2)}) async-start(bf16[16,32,384]{2,1,0:T(8,128)(2,1)} %shard_map.133.d_ref), calls=%async_computation.4 | async-start | bytes 786432 | tf_op jit(solution)/shard_map/all_to_all | solution.py:427
  88.3 0.0 copy-done
  88.3 0.0 copy-done.1
  88.3 2.3 %shard_map.134 = bf16[32,2560]{1,0:T(8,128)(2,1)} custom-call(bf16[16,32,384]{2,1,0:T(8,128)(2,1)} %shard_map.133.d_ref, bf16[2560,256]{1,0:T(8,128)(2,1)S(1)} %copy-done, bf16[80,2560]{1,0:T(8,128)(2,1)S(1)} %bitcast.10), custom_call_target="tpu_custom_call" | custom-call | tf_op jit(solution)/shard_map/pallas_call | solution.py:401
  90.6 7.1 %all-to-all-done.4.d_ref = bf16[16,32,384]{2,1,0:T(8,128)(2,1)S(1)} async-done(((bf16[16,32,384]{2,1,0:T(8,128)(2,1)}), bf16[16,32,384]{2,1,0:T(8,128)(2,1)S(1)}, u32[]{:S(2)}, u32[]{:S(2)}) %all-to-all-start.4) | async-done | bytes 393248 | tf_op jit(solution)/shard_map/all_to_all | solution.py:427
  97.6 0.9 shard_map.135
  98.5 1.6 %collective-permute-start = (bf16[432,128]{1,0:T(8,128)(2,1)S(1)}, bf16[432,128]{1,0:T(8,128)(2,1)S(1)}, u32[]{:S(2)}, u32[]{:S(2)}) collective-permute-start(bf16[432,128]{1,0:T(8,128)(2,1)S(1)} %get-tuple-element.32.a_ref), channel_id=1, source_target_pairs={{0,2},{2,0},{4,6},{6,4},{8,10},{10,8},{12,14},{14,12},{1,3},{3,1},... | collective-permute-start | bytes 331784 | tf_op jit(solution)/shard_map/ppermute | solution.py:484
  100.2 3.4 %collective-permute-done.b_ref = bf16[432,128]{1,0:T(8,128)(2,1)S(1)} collective-permute-done((bf16[432,128]{1,0:T(8,128)(2,1)S(1)}, bf16[432,128]{1,0:T(8,128)(2,1)S(1)}, u32[]{:S(2)}, u32[]{:S(2)}) %collective-permute-start) | collective-permute-done | bytes 110624 | tf_op jit(solution)/shard_map/ppermute | solution.py:484
  103.6 0.6 collective-permute-start.1
  104.2 5.3 %collective-permute-done.1.b_ref = bf16[432,128]{1,0:T(8,128)(2,1)S(1)} collective-permute-done((bf16[432,128]{1,0:T(8,128)(2,1)S(1)}, bf16[432,128]{1,0:T(8,128)(2,1)S(1)}, u32[]{:S(2)}, u32[]{:S(2)}) %collective-permute-start.1) | collective-permute-done | bytes 110624 | tf_op jit(solution)/shard_map/ppermute | solution.py:484
  109.5 2.3 %collective-permute-start.2 = (bf16[432,128]{1,0:T(8,128)(2,1)S(1)}, bf16[432,128]{1,0:T(8,128)(2,1)S(1)}, u32[]{:S(2)}, u32[]{:S(2)}) collective-permute-start(bf16[432,128]{1,0:T(8,128)(2,1)S(1)} %shard_map.137.a_ref), channel_id=1, source_target_pairs={{0,14},{2,12},{4,10},{6,8},{8,6},{10,4},{12,2},{14,0},{1,15},{3,13... | collective-permute-start | bytes 331784 | tf_op jit(solution)/shard_map/ppermute | solution.py:486
  111.8 5.7 %collective-permute-done.2.b_ref = bf16[432,128]{1,0:T(8,128)(2,1)S(1)} collective-permute-done((bf16[432,128]{1,0:T(8,128)(2,1)S(1)}, bf16[432,128]{1,0:T(8,128)(2,1)S(1)}, u32[]{:S(2)}, u32[]{:S(2)}) %collective-permute-start.2) | collective-permute-done | bytes 110624 | tf_op jit(solution)/shard_map/ppermute | solution.py:486
  117.5 1.3 shard_map.138
  118.8 0.0 copy-start.4
  118.8 4.3 %all-to-all-start.5 = ((bf16[16,432,128]{2,1,0:T(8,128)(2,1)}), bf16[16,432,128]{2,1,0:T(8,128)(2,1)S(1)}, u32[]{:S(2)}, u32[]{:S(2)}) async-start(bf16[16,432,128]{2,1,0:T(8,128)(2,1)} %shard_map.138), calls=%async_computation.5 | async-start | bytes 3538944 | tf_op jit(solution)/shard_map/all_to_all | solution.py:427
  123.1 0.0 copy-done.4
  123.1 0.1 shard_map.139
  123.2 1.2 collective-permute-start.3
  124.4 4.5 %collective-permute-start.4 = (bf16[32,1280]{1,0:T(8,128)(2,1)S(1)}, bf16[32,1280]{1,0:T(8,128)(2,1)S(1)}, u32[]{:S(2)}, u32[]{:S(2)}) collective-permute-start(bf16[32,1280]{1,0:T(8,128)(2,1)S(1)} %get-tuple-element.37), channel_id=1, source_target_pairs={{0,6},{2,8},{4,10},{6,12},{8,14},{10,0},{12,2},{14,4},{1,7},{3,9},... | collective-permute-start | bytes 245768 | tf_op jit(solution)/shard_map/ppermute | solution.py:499
  128.9 0.5 collective-permute-start.5
  129.4 0.6 collective-permute-start.6
  130.0 3.6 %collective-permute-start.7 = (bf16[32,1280]{1,0:T(8,128)(2,1)S(1)}, bf16[32,1280]{1,0:T(8,128)(2,1)S(1)}, u32[]{:S(2)}, u32[]{:S(2)}) collective-permute-start(bf16[32,1280]{1,0:T(8,128)(2,1)S(1)} %get-tuple-element.40), channel_id=1, source_target_pairs={{0,12},{2,14},{4,0},{6,2},{8,4},{10,6},{12,8},{14,10},{1,13},{3,15... | collective-permute-start | bytes 245768 | tf_op jit(solution)/shard_map/ppermute | solution.py:499
  133.6 0.0 collective-permute-done.3.refs_1_
  133.6 1.0 collective-permute-start.8
  134.6 0.0 collective-permute-done.4.refs_2_
  134.6 1.5 %collective-permute-start.9 = (bf16[32,1280]{1,0:T(8,128)(2,1)S(1)}, bf16[32,1280]{1,0:T(8,128)(2,1)S(1)}, u32[]{:S(2)}, u32[]{:S(2)}) collective-permute-start(bf16[32,1280]{1,0:T(8,128)(2,1)S(1)} %get-tuple-element.42), channel_id=1, source_target_pairs={{0,14},{2,0},{4,2},{6,4},{8,6},{10,8},{12,10},{14,12},{1,15},{3,1}... | collective-permute-start | bytes 245768 | tf_op jit(solution)/shard_map/ppermute | solution.py:499
  136.0 2.1 %collective-permute-done.5.refs_3_ = bf16[32,1280]{1,0:T(8,128)(2,1)S(1)} collective-permute-done((bf16[32,1280]{1,0:T(8,128)(2,1)S(1)}, bf16[32,1280]{1,0:T(8,128)(2,1)S(1)}, u32[]{:S(2)}, u32[]{:S(2)}) %collective-permute-start.5) | collective-permute-done | bytes 81952 | tf_op jit(solution)/shard_map/ppermute | solution.py:499
  138.2 0.0 collective-permute-done.6.refs_4_
  138.2 0.4 collective-permute-done.7.refs_5_
  138.5 0.0 collective-permute-done.8.refs_6_
  138.5 0.8 collective-permute-done.9.refs_7_
  139.4 0.9 shard_map.140
  140.3 3.1 %all-to-all-done.5.r_ref = bf16[16,432,128]{2,1,0:T(8,128)(2,1)S(1)} async-done(((bf16[16,432,128]{2,1,0:T(8,128)(2,1)}), bf16[16,432,128]{2,1,0:T(8,128)(2,1)S(1)}, u32[]{:S(2)}, u32[]{:S(2)}) %all-to-all-start.5) | async-done | bytes 1769504 | tf_op jit(solution)/shard_map/all_to_all | solution.py:427
  143.4 2.2 %shard_map.141 = (f32[2560,256]{1,0:T(8,128)}, f32[80,2560]{1,0:T(8,128)}) custom-call(bf16[16,432,128]{2,1,0:T(8,128)(2,1)S(1)} %all-to-all-done.5.r_ref), custom_call_target="tpu_custom_call" | custom-call | tf_op jit(solution)/shard_map/pallas_call | solution.py:412
  (3 shorter events, 0.1 us)
Async XLA Ops:
  0.6 11.7 %copy-start.2 = (bf16[32,2560]{1,0:T(8,128)(2,1)S(1)}, bf16[32,2560]{1,0:T(8,128)(2,1)}, u32[]{:S(2)}) copy-start(bf16[32,2560]{1,0:T(8,128)(2,1)} %hid_ref.1) | copy-start | bytes 491524
  3.6 8.9 %copy-start.5 = (f32[80]{0:T(128)S(1)}, f32[80]{0:T(128)}, u32[]{:S(2)}) copy-start(f32[80]{0:T(128)} %param.15) | copy-start | bytes 964
  3.6 8.9 %copy-start.6 = (f32[80]{0:T(128)S(1)}, f32[80]{0:T(128)}, u32[]{:S(2)}) copy-start(f32[80]{0:T(128)} %param.14) | copy-start | bytes 964
  3.6 8.9 %copy-start.7 = (f32[80]{0:T(128)S(1)}, f32[80]{0:T(128)}, u32[]{:S(2)}) copy-start(f32[80]{0:T(128)} %param.13) | copy-start | bytes 964
  3.7 31.8 %all-to-all-start = ((bf16[8,32,1664]{2,1,0:T(8,128)(2,1)}), bf16[8,32,1664]{2,1,0:T(8,128)(2,1)S(1)}, u32[]{:S(2)}, u32[]{:S(2)}) async-start(bf16[8,32,1664]{2,1,0:T(8,128)(2,1)} %shard_map.127), calls=%async_computation | async-start | bytes 1703936 | tf_op jit(solution)/shard_map/all_to_all | solution.py:427
  37.3 17.2 %all-to-all-start.1 = ((bf16[16,16,1024]{2,1,0:T(8,128)(2,1)}), bf16[16,16,1024]{2,1,0:T(8,128)(2,1)S(1)}, u32[]{:S(2)}, u32[]{:S(2)}) async-start(bf16[16,16,1024]{2,1,0:T(8,128)(2,1)} %shard_map.129), calls=%async_computation.1 | async-start | bytes 1048576 | tf_op jit(solution)/shard_map/all_to_all | solution.py:427
  69.3 0.8 copy-start.3
  70.1 18.1 %copy-start = (bf16[2560,256]{1,0:T(8,128)(2,1)S(1)}, bf16[2560,256]{1,0:T(8,128)(2,1)}, u32[]{:S(2)}) copy-start(bf16[2560,256]{1,0:T(8,128)(2,1)} %wbc_ref.1) | copy-start | bytes 3932164
  70.1 18.1 %copy-start.1 = (bf16[2560,80]{0,1:T(8,128)(2,1)S(1)}, bf16[2560,80]{0,1:T(8,128)(2,1)}, u32[]{:S(2)}) copy-start(bf16[2560,80]{0,1:T(8,128)(2,1)} %param.12) | copy-start | bytes 1228804
  84.7 12.9 %all-to-all-start.4 = ((bf16[16,32,384]{2,1,0:T(8,128)(2,1)}), bf16[16,32,384]{2,1,0:T(8,128)(2,1)S(1)}, u32[]{:S(2)}, u32[]{:S(2)}) async-start(bf16[16,32,384]{2,1,0:T(8,128)(2,1)} %shard_map.133.d_ref), calls=%async_computation.4 | async-start | bytes 786432 | tf_op jit(solution)/shard_map/all_to_all | solution.py:427
  98.5 5.0 %collective-permute-start = (bf16[432,128]{1,0:T(8,128)(2,1)S(1)}, bf16[432,128]{1,0:T(8,128)(2,1)S(1)}, u32[]{:S(2)}, u32[]{:S(2)}) collective-permute-start(bf16[432,128]{1,0:T(8,128)(2,1)S(1)} %get-tuple-element.32.a_ref), channel_id=1, source_target_pairs={{0,2},{2,0},{4,6},{6,4},{8,10},{10,8},{12,14},{14,12},{1,3},{3,1},... | collective-permute-start | bytes 331784 | tf_op jit(solution)/shard_map/ppermute | solution.py:484
  103.6 5.9 %collective-permute-start.1 = (bf16[432,128]{1,0:T(8,128)(2,1)S(1)}, bf16[432,128]{1,0:T(8,128)(2,1)S(1)}, u32[]{:S(2)}, u32[]{:S(2)}) collective-permute-start(bf16[432,128]{1,0:T(8,128)(2,1)S(1)} %shard_map.136.a_ref), channel_id=1, source_target_pairs={{0,4},{2,6},{4,0},{6,2},{8,12},{10,14},{12,8},{14,10},{1,5},{3,7},... | collective-permute-start | bytes 331784 | tf_op jit(solution)/shard_map/ppermute | solution.py:484
  109.5 7.9 %collective-permute-start.2 = (bf16[432,128]{1,0:T(8,128)(2,1)S(1)}, bf16[432,128]{1,0:T(8,128)(2,1)S(1)}, u32[]{:S(2)}, u32[]{:S(2)}) collective-permute-start(bf16[432,128]{1,0:T(8,128)(2,1)S(1)} %shard_map.137.a_ref), channel_id=1, source_target_pairs={{0,14},{2,12},{4,10},{6,8},{8,6},{10,4},{12,2},{14,0},{1,15},{3,13... | collective-permute-start | bytes 331784 | tf_op jit(solution)/shard_map/ppermute | solution.py:486
  118.8 4.3 %copy-start.4 = (bf16[256,1280]{1,0:T(8,128)(2,1)S(1)}, bf16[256,1280]{1,0:T(8,128)(2,1)}, u32[]{:S(2)}) copy-start(bf16[256,1280]{1,0:T(8,128)(2,1)} %copy-done.3) | copy-start | bytes 1966084
  118.8 24.6 %all-to-all-start.5 = ((bf16[16,432,128]{2,1,0:T(8,128)(2,1)}), bf16[16,432,128]{2,1,0:T(8,128)(2,1)S(1)}, u32[]{:S(2)}, u32[]{:S(2)}) async-start(bf16[16,432,128]{2,1,0:T(8,128)(2,1)} %shard_map.138), calls=%async_computation.5 | async-start | bytes 3538944 | tf_op jit(solution)/shard_map/all_to_all | solution.py:427
  123.2 10.4 %collective-permute-start.3 = (bf16[32,1280]{1,0:T(8,128)(2,1)S(1)}, bf16[32,1280]{1,0:T(8,128)(2,1)S(1)}, u32[]{:S(2)}, u32[]{:S(2)}) collective-permute-start(bf16[32,1280]{1,0:T(8,128)(2,1)S(1)} %get-tuple-element.36), channel_id=1, source_target_pairs={{0,8},{2,10},{4,12},{6,14},{8,0},{10,2},{12,4},{14,6},{1,9},{3,11}... | collective-permute-start | bytes 245768 | tf_op jit(solution)/shard_map/ppermute | solution.py:499
  124.4 10.2 %collective-permute-start.4 = (bf16[32,1280]{1,0:T(8,128)(2,1)S(1)}, bf16[32,1280]{1,0:T(8,128)(2,1)S(1)}, u32[]{:S(2)}, u32[]{:S(2)}) collective-permute-start(bf16[32,1280]{1,0:T(8,128)(2,1)S(1)} %get-tuple-element.37), channel_id=1, source_target_pairs={{0,6},{2,8},{4,10},{6,12},{8,14},{10,0},{12,2},{14,4},{1,7},{3,9},... | collective-permute-start | bytes 245768 | tf_op jit(solution)/shard_map/ppermute | solution.py:499
  128.9 9.2 %collective-permute-start.5 = (bf16[32,1280]{1,0:T(8,128)(2,1)S(1)}, bf16[32,1280]{1,0:T(8,128)(2,1)S(1)}, u32[]{:S(2)}, u32[]{:S(2)}) collective-permute-start(bf16[32,1280]{1,0:T(8,128)(2,1)S(1)} %get-tuple-element.38), channel_id=1, source_target_pairs={{0,10},{2,12},{4,14},{6,0},{8,2},{10,4},{12,6},{14,8},{1,11},{3,13... | collective-permute-start | bytes 245768 | tf_op jit(solution)/shard_map/ppermute | solution.py:499
  129.4 8.7 %collective-permute-start.6 = (bf16[32,1280]{1,0:T(8,128)(2,1)S(1)}, bf16[32,1280]{1,0:T(8,128)(2,1)S(1)}, u32[]{:S(2)}, u32[]{:S(2)}) collective-permute-start(bf16[32,1280]{1,0:T(8,128)(2,1)S(1)} %get-tuple-element.39), channel_id=1, source_target_pairs={{0,4},{2,6},{4,8},{6,10},{8,12},{10,14},{12,0},{14,2},{1,5},{3,7},... | collective-permute-start | bytes 245768 | tf_op jit(solution)/shard_map/ppermute | solution.py:499
  130.0 8.5 %collective-permute-start.7 = (bf16[32,1280]{1,0:T(8,128)(2,1)S(1)}, bf16[32,1280]{1,0:T(8,128)(2,1)S(1)}, u32[]{:S(2)}, u32[]{:S(2)}) collective-permute-start(bf16[32,1280]{1,0:T(8,128)(2,1)S(1)} %get-tuple-element.40), channel_id=1, source_target_pairs={{0,12},{2,14},{4,0},{6,2},{8,4},{10,6},{12,8},{14,10},{1,13},{3,15... | collective-permute-start | bytes 245768 | tf_op jit(solution)/shard_map/ppermute | solution.py:499
  133.6 5.0 %collective-permute-start.8 = (bf16[32,1280]{1,0:T(8,128)(2,1)S(1)}, bf16[32,1280]{1,0:T(8,128)(2,1)S(1)}, u32[]{:S(2)}, u32[]{:S(2)}) collective-permute-start(bf16[32,1280]{1,0:T(8,128)(2,1)S(1)} %get-tuple-element.41), channel_id=1, source_target_pairs={{0,2},{2,4},{4,6},{6,8},{8,10},{10,12},{12,14},{14,0},{1,3},{3,5},... | collective-permute-start | bytes 245768 | tf_op jit(solution)/shard_map/ppermute | solution.py:499
  134.6 4.8 %collective-permute-start.9 = (bf16[32,1280]{1,0:T(8,128)(2,1)S(1)}, bf16[32,1280]{1,0:T(8,128)(2,1)S(1)}, u32[]{:S(2)}, u32[]{:S(2)}) collective-permute-start(bf16[32,1280]{1,0:T(8,128)(2,1)S(1)} %get-tuple-element.42), channel_id=1, source_target_pairs={{0,14},{2,0},{4,2},{6,4},{8,6},{10,8},{12,10},{14,12},{1,15},{3,1}... | collective-permute-start | bytes 245768 | tf_op jit(solution)/shard_map/ppermute | solution.py:499
